TPU v7x, 32 devices: a whole 2x2x4 slice. The times are simulated.
32 devices in a mesh: groups: 2 (over x), chan: 16 (over z, y, core).
Axes of the slice: x: 2, y: 2, z: 4, core: 2. Of those that a mesh axis runs over, the one named last changes fastest.
Arguments:
- spectra: bfloat16 [32, 2, 2, 64, 4096], P(('groups', 'chan')), parts along dimension 0, may hold values from -6 to 6
- pair_valid: int32 [32, 8], P(('groups', 'chan')), parts along dimension 0, may hold values from 0 to 1, as said below
Outputs:
- correlations: float32 [32, 8, 64, 512], P(('groups', 'chan')), parts along dimension 0
There are 2 independent parts, one for each index of `groups`. A program takes and returns all parts, laid end to end along the dimension named above; each array names one. Nothing has to cross between parts.
Inputs may be any that keep to these rules, and one draw needn't show every extreme that they name: pair_valid[b,0] is 1 for every block.
All inputs are finite; a program needn't handle non-finite values.
Results may differ from a plain program's by a relative error of at most 0.0034.
Values may be sent and summed in bfloat16 or wider, within the bound.
No kernel may reach another device: no remote copies, remote signals or barrier semaphores. Data moves between devices by JAX's collectives and lax.ppermute only.
A program may use at most 128 MiB of HBM per device.

v0:
```python
import math

import jax
import jax.numpy as jnp
from jax import lax
from jax.sharding import PartitionSpec as P

F = 4096
SEG = 2
LAGS = 8
STEPS = 8


def shifted(value, axis, steps):
    count = lax.axis_size(axis)
    pairs = [(source, (source + steps) % count) for source in range(count)]
    return lax.ppermute(value, axis, pairs)


def lag_table(bins, lags):
    freq = jnp.arange(bins, dtype=jnp.int32)[:, None]
    shift = jnp.arange(lags, dtype=jnp.int32)[None, :] - lags // 2
    phase = jnp.mod(freq * shift, 2 * bins)
    angle = phase.astype(jnp.float32) * (math.pi / bins)
    return jnp.concatenate([jnp.cos(angle), -jnp.sin(angle)], 0).astype(jnp.bfloat16)


def modulate(own, table, bins):
    cosine = table[:bins].astype(jnp.float32).T
    sine = table[bins:].astype(jnp.float32).T
    real_part = own[:, 0].astype(jnp.float32)[:, :, None, :]
    imag_part = own[:, 1].astype(jnp.float32)[:, :, None, :]
    first = real_part * cosine[None, None] + imag_part * sine[None, None]
    second = imag_part * cosine[None, None] - real_part * sine[None, None]
    stacked = jnp.stack([first, second], 1)
    return jnp.transpose(stacked, (2, 3, 0, 1, 4)).astype(jnp.bfloat16)


def per_device(spectra, pair_valid):
    own = spectra[0]
    flags = pair_valid[0]
    width = own.shape[2]
    stride = lax.axis_size("chan") // (2 * STEPS)
    table = lag_table(F, LAGS)
    norm = 1.0 / math.sqrt(2.0 * SEG * F)
    modulated = modulate(own, table, F)

    def pair_result(moving, flag):
        result = jnp.einsum(
            "itscf,scjf->itj", modulated, moving, preferred_element_type=jnp.float32
        )
        return result.reshape(width, LAGS * width) * norm * flag.astype(jnp.float32)

    def place(output, moving, distance):
        value = pair_result(moving, flags[distance])
        return output.at[0, distance].set(value)

    output = jnp.zeros((1, STEPS, width, LAGS * width), jnp.float32)

    def one_step(count, carry):
        moving, result = carry
        result = place(result, moving, count)
        moving = shifted(moving, "chan", stride)
        return (moving, result)

    moving, output = lax.fori_loop(0, STEPS - 1, one_step, (own, output))
    output = place(output, moving, STEPS - 1)
    return output


def solution(mesh):
    return jax.shard_map(
        per_device,
        mesh=mesh,
        in_specs=(P(("groups", "chan"), None, None, None, None), P(("groups", "chan"), None)),
        out_specs=P(("groups", "chan"), None, None, None),
        check_vma=False,
    )
```

profile of v0, /device:TPU:0, one launch (start us, length us, event | category | flops | bytes accessed | tf_op | source)
XLA Modules:
  0.0 252.4 jit_solution(12959641565795549780)
XLA Ops:
  0.0 3.1 %copy.13 = bf16[1,2,2,64,4096]{4,3,1,2,0:T(8,128)(2,1)} copy(bf16[1,2,2,64,4096]{4,3,2,1,0:T(8,128)(2,1)} %param.8) | data formatting | bytes 4194304 | tf_op args[0]
  3.1 2.0 fusion.17
  5.2 1.6 copy.4
  9.0 5.8 %add_convert_fusion = (bf16[2,1,64,8,4096]{4,3,0,1,2:T(8,128)(2,1)S(1)}, bf16[2,1,64,8,4096]{4,3,0,1,2:T(8,128)(2,1)S(1)}) fusion(f32[8,4096]{1,0:T(8,128)S(1)} %get-tuple-element.151, f32[2,64,4096]{2,0,1:T(2,128)S(1)} %copy.5, f32[8,4096]{1,0:T(8,128)S(1)} %get-tuple-element.150, f32[2,64,4096]{2,0,1:T(2,128)S(1)} %copy.4), kind=kLoop, calls=%fused_computation.8 | loop fusion | flops 33554432 | bytes 21233664 | tf_op jit(solution)/shard_map/convert.4
  14.8 3.2 %copy-done = bf16[2,1,64,8,4096]{4,3,0,1,2:T(8,128)(2,1)} copy-done((bf16[2,1,64,8,4096]{4,3,0,1,2:T(8,128)(2,1)}, bf16[2,1,64,8,4096]{4,3,0,1,2:T(8,128)(2,1)S(1)}, u32[]{:S(2)}) %copy-start) | copy-done | bytes 8388632
  18.0 2.5 copy-done.1
  20.5 6.7 %maximum_bitcast_fusion = bf16[64,8,2,2,4096]{4,1,2,3,0:T(8,128)(2,1)} fusion(bf16[2,1,64,8,4096]{4,3,0,1,2:T(8,128)(2,1)S(1)} %get-tuple-element.147, bf16[2,1,64,8,4096]{4,3,0,1,2:T(8,128)(2,1)S(1)} %get-tuple-element.146), kind=kLoop, calls=%fused_computation.6 | loop fusion | flops 8388608 | bytes 33554432 | tf_op jit(solution)/shard_map/convert_element_type | solution.py:36
  27.4 210.0 %while.17 = (s32[]{:T(128)}, bf16[2,2,64,4096]{3,2,0,1:T(8,128)(2,1)}, f32[1,8,64,512]{3,2,1,0:T(8,128)S(1)}, bf16[64,8,2,2,4096]{4,1,2,3,0:T(8,128)(2,1)}, s32[...) while((s32[]{:T(128)}, bf16[2,2,64,4096]{3,2,0,1:T(8,128)(2,1)}, ...), condition=%wide.region_2.3_spmd, body=%wide.region_0.2_spmd.sunk | while | flops 1073807360 | bytes 32243916 | solution.py:66
  30.7 8.1 %fusion.30 = f32[64,8,64]{2,1,0:T(8,128)S(1)} fusion(bf16[64,8,2,2,4096]{4,1,2,3,0:T(8,128)(2,1)} %get-tuple-element.204, bf16[2,2,64,4096]{3,2,0,1:T(8,128)(2,1)S(1)} %copy.19, f32[]{:T(128)} %bitcast.72), kind=kOutput, calls=%fused_computation.3.clone.1 | convolution fusion | flops 1073774592 | bytes 19005444 | tf_op jit(solution)/shard_map/while/body/eval_jaxpr/itscf,scjf->itj/dot_general | solution.py:49
  40.3 17.9 %collective-permute-done = bf16[2,2,64,4096]{3,2,0,1:T(8,128)(2,1)} collective-permute-done((bf16[2,2,64,4096]{3,2,0,1:T(8,128)(2,1)S(1)}, bf16[2,2,64,4096]{3,2,0,1:T(8,128)(2,1)}, u32[]{:S(2)}, u32[]{:S(2)}) %collective-permute-start) | collective-permute-done | bytes 2097184 | tf_op jit(solution)/shard_map/while/body/eval_jaxpr/ppermute | solution.py:17
  61.1 8.1 %fusion.30 = f32[64,8,64]{2,1,0:T(8,128)S(1)} fusion(bf16[64,8,2,2,4096]{4,1,2,3,0:T(8,128)(2,1)} %get-tuple-element.204, bf16[2,2,64,4096]{3,2,0,1:T(8,128)(2,1)S(1)} %copy.19, f32[]{:T(128)} %bitcast.72), kind=kOutput, calls=%fused_computation.3.clone.1 | convolution fusion | flops 1073774592 | bytes 19005444 | tf_op jit(solution)/shard_map/while/body/eval_jaxpr/itscf,scjf->itj/dot_general | solution.py:49
  70.7 17.4 %collective-permute-done = bf16[2,2,64,4096]{3,2,0,1:T(8,128)(2,1)} collective-permute-done((bf16[2,2,64,4096]{3,2,0,1:T(8,128)(2,1)S(1)}, bf16[2,2,64,4096]{3,2,0,1:T(8,128)(2,1)}, u32[]{:S(2)}, u32[]{:S(2)}) %collective-permute-start) | collective-permute-done | bytes 2097184 | tf_op jit(solution)/shard_map/while/body/eval_jaxpr/ppermute | solution.py:17
  90.9 8.1 %fusion.30 = f32[64,8,64]{2,1,0:T(8,128)S(1)} fusion(bf16[64,8,2,2,4096]{4,1,2,3,0:T(8,128)(2,1)} %get-tuple-element.204, bf16[2,2,64,4096]{3,2,0,1:T(8,128)(2,1)S(1)} %copy.19, f32[]{:T(128)} %bitcast.72), kind=kOutput, calls=%fused_computation.3.clone.1 | convolution fusion | flops 1073774592 | bytes 19005444 | tf_op jit(solution)/shard_map/while/body/eval_jaxpr/itscf,scjf->itj/dot_general | solution.py:49
  100.6 17.4 %collective-permute-done = bf16[2,2,64,4096]{3,2,0,1:T(8,128)(2,1)} collective-permute-done((bf16[2,2,64,4096]{3,2,0,1:T(8,128)(2,1)S(1)}, bf16[2,2,64,4096]{3,2,0,1:T(8,128)(2,1)}, u32[]{:S(2)}, u32[]{:S(2)}) %collective-permute-start) | collective-permute-done | bytes 2097184 | tf_op jit(solution)/shard_map/while/body/eval_jaxpr/ppermute | solution.py:17
  120.8 8.1 %fusion.30 = f32[64,8,64]{2,1,0:T(8,128)S(1)} fusion(bf16[64,8,2,2,4096]{4,1,2,3,0:T(8,128)(2,1)} %get-tuple-element.204, bf16[2,2,64,4096]{3,2,0,1:T(8,128)(2,1)S(1)} %copy.19, f32[]{:T(128)} %bitcast.72), kind=kOutput, calls=%fused_computation.3.clone.1 | convolution fusion | flops 1073774592 | bytes 19005444 | tf_op jit(solution)/shard_map/while/body/eval_jaxpr/itscf,scjf->itj/dot_general | solution.py:49
  130.5 17.4 %collective-permute-done = bf16[2,2,64,4096]{3,2,0,1:T(8,128)(2,1)} collective-permute-done((bf16[2,2,64,4096]{3,2,0,1:T(8,128)(2,1)S(1)}, bf16[2,2,64,4096]{3,2,0,1:T(8,128)(2,1)}, u32[]{:S(2)}, u32[]{:S(2)}) %collective-permute-start) | collective-permute-done | bytes 2097184 | tf_op jit(solution)/shard_map/while/body/eval_jaxpr/ppermute | solution.py:17
  150.7 8.1 %fusion.30 = f32[64,8,64]{2,1,0:T(8,128)S(1)} fusion(bf16[64,8,2,2,4096]{4,1,2,3,0:T(8,128)(2,1)} %get-tuple-element.204, bf16[2,2,64,4096]{3,2,0,1:T(8,128)(2,1)S(1)} %copy.19, f32[]{:T(128)} %bitcast.72), kind=kOutput, calls=%fused_computation.3.clone.1 | convolution fusion | flops 1073774592 | bytes 19005444 | tf_op jit(solution)/shard_map/while/body/eval_jaxpr/itscf,scjf->itj/dot_general | solution.py:49
  160.3 17.4 %collective-permute-done = bf16[2,2,64,4096]{3,2,0,1:T(8,128)(2,1)} collective-permute-done((bf16[2,2,64,4096]{3,2,0,1:T(8,128)(2,1)S(1)}, bf16[2,2,64,4096]{3,2,0,1:T(8,128)(2,1)}, u32[]{:S(2)}, u32[]{:S(2)}) %collective-permute-start) | collective-permute-done | bytes 2097184 | tf_op jit(solution)/shard_map/while/body/eval_jaxpr/ppermute | solution.py:17
  180.5 8.1 %fusion.30 = f32[64,8,64]{2,1,0:T(8,128)S(1)} fusion(bf16[64,8,2,2,4096]{4,1,2,3,0:T(8,128)(2,1)} %get-tuple-element.204, bf16[2,2,64,4096]{3,2,0,1:T(8,128)(2,1)S(1)} %copy.19, f32[]{:T(128)} %bitcast.72), kind=kOutput, calls=%fused_computation.3.clone.1 | convolution fusion | flops 1073774592 | bytes 19005444 | tf_op jit(solution)/shard_map/while/body/eval_jaxpr/itscf,scjf->itj/dot_general | solution.py:49
  190.2 17.4 %collective-permute-done = bf16[2,2,64,4096]{3,2,0,1:T(8,128)(2,1)} collective-permute-done((bf16[2,2,64,4096]{3,2,0,1:T(8,128)(2,1)S(1)}, bf16[2,2,64,4096]{3,2,0,1:T(8,128)(2,1)}, u32[]{:S(2)}, u32[]{:S(2)}) %collective-permute-start) | collective-permute-done | bytes 2097184 | tf_op jit(solution)/shard_map/while/body/eval_jaxpr/ppermute | solution.py:17
  210.4 8.1 %fusion.30 = f32[64,8,64]{2,1,0:T(8,128)S(1)} fusion(bf16[64,8,2,2,4096]{4,1,2,3,0:T(8,128)(2,1)} %get-tuple-element.204, bf16[2,2,64,4096]{3,2,0,1:T(8,128)(2,1)S(1)} %copy.19, f32[]{:T(128)} %bitcast.72), kind=kOutput, calls=%fused_computation.3.clone.1 | convolution fusion | flops 1073774592 | bytes 19005444 | tf_op jit(solution)/shard_map/while/body/eval_jaxpr/itscf,scjf->itj/dot_general | solution.py:49
  220.0 17.4 %collective-permute-done = bf16[2,2,64,4096]{3,2,0,1:T(8,128)(2,1)} collective-permute-done((bf16[2,2,64,4096]{3,2,0,1:T(8,128)(2,1)S(1)}, bf16[2,2,64,4096]{3,2,0,1:T(8,128)(2,1)}, u32[]{:S(2)}, u32[]{:S(2)}) %collective-permute-start) | collective-permute-done | bytes 2097184 | tf_op jit(solution)/shard_map/while/body/eval_jaxpr/ppermute | solution.py:17
  238.7 9.5 %fusion.13 = f32[64,8,64]{2,1,0:T(8,128)S(1)} fusion(bf16[2,2,64,4096]{3,2,0,1:T(8,128)(2,1)} %get-tuple-element.135, f32[]{:T(128)} %bitcast.17, bf16[2,1,64,8,4096]{4,3,0,1,2:T(8,128)(2,1)} %copy-done.1, bf16[2,1,64,8,4096]{4,3,0,1,2:T(8,128)(2,1)} %copy-done), kind=kOutput, calls=%fused_computation.13 | convolution fusion | flops 1082163200 | bytes 19005444 | tf_op jit(solution)/shard_map/itscf,scjf->itj/dot_general | solution.py:49
  249.7 2.8 %select_dynamic-update-slice_fusion.1 = f32[1,8,64,512]{3,2,1,0:T(8,128)} fusion(f32[1,8,64,512]{3,2,1,0:T(8,128)} %copy-done.2, s32[]{:T(128)} %bitcast.18, f32[1,1,64,512]{3,2,1,0:T(8,128)S(1)} %mul.162, pred[]{:T(512)} %and_reduce_fusion.1), kind=kLoop, calls=%fused_computation.26 | loop fusion | flops 32768 | bytes 394240 | tf_op jit(solution)/shard_map/scatter | solution.py:56
  (59 shorter events, 30.9 us)
Async XLA Ops:
  14.8 3.2 %copy-start = (bf16[2,1,64,8,4096]{4,3,0,1,2:T(8,128)(2,1)}, bf16[2,1,64,8,4096]{4,3,0,1,2:T(8,128)(2,1)S(1)}, u32[]{:S(2)}) copy-start(bf16[2,1,64,8,4096]{4,3,0,1,2:T(8,128)(2,1)S(1)} %get-tuple-element.146) | copy-start | bytes 25165828
  14.8 5.7 %copy-start.1 = (bf16[2,1,64,8,4096]{4,3,0,1,2:T(8,128)(2,1)}, bf16[2,1,64,8,4096]{4,3,0,1,2:T(8,128)(2,1)S(1)}, u32[]{:S(2)}) copy-start(bf16[2,1,64,8,4096]{4,3,0,1,2:T(8,128)(2,1)S(1)} %get-tuple-element.147) | copy-start | bytes 25165828
  20.5 6.8 %copy-start.3 = (s32[4]{0:T(128)S(1)}, s32[4]{0:T(128)}, u32[]{:S(2)}) copy-start(s32[4]{0:T(128)} %constant.126.clone.1) | copy-start | bytes 52
  20.5 6.8 %copy-start.4 = (s32[1,8]{1,0:T(1,128)S(1)}, s32[1,8]{1,0:T(1,128)}, u32[]{:S(2)}) copy-start(s32[1,8]{1,0:T(1,128)} %param.9) | copy-start | bytes 100
  29.0 29.3 %collective-permute-start = (bf16[2,2,64,4096]{3,2,0,1:T(8,128)(2,1)S(1)}, bf16[2,2,64,4096]{3,2,0,1:T(8,128)(2,1)}, u32[]{:S(2)}, u32[]{:S(2)}) collective-permute-start(bf16[2,2,64,4096]{3,2,0,1:T(8,128)(2,1)S(1)} %copy.19), channel_id=1, source_target_pairs={{0,1},{1,2},{2,3},{3,4},{4,5},{5,6},{6,7},{7,8},{8,9},{9,10},{10,1... | collective-permute-start | bytes 6291464 | tf_op jit(solution)/shard_map/while/body/eval_jaxpr/ppermute | solution.py:17
  59.9 28.3 %collective-permute-start = (bf16[2,2,64,4096]{3,2,0,1:T(8,128)(2,1)S(1)}, bf16[2,2,64,4096]{3,2,0,1:T(8,128)(2,1)}, u32[]{:S(2)}, u32[]{:S(2)}) collective-permute-start(bf16[2,2,64,4096]{3,2,0,1:T(8,128)(2,1)S(1)} %copy.19), channel_id=1, source_target_pairs={{0,1},{1,2},{2,3},{3,4},{4,5},{5,6},{6,7},{7,8},{8,9},{9,10},{10,1... | collective-permute-start | bytes 6291464 | tf_op jit(solution)/shard_map/while/body/eval_jaxpr/ppermute | solution.py:17
  89.7 28.3 %collective-permute-start = (bf16[2,2,64,4096]{3,2,0,1:T(8,128)(2,1)S(1)}, bf16[2,2,64,4096]{3,2,0,1:T(8,128)(2,1)}, u32[]{:S(2)}, u32[]{:S(2)}) collective-permute-start(bf16[2,2,64,4096]{3,2,0,1:T(8,128)(2,1)S(1)} %copy.19), channel_id=1, source_target_pairs={{0,1},{1,2},{2,3},{3,4},{4,5},{5,6},{6,7},{7,8},{8,9},{9,10},{10,1... | collective-permute-start | bytes 6291464 | tf_op jit(solution)/shard_map/while/body/eval_jaxpr/ppermute | solution.py:17
  119.6 28.3 %collective-permute-start = (bf16[2,2,64,4096]{3,2,0,1:T(8,128)(2,1)S(1)}, bf16[2,2,64,4096]{3,2,0,1:T(8,128)(2,1)}, u32[]{:S(2)}, u32[]{:S(2)}) collective-permute-start(bf16[2,2,64,4096]{3,2,0,1:T(8,128)(2,1)S(1)} %copy.19), channel_id=1, source_target_pairs={{0,1},{1,2},{2,3},{3,4},{4,5},{5,6},{6,7},{7,8},{8,9},{9,10},{10,1... | collective-permute-start | bytes 6291464 | tf_op jit(solution)/shard_map/while/body/eval_jaxpr/ppermute | solution.py:17
  149.4 28.3 %collective-permute-start = (bf16[2,2,64,4096]{3,2,0,1:T(8,128)(2,1)S(1)}, bf16[2,2,64,4096]{3,2,0,1:T(8,128)(2,1)}, u32[]{:S(2)}, u32[]{:S(2)}) collective-permute-start(bf16[2,2,64,4096]{3,2,0,1:T(8,128)(2,1)S(1)} %copy.19), channel_id=1, source_target_pairs={{0,1},{1,2},{2,3},{3,4},{4,5},{5,6},{6,7},{7,8},{8,9},{9,10},{10,1... | collective-permute-start | bytes 6291464 | tf_op jit(solution)/shard_map/while/body/eval_jaxpr/ppermute | solution.py:17
  179.3 28.3 %collective-permute-start = (bf16[2,2,64,4096]{3,2,0,1:T(8,128)(2,1)S(1)}, bf16[2,2,64,4096]{3,2,0,1:T(8,128)(2,1)}, u32[]{:S(2)}, u32[]{:S(2)}) collective-permute-start(bf16[2,2,64,4096]{3,2,0,1:T(8,128)(2,1)S(1)} %copy.19), channel_id=1, source_target_pairs={{0,1},{1,2},{2,3},{3,4},{4,5},{5,6},{6,7},{7,8},{8,9},{9,10},{10,1... | collective-permute-start | bytes 6291464 | tf_op jit(solution)/shard_map/while/body/eval_jaxpr/ppermute | solution.py:17
  209.1 28.3 %collective-permute-start = (bf16[2,2,64,4096]{3,2,0,1:T(8,128)(2,1)S(1)}, bf16[2,2,64,4096]{3,2,0,1:T(8,128)(2,1)}, u32[]{:S(2)}, u32[]{:S(2)}) collective-permute-start(bf16[2,2,64,4096]{3,2,0,1:T(8,128)(2,1)S(1)} %copy.19), channel_id=1, source_target_pairs={{0,1},{1,2},{2,3},{3,4},{4,5},{5,6},{6,7},{7,8},{8,9},{9,10},{10,1... | collective-permute-start | bytes 6291464 | tf_op jit(solution)/shard_map/while/body/eval_jaxpr/ppermute | solution.py:17
  237.4 10.9 %copy-start.2 = (f32[1,8,64,512]{3,2,1,0:T(8,128)}, f32[1,8,64,512]{3,2,1,0:T(8,128)S(1)}, u32[]{:S(2)}) copy-start(f32[1,8,64,512]{3,2,1,0:T(8,128)S(1)} %get-tuple-element.134) | copy-start | bytes 3145732
where the time goes:
time: 253 us; the launch traced here: 252 us
  waiting for transfers between devices  122 us (48%)
  matrix products  66.3 us (26%)
  local copies, waits for them, and re-layouts  29.6 us (12%)
  other arithmetic  28.5 us (11%)
  loops' own time  4.71 us (2%)
    ppermute x7, waiting for transfers between devices, shifted(): return lax.ppermute(value, axis, pairs)  122 us
    dot_general x8, matrix products, pair_result(): jnp.einsum('itscf,scjf->itj', modulated, moving, preferred_element_type=j...  66.3 us
    another operation x10, other arithmetic  11.8 us
    another operation x8, local copies, waits for them, and re-layouts  11.7 us
    unnamed x11, local copies, waits for them, and re-layouts  8.86 us
    scatter x8, other arithmetic, place(): return output.at[0, distance].set(value)  7.32 us
    convert_element_type x1, other arithmetic, modulate(): return jnp.transpose(stacked, (2, 3, 0, 1, 4)).astype(jnp.bfloat16)  6.71 us
  transfers between devices with their start and end apart: 7, of which 7 were waited for; matrix products, arithmetic and copies ran while one was open for 28% of the time, Pallas kernels for 0%

commit v1 on v0

v1 whole, which is shorter than its diff:
```python
import functools
import math

import jax
import jax.numpy as jnp
import ml_dtypes
import numpy as np
from jax import lax
from jax.experimental import pallas as pl
from jax.experimental.pallas import tpu as pltpu
from jax.sharding import PartitionSpec as P

PLANE = 4


def lag_rows(bins, lags):
    rows = np.arange(8)[:, None]
    phase = np.mod(np.arange(bins)[None, :] * rows, 2 * bins)
    angle = phase.astype(np.float64) * (math.pi / bins)
    def rounded(x):
        return x.astype(np.float32).astype(ml_dtypes.bfloat16).astype(np.float32)
    return rounded(np.cos(angle)), rounded(np.sin(angle))


def pair_kernel(lags, steps, first, count, cols_ref, half_ref, *refs):
    own = refs[:PLANE]
    other = refs[PLANE:PLANE + count]
    cos_ref, sin_ref = refs[PLANE + count:PLANE + count + 2]
    outs = refs[PLANE + count + 2:2 * PLANE + count + 2]
    rhs, mod, acc = refs[2 * PLANE + count + 2:]
    width = own[0].shape[1]
    tile = own[0].shape[2]
    step = pl.program_id(0)
    for n in range(count):
        for c in range(2):
            rhs[cols_ref[n], :, c * tile:(c + 1) * tile] = other[n][c]
    weights = rhs[...].reshape(PLANE * width, 2 * tile)
    mid = lags // 2

    def put(slot, t, real, imag):
        mod[slot, t * width:(t + 1) * width, :tile] = real.astype(jnp.bfloat16)
        mod[slot, t * width:(t + 1) * width, tile:] = imag.astype(jnp.bfloat16)

    for m in range(PLANE):
        slot = m % 2
        real, imag = own[m][0].astype(jnp.float32), own[m][1].astype(jnp.float32)
        for lag in range(mid + 1):
            cosine = cos_ref[lag:lag + 1, :]
            sine = sin_ref[lag:lag + 1, :]
            rc, rs, ic, im = real * cosine, real * sine, imag * cosine, imag * sine
            put(slot, mid - lag, rc + im, ic - rs)
            if 0 < lag < lags - mid:
                put(slot, mid + lag, rc - im, ic + rs)
        part = lax.dot_general(
            mod[slot], weights, (((1,), (1,)), ((), ())), preferred_element_type=jnp.float32
        )

        @pl.when(step == 0)
        def _():
            acc[m] = part

        @pl.when(step > 0)
        def _():
            acc[m] += part

    @pl.when(step == steps - 1)
    def _():
        for m in range(PLANE):
            for j in range(first, PLANE):
                for t in range(0, lags, 2):
                    pair = [
                        acc[m, u * width:(u + 1) * width, j * width:(j + 1) * width]
                        for u in (t, t + 1)
                    ]
                    outs[m][j - first, :, t * width:(t + 2) * width] = jnp.concatenate(pair, 1)


def pair_products(own, other, cols, half, tables, lags, first):
    _, width, bins = own[0].shape
    tile = min(512, bins)
    steps = bins // tile
    count = len(other)
    block = pl.BlockSpec((2, width, tile), lambda f, cols, half: (0, 0, f))
    table = pl.BlockSpec((8, tile), lambda f, cols, half: (0, half[0] * steps + f))
    shape = (PLANE - first, width, lags * width)
    return pl.pallas_call(
        functools.partial(pair_kernel, lags, steps, first, count),
        out_shape=[jax.ShapeDtypeStruct(shape, jnp.float32)] * PLANE,
        grid_spec=pltpu.PrefetchScalarGridSpec(
            num_scalar_prefetch=2,
            grid=(steps,),
            in_specs=[block] * (PLANE + count) + [table] * 2,
            out_specs=[pl.BlockSpec(shape, lambda f, cols, half: (0, 0, 0))] * PLANE,
            scratch_shapes=[
                pltpu.VMEM((PLANE, width, 2 * tile), jnp.bfloat16),
                pltpu.VMEM((2, lags * width, 2 * tile), jnp.bfloat16),
                pltpu.VMEM((PLANE, lags * width, PLANE * width), jnp.float32),
            ],
        ),
        compiler_params=pltpu.CompilerParams(vmem_limit_bytes=40 * 1024 * 1024),
        cost_estimate=pl.CostEstimate(
            flops=2 * PLANE * lags * width * PLANE * width * 2 * bins,
            bytes_accessed=4 * 4 * 2 * width * bins + 4 * PLANE * width * lags * width,
            transcendentals=0,
        ),
    )(cols, half, *own, *other, *tables)


def final_kernel(norm, q_ref, flags_ref, *refs):
    same, near, far = refs[0:3], refs[3:6], refs[6:9]
    out = refs[9]
    q = q_ref[0]

    def emit(parts, j, d):
        scale = flags_ref[d].astype(jnp.float32) * norm
        out[0, d] = (parts[0][j] + parts[1][j] + parts[2][j]) * scale

    for j in range(PLANE):
        emit(near, j, PLANE + q - j)

        @pl.when(j <= q)
        def _():
            emit(same, j, q - j)

        if j > 0:
            @pl.when(j > q)
            def _():
                scale = flags_ref[2 * PLANE + q - j].astype(jnp.float32) * norm
                out[0, 2 * PLANE + q - j] = (far[0][j - 1] + far[1][j - 1] + far[2][j - 1]) * scale


def per_device(spectra, pair_valid):
    own = spectra[0]
    segments, _, width, bins = own.shape
    steps = pair_valid.shape[1]
    lags = 8
    ring = 2 * steps
    stride = lax.axis_size("chan") // ring
    place = lax.axis_index("chan") // stride
    q = lax.rem(place, PLANE)
    y, c = q // 2, lax.rem(q, 2)
    half_bins = bins // 2
    norm = 1.0 / math.sqrt(2.0 * segments * bins)
    tables = [jnp.asarray(t) for t in lag_rows(bins, lags)]

    def move(value, to):
        pairs = [
            (r * stride + s, to(r) * stride + s) for r in range(ring) for s in range(stride)
        ]
        return lax.ppermute(value, "chan", pairs)

    def to_plane(k):
        return lambda r: r - r % PLANE + ((r % PLANE) ^ k)

    def up(r):
        return (r + PLANE) % ring

    def piece(k):
        s = y ^ (k >> 1)
        h = c ^ (k & 1)
        return lax.dynamic_slice(own, (s, 0, 0, h * half_bins), (1, 2, width, half_bins))[0]

    sib = move(piece(1), to_plane(1))
    mine = piece(0)
    cross = move(piece(2), to_plane(2))
    diag = move(piece(3), to_plane(3))
    here = [mine, sib, cross, diag]
    near = [move(x, up) for x in here]
    odd = c == 1
    low = y == 0
    first_send = jnp.where(odd, near[0], near[1])
    even_send = jnp.where(odd, near[1], near[0])
    second_send = jnp.where(low, near[2], even_send)
    third_send = jnp.where(low, near[3], jnp.where(odd, near[2], near[3]))
    far = [move(x, up) for x in (first_send, second_send, third_send)]

    slots = jnp.stack([q ^ k for k in range(PLANE)]).astype(jnp.int32)
    far_slots = jnp.stack([
        jnp.where(low, 1, 3), jnp.where(low, q ^ 2, 2), jnp.where(low, q ^ 3, 1)
    ]).astype(jnp.int32)
    half = c.astype(jnp.int32)[None]

    def reduced(parts):
        from_sib = move(parts[1], to_plane(1))
        pass_on = parts[2] + move(parts[3], to_plane(1))
        return [parts[0], from_sib, move(pass_on, to_plane(2))]

    same_sum = reduced(pair_products(here, here, slots, half, tables, lags, 0))
    near_sum = reduced(pair_products(here, near, slots, half, tables, lags, 0))
    far_sum = reduced(pair_products(here, far, far_slots, half, tables, lags, 1))

    return pl.pallas_call(
        functools.partial(final_kernel, norm),
        out_shape=jax.ShapeDtypeStruct((1, steps, width, lags * width), jnp.float32),
        in_specs=[pl.BlockSpec(memory_space=pltpu.SMEM)] * 2
        + [pl.BlockSpec(memory_space=pltpu.VMEM)] * 9,
        out_specs=pl.BlockSpec(memory_space=pltpu.VMEM),
        compiler_params=pltpu.CompilerParams(vmem_limit_bytes=40 * 1024 * 1024),
    )(q.astype(jnp.int32)[None], pair_valid[0], *same_sum, *near_sum, *far_sum)


def solution(mesh):
    return jax.shard_map(
        per_device,
        mesh=mesh,
        in_specs=(P(("groups", "chan"), None, None, None, None), P(("groups", "chan"), None)),
        out_specs=P(("groups", "chan"), None, None, None),
        check_vma=False,
    )
```

time: 253 us -> 144 us (0.57)
  matrix products: 66.3 us -> 0 us
  Pallas kernels: 0 us -> 46 us
  waiting for transfers between devices: 122 us -> 77.4 us
  other arithmetic: 28.5 us -> 0.49 us
  local copies, waits for them, and re-layouts: 29.6 us -> 1.67 us
  starting transfers between devices: 0.47 us -> 17.9 us
  loops' own time: 4.71 us -> 0 us
    dot_general x8 -> x0, matrix products: 66.3 us -> none  [pair_result(): jnp.einsum('itscf,scjf->itj', modulated, moving, preferred_element_type=j...]
    pallas_call x0 -> x4, Pallas kernels: none -> 46 us  [the longest x3 44.3 us: pair_products(): pl.pallas_call(functools.partial(pair_kernel, lags, steps, first, count),...]
    ppermute x7 -> x19, waiting for transfers between devices: 122 us -> 77.4 us  [move(): return lax.ppermute(value, 'chan', pairs)]
    ppermute x7 -> x19, starting transfers between devices: 0.47 us -> 17.9 us  [move(): return lax.ppermute(value, 'chan', pairs)]
    another operation x8 -> x0, local copies, waits for them, and re-layouts: 11.7 us -> none
    another operation x10 -> x2, other arithmetic: 11.8 us -> 0.15 us  [the longest x1 0.08 us: per_device(): slots = jnp.stack([q ^ k for k in range(PLANE)]).astype(jnp.int32)]
    unnamed x11 -> x6, local copies, waits for them, and re-layouts: 8.86 us -> 0.02 us
    convert_element_type x2 -> x0, other arithmetic: 8.73 us -> none  [the longest x1 6.71 us: modulate(): return jnp.transpose(stacked, (2, 3, 0, 1, 4)).astype(jnp.bfloat16)]
  transfers between devices with their start and end apart: 7 -> 19, of which waited for: 7 -> 9; matrix products, arithmetic and copies ran while one was open for 28% -> 0% of each run, Pallas kernels for 0% -> 31%
where the time goes in v1:
time: 144 us
  waiting for transfers between devices  77.4 us (54%)
  Pallas kernels  46 us (32%)
  starting transfers between devices  17.9 us (12%)
  local copies, waits for them, and re-layouts  1.67 us (1%)
    ppermute x19, waiting for transfers between devices, move(): return lax.ppermute(value, 'chan', pairs)  77.4 us
    pallas_call x3, Pallas kernels, pair_products(): pl.pallas_call(functools.partial(pair_kernel, lags, steps, first, count),...  44.3 us
    ppermute x19, starting transfers between devices, move(): return lax.ppermute(value, 'chan', pairs)  17.9 us
  transfers between devices with their start and end apart: 19, of which 9 were waited for; matrix products, arithmetic and copies ran while one was open for 0% of the time, Pallas kernels for 31%

profile of v1, /device:TPU:0, one launch (start us, length us, event | category | flops | bytes accessed | tf_op | source)
XLA Modules:
  0.0 143.5 jit_solution(2259704006873148100)
XLA Ops:
  0.0 1.7 %dynamic-slice_bitcast_fusion = (bf16[2,64,2048]{2,1,0:T(8,128)(2,1)S(1)}, bf16[2,64,2048]{2,1,0:T(8,128)(2,1)S(1)}, bf16[2,64,2048]{2,1,0:T(8,128)(2,1)S(1)}, bf16[2,64,2048]{2,1,0:T(8,128)(2,1)S(1)}) fusion(bf16[1,2,2,64,4096]{4,3,2,1,0:T(8,128)(2,1)} %param.4, s32[]{:T(128)S(6)} %select_n.63, s32[]{:T(128)S(6)} %select_n.62, s32[]{:T(128)S(6)} %select_n.60, ...), kind=kLoop, calls=%fused_computation.2 | loop fusion | bytes 4194320 | tf_op jit(solution)/shard_map/squeeze | solution.py:161
  2.2 2.6 %collective-permute-start.1 = (bf16[2,64,2048]{2,1,0:T(8,128)(2,1)S(1)}, bf16[2,64,2048]{2,1,0:T(8,128)(2,1)}, u32[]{:S(2)}, u32[]{:S(2)}) collective-permute-start(bf16[2,64,2048]{2,1,0:T(8,128)(2,1)S(1)} %get-tuple-element.32), channel_id=1, source_target_pairs={{0,2},{1,3},{2,0},{3,1},{4,6},{5,7},{6,4},{7,5},{8,10},{9,11},{10,... | collective-permute-start | bytes 1572872 | tf_op jit(solution)/shard_map/ppermute | solution.py:150
  4.9 1.8 %collective-permute-start.6 = (bf16[2,64,2048]{2,1,0:T(8,128)(2,1)S(1)}, bf16[2,64,2048]{2,1,0:T(8,128)(2,1)S(1)}, u32[]{:S(2)}, u32[]{:S(2)}) collective-permute-start(bf16[2,64,2048]{2,1,0:T(8,128)(2,1)S(1)} %get-tuple-element.31.refs_0_.refs_4_), channel_id=1, source_target_pairs={{0,4},{1,5},{2,6},{3,7},{4,8},{5,9},{6,10},{7,11},{8,12},{9,13},{1... | collective-permute-start | bytes 1572872 | tf_op jit(solution)/shard_map/ppermute | solution.py:150
  6.6 1.6 %collective-permute-start.7 = (bf16[2,64,2048]{2,1,0:T(8,128)(2,1)S(1)}, bf16[2,64,2048]{2,1,0:T(8,128)(2,1)S(1)}, u32[]{:S(2)}, u32[]{:S(2)}) collective-permute-start(bf16[2,64,2048]{2,1,0:T(8,128)(2,1)S(1)} %collective-permute-done.refs_1_.refs_5_), channel_id=1, source_target_pairs={{0,4},{1,5},{2,6},{3,7},{4,8},{5,9},{6,10},{7,11},{8,12},{9,13},{1... | collective-permute-start | bytes 1572872 | tf_op jit(solution)/shard_map/ppermute | solution.py:150
  8.2 9.4 %collective-permute-done.1.refs_2_.refs_6_ = bf16[2,64,2048]{2,1,0:T(8,128)(2,1)} collective-permute-done((bf16[2,64,2048]{2,1,0:T(8,128)(2,1)S(1)}, bf16[2,64,2048]{2,1,0:T(8,128)(2,1)}, u32[]{:S(2)}, u32[]{:S(2)}) %collective-permute-start.1) | collective-permute-done | bytes 524320 | tf_op jit(solution)/shard_map/ppermute | solution.py:150
  17.7 2.0 %collective-permute-start.8 = (bf16[2,64,2048]{2,1,0:T(8,128)(2,1)}, bf16[2,64,2048]{2,1,0:T(8,128)(2,1)S(1)}, u32[]{:S(2)}, u32[]{:S(2)}) collective-permute-start(bf16[2,64,2048]{2,1,0:T(8,128)(2,1)} %collective-permute-done.1.refs_2_.refs_6_), channel_id=1, source_target_pairs={{0,4},{1,5},{2,6},{3,7},{4,8},{5,9},{6,10},{7,11},{8,12},{9,13},{1... | collective-permute-start | bytes 1572872 | tf_op jit(solution)/shard_map/ppermute | solution.py:150
  19.7 8.7 %collective-permute-done.2.refs_3_.refs_7_ = bf16[2,64,2048]{2,1,0:T(8,128)(2,1)} collective-permute-done((bf16[2,64,2048]{2,1,0:T(8,128)(2,1)S(1)}, bf16[2,64,2048]{2,1,0:T(8,128)(2,1)}, u32[]{:S(2)}, u32[]{:S(2)}) %collective-permute-start.2) | collective-permute-done | bytes 524320 | tf_op jit(solution)/shard_map/ppermute | solution.py:150
  28.4 1.6 %collective-permute-start.9 = (bf16[2,64,2048]{2,1,0:T(8,128)(2,1)}, bf16[2,64,2048]{2,1,0:T(8,128)(2,1)S(1)}, u32[]{:S(2)}, u32[]{:S(2)}) collective-permute-start(bf16[2,64,2048]{2,1,0:T(8,128)(2,1)} %collective-permute-done.2.refs_3_.refs_7_), channel_id=1, source_target_pairs={{0,4},{1,5},{2,6},{3,7},{4,8},{5,9},{6,10},{7,11},{8,12},{9,13},{1... | collective-permute-start | bytes 1572872 | tf_op jit(solution)/shard_map/ppermute | solution.py:150
  30.2 2.4 %collective-permute-done.7.refs_5_ = bf16[2,64,2048]{2,1,0:T(8,128)(2,1)S(1)} collective-permute-done((bf16[2,64,2048]{2,1,0:T(8,128)(2,1)S(1)}, bf16[2,64,2048]{2,1,0:T(8,128)(2,1)S(1)}, u32[]{:S(2)}, u32[]{:S(2)}) %collective-permute-start.7) | collective-permute-done | bytes 524320 | tf_op jit(solution)/shard_map/ppermute | solution.py:150
  32.6 11.2 %collective-permute-done.8.refs_6_ = bf16[2,64,2048]{2,1,0:T(8,128)(2,1)S(1)} collective-permute-done((bf16[2,64,2048]{2,1,0:T(8,128)(2,1)}, bf16[2,64,2048]{2,1,0:T(8,128)(2,1)S(1)}, u32[]{:S(2)}, u32[]{:S(2)}) %collective-permute-start.8) | collective-permute-done | bytes 524320 | tf_op jit(solution)/shard_map/ppermute | solution.py:150
  43.8 11.0 %collective-permute-done.9.refs_7_ = bf16[2,64,2048]{2,1,0:T(8,128)(2,1)S(1)} collective-permute-done((bf16[2,64,2048]{2,1,0:T(8,128)(2,1)}, bf16[2,64,2048]{2,1,0:T(8,128)(2,1)S(1)}, u32[]{:S(2)}, u32[]{:S(2)}) %collective-permute-start.9) | collective-permute-done | bytes 524320 | tf_op jit(solution)/shard_map/ppermute | solution.py:150
  55.0 1.3 collective-permute-start.14
  56.3 1.6 %collective-permute-start.15 = (bf16[2,64,2048]{2,1,0:T(8,128)(2,1)S(1)}, bf16[2,64,2048]{2,1,0:T(8,128)(2,1)S(1)}, u32[]{:S(2)}, u32[]{:S(2)}) collective-permute-start(bf16[2,64,2048]{2,1,0:T(8,128)(2,1)S(1)} %get-tuple-element.35), channel_id=1, source_target_pairs={{0,4},{1,5},{2,6},{3,7},{4,8},{5,9},{6,10},{7,11},{8,12},{9,13},{1... | collective-permute-start | bytes 1572872 | tf_op jit(solution)/shard_map/ppermute | solution.py:150
  57.9 14.9 %shard_map.46 = (f32[4,64,512]{2,1,0:T(8,128)S(1)}, f32[4,64,512]{2,1,0:T(8,128)S(1)}, f32[4,64,512]{2,1,0:T(8,128)S(1)}, f32[4,64,512]{2,1,0:T(8,128)S(1)}) custom-call(s32[4]{0:T(128)S(1)} %pad_add_fusion.cols_ref, s32[1]{0:T(128)} %bitcast.5.half_ref, bf16[2,64,2048]{2,1,0:T(8,128)(2,1)S(1)} %get-tuple-element.31.refs_0_.refs_4_, ...), custom_call_target="tpu_custom_call" | custom-call | flops 4294967296 | bytes 4718592 | tf_op jit(solution)/shard_map/pallas_call | solution.py:86
  73.3 14.8 %shard_map.47 = (f32[4,64,512]{2,1,0:T(8,128)S(1)}, f32[4,64,512]{2,1,0:T(8,128)S(1)}, f32[4,64,512]{2,1,0:T(8,128)S(1)}, f32[4,64,512]{2,1,0:T(8,128)S(1)}) custom-call(s32[4]{0:T(128)S(1)} %pad_add_fusion.cols_ref, s32[1]{0:T(128)} %bitcast.5.half_ref, bf16[2,64,2048]{2,1,0:T(8,128)(2,1)S(1)} %get-tuple-element.31.refs_0_.refs_4_, ...), custom_call_target="tpu_custom_call" | custom-call | flops 4294967296 | bytes 4718592 | tf_op jit(solution)/shard_map/pallas_call | solution.py:86
  88.3 4.7 %collective-permute-done.15.refs_6_ = bf16[2,64,2048]{2,1,0:T(8,128)(2,1)S(1)} collective-permute-done((bf16[2,64,2048]{2,1,0:T(8,128)(2,1)S(1)}, bf16[2,64,2048]{2,1,0:T(8,128)(2,1)S(1)}, u32[]{:S(2)}, u32[]{:S(2)}) %collective-permute-start.15) | collective-permute-done | bytes 524320 | tf_op jit(solution)/shard_map/ppermute | solution.py:150
  92.9 14.6 %shard_map.48 = (f32[3,64,512]{2,1,0:T(8,128)S(1)}, f32[3,64,512]{2,1,0:T(8,128)S(1)}, f32[3,64,512]{2,1,0:T(8,128)S(1)}, f32[3,64,512]{2,1,0:T(8,128)S(1)}) custom-call(s32[3]{0:T(128)S(1)} %pad_add_fusion.1.cols_ref, s32[1]{0:T(128)} %bitcast.5.half_ref, bf16[2,64,2048]{2,1,0:T(8,128)(2,1)S(1)} %get-tuple-element.31.refs_0_.refs_4_, ...), custom_call_target="tpu_custom_call" | custom-call | flops 4294967296 | bytes 4718592 | tf_op jit(solution)/shard_map/pallas_call | solution.py:86
  108.2 1.4 collective-permute-start.5
  109.6 0.8 collective-permute-start.12
  110.5 1.4 collective-permute-start.18
  111.9 11.2 %collective-permute-done.5.refs_2_ = f32[4,64,512]{2,1,0:T(8,128)S(1)} collective-permute-done((f32[4,64,512]{2,1,0:T(8,128)S(1)}, f32[4,64,512]{2,1,0:T(8,128)S(1)}, u32[]{:S(2)}, u32[]{:S(2)}) %collective-permute-start.5) | collective-permute-done | bytes 524320 | tf_op jit(solution)/shard_map/ppermute | solution.py:150
  123.0 11.2 %collective-permute-done.12.refs_5_ = f32[4,64,512]{2,1,0:T(8,128)S(1)} collective-permute-done((f32[4,64,512]{2,1,0:T(8,128)S(1)}, f32[4,64,512]{2,1,0:T(8,128)S(1)}, u32[]{:S(2)}, u32[]{:S(2)}) %collective-permute-start.12) | collective-permute-done | bytes 524320 | tf_op jit(solution)/shard_map/ppermute | solution.py:150
  134.3 7.5 %collective-permute-done.18.refs_8_ = f32[3,64,512]{2,1,0:T(8,128)S(1)} collective-permute-done((f32[3,64,512]{2,1,0:T(8,128)S(1)}, f32[3,64,512]{2,1,0:T(8,128)S(1)}, u32[]{:S(2)}, u32[]{:S(2)}) %collective-permute-start.18) | collective-permute-done | bytes 393248 | tf_op jit(solution)/shard_map/ppermute | solution.py:150
  141.8 1.7 %shard_map.49 = f32[1,8,64,512]{3,2,1,0:T(8,128)} custom-call(s32[1]{0:T(128)} %bitcast.q_ref, s32[8]{0:T(128)S(1)} %bitcast.17, f32[4,64,512]{2,1,0:T(8,128)S(1)} %get-tuple-element.17.refs_0_, f32[4,64,512]{2,1,0:T(8,128)S(1)} %collective-permute-done.3.refs_1_, f32[4,64,512]{2,1,0:T(8,128)S(1)} %collective-permute-done.5.refs_2_, ...), custom_call_target="tpu_custom_call" | custom-call | tf_op jit(solution)/shard_map/pallas_call | solution.py:192
  (31 shorter events, 2.5 us)
Async XLA Ops:
  1.7 56.2 %copy-start.1 = (f32[8,4096]{1,0:T(8,128)S(1)}, f32[8,4096]{1,0:T(8,128)}, u32[]{:S(2)}) copy-start(f32[8,4096]{1,0:T(8,128)} %constant.46.clone.refs_8_.refs_7_) | copy-start | bytes 393220
  1.7 56.2 %copy-start.2 = (f32[8,4096]{1,0:T(8,128)S(1)}, f32[8,4096]{1,0:T(8,128)}, u32[]{:S(2)}) copy-start(f32[8,4096]{1,0:T(8,128)} %constant.47.clone.refs_9_.refs_8_) | copy-start | bytes 393220
  1.7 5.0 %collective-permute-start = (bf16[2,64,2048]{2,1,0:T(8,128)(2,1)S(1)}, bf16[2,64,2048]{2,1,0:T(8,128)(2,1)S(1)}, u32[]{:S(2)}, u32[]{:S(2)}) collective-permute-start(bf16[2,64,2048]{2,1,0:T(8,128)(2,1)S(1)} %get-tuple-element.30), channel_id=1, source_target_pairs={{0,1},{1,0},{2,3},{3,2},{4,5},{5,4},{6,7},{7,6},{8,9},{9,8},{10,11... | collective-permute-start | bytes 1572872 | tf_op jit(solution)/shard_map/ppermute | solution.py:150
  2.2 15.5 %collective-permute-start.1 = (bf16[2,64,2048]{2,1,0:T(8,128)(2,1)S(1)}, bf16[2,64,2048]{2,1,0:T(8,128)(2,1)}, u32[]{:S(2)}, u32[]{:S(2)}) collective-permute-start(bf16[2,64,2048]{2,1,0:T(8,128)(2,1)S(1)} %get-tuple-element.32), channel_id=1, source_target_pairs={{0,2},{1,3},{2,0},{3,1},{4,6},{5,7},{6,4},{7,5},{8,10},{9,11},{10,... | collective-permute-start | bytes 1572872 | tf_op jit(solution)/shard_map/ppermute | solution.py:150
  4.8 23.6 %collective-permute-start.2 = (bf16[2,64,2048]{2,1,0:T(8,128)(2,1)S(1)}, bf16[2,64,2048]{2,1,0:T(8,128)(2,1)}, u32[]{:S(2)}, u32[]{:S(2)}) collective-permute-start(bf16[2,64,2048]{2,1,0:T(8,128)(2,1)S(1)} %get-tuple-element.29), channel_id=1, source_target_pairs={{0,3},{1,2},{2,1},{3,0},{4,7},{5,6},{6,5},{7,4},{8,11},{9,10},{10,... | collective-permute-start | bytes 1572872 | tf_op jit(solution)/shard_map/ppermute | solution.py:150
  4.9 25.3 %collective-permute-start.6 = (bf16[2,64,2048]{2,1,0:T(8,128)(2,1)S(1)}, bf16[2,64,2048]{2,1,0:T(8,128)(2,1)S(1)}, u32[]{:S(2)}, u32[]{:S(2)}) collective-permute-start(bf16[2,64,2048]{2,1,0:T(8,128)(2,1)S(1)} %get-tuple-element.31.refs_0_.refs_4_), channel_id=1, source_target_pairs={{0,4},{1,5},{2,6},{3,7},{4,8},{5,9},{6,10},{7,11},{8,12},{9,13},{1... | collective-permute-start | bytes 1572872 | tf_op jit(solution)/shard_map/ppermute | solution.py:150
  6.6 26.0 %collective-permute-start.7 = (bf16[2,64,2048]{2,1,0:T(8,128)(2,1)S(1)}, bf16[2,64,2048]{2,1,0:T(8,128)(2,1)S(1)}, u32[]{:S(2)}, u32[]{:S(2)}) collective-permute-start(bf16[2,64,2048]{2,1,0:T(8,128)(2,1)S(1)} %collective-permute-done.refs_1_.refs_5_), channel_id=1, source_target_pairs={{0,4},{1,5},{2,6},{3,7},{4,8},{5,9},{6,10},{7,11},{8,12},{9,13},{1... | collective-permute-start | bytes 1572872 | tf_op jit(solution)/shard_map/ppermute | solution.py:150
  17.7 26.2 %collective-permute-start.8 = (bf16[2,64,2048]{2,1,0:T(8,128)(2,1)}, bf16[2,64,2048]{2,1,0:T(8,128)(2,1)S(1)}, u32[]{:S(2)}, u32[]{:S(2)}) collective-permute-start(bf16[2,64,2048]{2,1,0:T(8,128)(2,1)} %collective-permute-done.1.refs_2_.refs_6_), channel_id=1, source_target_pairs={{0,4},{1,5},{2,6},{3,7},{4,8},{5,9},{6,10},{7,11},{8,12},{9,13},{1... | collective-permute-start | bytes 1572872 | tf_op jit(solution)/shard_map/ppermute | solution.py:150
  28.4 26.4 %collective-permute-start.9 = (bf16[2,64,2048]{2,1,0:T(8,128)(2,1)}, bf16[2,64,2048]{2,1,0:T(8,128)(2,1)S(1)}, u32[]{:S(2)}, u32[]{:S(2)}) collective-permute-start(bf16[2,64,2048]{2,1,0:T(8,128)(2,1)} %collective-permute-done.2.refs_3_.refs_7_), channel_id=1, source_target_pairs={{0,4},{1,5},{2,6},{3,7},{4,8},{5,9},{6,10},{7,11},{8,12},{9,13},{1... | collective-permute-start | bytes 1572872 | tf_op jit(solution)/shard_map/ppermute | solution.py:150
  54.9 33.2 %collective-permute-start.13 = (bf16[2,64,2048]{2,1,0:T(8,128)(2,1)S(1)}, bf16[2,64,2048]{2,1,0:T(8,128)(2,1)S(1)}, u32[]{:S(2)}, u32[]{:S(2)}) collective-permute-start(bf16[2,64,2048]{2,1,0:T(8,128)(2,1)S(1)} %get-tuple-element.34), channel_id=1, source_target_pairs={{0,4},{1,5},{2,6},{3,7},{4,8},{5,9},{6,10},{7,11},{8,12},{9,13},{1... | collective-permute-start | bytes 1572872 | tf_op jit(solution)/shard_map/ppermute | solution.py:150
  55.0 33.3 %collective-permute-start.14 = (bf16[2,64,2048]{2,1,0:T(8,128)(2,1)S(1)}, bf16[2,64,2048]{2,1,0:T(8,128)(2,1)S(1)}, u32[]{:S(2)}, u32[]{:S(2)}) collective-permute-start(bf16[2,64,2048]{2,1,0:T(8,128)(2,1)S(1)} %get-tuple-element.33), channel_id=1, source_target_pairs={{0,4},{1,5},{2,6},{3,7},{4,8},{5,9},{6,10},{7,11},{8,12},{9,13},{1... | collective-permute-start | bytes 1572872 | tf_op jit(solution)/shard_map/ppermute | solution.py:150
  56.3 36.6 %collective-permute-start.15 = (bf16[2,64,2048]{2,1,0:T(8,128)(2,1)S(1)}, bf16[2,64,2048]{2,1,0:T(8,128)(2,1)S(1)}, u32[]{:S(2)}, u32[]{:S(2)}) collective-permute-start(bf16[2,64,2048]{2,1,0:T(8,128)(2,1)S(1)} %get-tuple-element.35), channel_id=1, source_target_pairs={{0,4},{1,5},{2,6},{3,7},{4,8},{5,9},{6,10},{7,11},{8,12},{9,13},{1... | collective-permute-start | bytes 1572872 | tf_op jit(solution)/shard_map/ppermute | solution.py:150
  72.8 35.4 %collective-permute-start.4 = (f32[4,64,512]{2,1,0:T(8,128)S(1)}, f32[4,64,512]{2,1,0:T(8,128)S(1)}, u32[]{:S(2)}, u32[]{:S(2)}) collective-permute-start(f32[4,64,512]{2,1,0:T(8,128)S(1)} %get-tuple-element.20), channel_id=1, source_target_pairs={{0,1},{1,0},{2,3},{3,2},{4,5},{5,4},{6,7},{7,6},{8,9},{9,8},{10,11... | collective-permute-start | bytes 1572872 | tf_op jit(solution)/shard_map/ppermute | solution.py:150
  72.8 37.7 %collective-permute-start.3 = (f32[4,64,512]{2,1,0:T(8,128)S(1)}, f32[4,64,512]{2,1,0:T(8,128)S(1)}, u32[]{:S(2)}, u32[]{:S(2)}) collective-permute-start(f32[4,64,512]{2,1,0:T(8,128)S(1)} %get-tuple-element.18), channel_id=1, source_target_pairs={{0,1},{1,0},{2,3},{3,2},{4,5},{5,4},{6,7},{7,6},{8,9},{9,8},{10,11... | collective-permute-start | bytes 1572872 | tf_op jit(solution)/shard_map/ppermute | solution.py:150
  88.1 21.4 %collective-permute-start.11 = (f32[4,64,512]{2,1,0:T(8,128)S(1)}, f32[4,64,512]{2,1,0:T(8,128)S(1)}, u32[]{:S(2)}, u32[]{:S(2)}) collective-permute-start(f32[4,64,512]{2,1,0:T(8,128)S(1)} %get-tuple-element.24), channel_id=1, source_target_pairs={{0,1},{1,0},{2,3},{3,2},{4,5},{5,4},{6,7},{7,6},{8,9},{9,8},{10,11... | collective-permute-start | bytes 1572872 | tf_op jit(solution)/shard_map/ppermute | solution.py:150
  107.5 2.9 %collective-permute-start.17 = (f32[3,64,512]{2,1,0:T(8,128)S(1)}, f32[3,64,512]{2,1,0:T(8,128)S(1)}, u32[]{:S(2)}, u32[]{:S(2)}) collective-permute-start(f32[3,64,512]{2,1,0:T(8,128)S(1)} %get-tuple-element.28), channel_id=1, source_target_pairs={{0,1},{1,0},{2,3},{3,2},{4,5},{5,4},{6,7},{7,6},{8,9},{9,8},{10,11... | collective-permute-start | bytes 1179656 | tf_op jit(solution)/shard_map/ppermute | solution.py:150
  107.6 4.3 %collective-permute-start.10 = (f32[4,64,512]{2,1,0:T(8,128)S(1)}, f32[4,64,512]{2,1,0:T(8,128)S(1)}, u32[]{:S(2)}, u32[]{:S(2)}) collective-permute-start(f32[4,64,512]{2,1,0:T(8,128)S(1)} %get-tuple-element.22), channel_id=1, source_target_pairs={{0,1},{1,0},{2,3},{3,2},{4,5},{5,4},{6,7},{7,6},{8,9},{9,8},{10,11... | collective-permute-start | bytes 1572872 | tf_op jit(solution)/shard_map/ppermute | solution.py:150
  108.1 33.7 %copy-start = (s32[1,8]{1,0:T(1,128)S(1)}, s32[1,8]{1,0:T(1,128)}, u32[]{:S(2)}) copy-start(s32[1,8]{1,0:T(1,128)} %param.5) | copy-start | bytes 100
  108.2 14.8 %collective-permute-start.5 = (f32[4,64,512]{2,1,0:T(8,128)S(1)}, f32[4,64,512]{2,1,0:T(8,128)S(1)}, u32[]{:S(2)}, u32[]{:S(2)}) collective-permute-start(f32[4,64,512]{2,1,0:T(8,128)S(1)} %add.31), channel_id=1, source_target_pairs={{0,2},{1,3},{2,0},{3,1},{4,6},{5,7},{6,4},{7,5},{8,10},{9,11},{10,... | collective-permute-start | bytes 1572872 | tf_op jit(solution)/shard_map/ppermute | solution.py:150
  109.6 24.6 %collective-permute-start.12 = (f32[4,64,512]{2,1,0:T(8,128)S(1)}, f32[4,64,512]{2,1,0:T(8,128)S(1)}, u32[]{:S(2)}, u32[]{:S(2)}) collective-permute-start(f32[4,64,512]{2,1,0:T(8,128)S(1)} %add.32), channel_id=1, source_target_pairs={{0,2},{1,3},{2,0},{3,1},{4,6},{5,7},{6,4},{7,5},{8,10},{9,11},{10,... | collective-permute-start | bytes 1572872 | tf_op jit(solution)/shard_map/ppermute | solution.py:150
  110.4 12.6 %collective-permute-start.16 = (f32[3,64,512]{2,1,0:T(8,128)S(1)}, f32[3,64,512]{2,1,0:T(8,128)S(1)}, u32[]{:S(2)}, u32[]{:S(2)}) collective-permute-start(f32[3,64,512]{2,1,0:T(8,128)S(1)} %get-tuple-element.26), channel_id=1, source_target_pairs={{0,1},{1,0},{2,3},{3,2},{4,5},{5,4},{6,7},{7,6},{8,9},{9,8},{10,11... | collective-permute-start | bytes 1179656 | tf_op jit(solution)/shard_map/ppermute | solution.py:150
  110.5 31.3 %collective-permute-start.18 = (f32[3,64,512]{2,1,0:T(8,128)S(1)}, f32[3,64,512]{2,1,0:T(8,128)S(1)}, u32[]{:S(2)}, u32[]{:S(2)}) collective-permute-start(f32[3,64,512]{2,1,0:T(8,128)S(1)} %add.33), channel_id=1, source_target_pairs={{0,2},{1,3},{2,0},{3,1},{4,6},{5,7},{6,4},{7,5},{8,10},{9,11},{10,... | collective-permute-start | bytes 1179656 | tf_op jit(solution)/shard_map/ppermute | solution.py:150

commit v2 on v0

v2 whole, which is shorter than its diff:
```python
import functools
import math

import jax
import jax.numpy as jnp
import ml_dtypes
import numpy as np
from jax import lax
from jax.experimental import pallas as pl
from jax.experimental.pallas import tpu as pltpu
from jax.sharding import PartitionSpec as P

PLANE = 4
LAGS = 8
MID = LAGS // 2
TILE = 512
LIMIT = 40 * 1024 * 1024


def lag_rows(bins):
    rows = np.arange(8)[:, None]
    phase = np.mod(np.arange(bins)[None, :] * rows, 2 * bins)
    angle = phase.astype(np.float64) * (math.pi / bins)

    def rounded(x):
        return x.astype(np.float32).astype(ml_dtypes.bfloat16).astype(np.float32)

    return rounded(np.cos(angle)), rounded(np.sin(angle))


def modulate_into(mod, real_imag, half, cos_ref, sin_ref):
    _, width, bins = real_imag.shape
    for f in range(0, bins, TILE):
        here = slice(f, f + TILE)
        there = slice(bins + f, bins + f + TILE)
        table = pl.ds(pl.multiple_of(half * bins + f, TILE), TILE)
        real = real_imag[0, :, here].astype(jnp.float32)
        imag = real_imag[1, :, here].astype(jnp.float32)
        for lag in range(MID + 1):
            cosine = cos_ref[lag:lag + 1, table]
            sine = sin_ref[lag:lag + 1, table]
            rc, rs, ic, im = real * cosine, real * sine, imag * cosine, imag * sine
            low = slice((MID - lag) * width, (MID - lag + 1) * width)
            mod[low, here] = (rc + im).astype(jnp.bfloat16)
            mod[low, there] = (ic - rs).astype(jnp.bfloat16)
            if 0 < lag < LAGS - MID:
                high = slice((MID + lag) * width, (MID + lag + 1) * width)
                mod[high, here] = (rc - im).astype(jnp.bfloat16)
                mod[high, there] = (ic + rs).astype(jnp.bfloat16)


def gather_columns(rhs, other, cols_ref):
    _, width, bins = other[0].shape
    for n, ref in enumerate(other):
        row = pl.multiple_of(cols_ref[n] * width, width)
        for c in range(2):
            rhs[pl.ds(row, width), c * bins:(c + 1) * bins] = ref[c]


def product(acc, mod, rhs, outs, width):
    acc[...] = lax.dot_general(
        mod[...], rhs[...], (((1,), (1,)), ((), ())), preferred_element_type=jnp.float32
    )
    places = [out.at[j] for out in outs for j in range(out.shape[0])]
    for j, out in enumerate(places):
        for t in range(0, LAGS, 2):
            pair = [acc[u * width:(u + 1) * width, j * width:(j + 1) * width] for u in (t, t + 1)]
            out[:, t * width:(t + 2) * width] = jnp.concatenate(pair, 1)


def plane_kernel(count, skip, half_ref, rows_ref, cols_ref, *refs):
    here, other, refs = refs[:PLANE], refs[PLANE:PLANE + count], refs[PLANE + count:]
    (cos_ref, sin_ref), outs, (mod, rhs, acc) = refs[:2], refs[2:-3], refs[-3:]
    if not count:
        other = here
    each = len(outs) // PLANE
    width = here[0].shape[1]
    gather_columns(rhs, other, cols_ref)

    def one(m):
        modulate_into(mod.at[m % 2], here[m], half_ref[0], cos_ref, sin_ref)
        product(acc, mod.at[m % 2], rhs, outs[m * each:(m + 1) * each], width)

    for m in range(PLANE):
        if skip is None:
            one(m)
        else:
            pl.when(rows_ref[m] != skip)(functools.partial(one, m))


def last_kernel(half_ref, rows_ref, cols_ref, *refs):
    here, (other, cos_ref, sin_ref, out, mod, rhs, acc) = refs[:PLANE], refs[PLANE:]
    gather_columns(rhs, [other], cols_ref)
    for m in range(PLANE):
        @pl.when(rows_ref[m] == 0)
        def _():
            modulate_into(mod.at[0], here[m], half_ref[0], cos_ref, sin_ref)
    product(acc, mod.at[0], rhs, [out], here[0].shape[1])


def products(here, other, half, rows, cols, tables, skip=None, last=False):
    count = len(other)
    _, width, bins = here[0].shape
    columns = (count or PLANE) * width
    body = last_kernel if last else functools.partial(plane_kernel, count, skip)
    shape = (1 if last else 2, width, LAGS * width)
    outs = [jax.ShapeDtypeStruct(shape, jnp.float32)]
    if not last:
        outs = outs * (PLANE * (count or PLANE) // 2)
    arrays = [*here, *other, *tables]

    def whole(x):
        zeros = (0,) * len(x.shape)
        return pl.BlockSpec(x.shape, lambda *_: zeros)

    return pl.pallas_call(
        body,
        out_shape=outs,
        grid_spec=pltpu.PrefetchScalarGridSpec(
            num_scalar_prefetch=3,
            grid=(1,),
            in_specs=[whole(x) for x in arrays],
            out_specs=[whole(x) for x in outs],
            scratch_shapes=[
                pltpu.VMEM((1 if last else 2, LAGS * width, 2 * bins), jnp.bfloat16),
                pltpu.VMEM((columns, 2 * bins), jnp.bfloat16),
                pltpu.VMEM((LAGS * width, columns), jnp.float32),
            ],
        ),
        compiler_params=pltpu.CompilerParams(vmem_limit_bytes=LIMIT),
        cost_estimate=pl.CostEstimate(flops=1024, bytes_accessed=1024, transcendentals=0),
    )(half, rows, cols, *arrays)


def final_kernel(norm, q_ref, flags_ref, *refs):
    same, near, far, last = refs[0:5], refs[5:10], refs[10:13], refs[13:17]
    out = refs[17]
    q = q_ref[0]

    def emit(total, d):
        out[0, d] = total * (flags_ref[d].astype(jnp.float32) * norm)

    def plane_sum(parts, j):
        each = len(parts) // 2
        n, r = divmod(j, 2)
        return parts[n][r] + parts[each + n][r] + parts[-1][j]

    for j in range(PLANE):
        emit(plane_sum(near, j), PLANE + q - j)

        @pl.when(j <= q)
        def _():
            emit(plane_sum(same, j), q - j)

    for j in (2, 3):
        @pl.when(j > q)
        def _():
            emit(plane_sum(far, j - 2), 2 * PLANE + q - j)

    @pl.when(q == 0)
    def _():
        emit(last[0][0] + last[1][0] + last[2][0] + last[3][0], 2 * PLANE - 1)


def per_device(spectra, pair_valid):
    own = spectra[0]
    segments, _, width, bins = own.shape
    steps = pair_valid.shape[1]
    ring = 2 * steps
    stride = lax.axis_size("chan") // ring
    place = lax.axis_index("chan") // stride
    q = lax.rem(place, PLANE).astype(jnp.int32)
    y, c = q // 2, lax.rem(q, 2)
    half_bins = bins // 2
    norm = 1.0 / math.sqrt(2.0 * segments * bins)
    tables = [jnp.asarray(t) for t in lag_rows(bins)]

    def move(value, to, only=None):
        pairs = [
            (r * stride + s, to(r) * stride + s)
            for r in range(ring) if only is None or r % PLANE == only for s in range(stride)
        ]
        return lax.ppermute(value, "chan", pairs)

    def to_plane(k):
        return lambda r: r - r % PLANE + ((r % PLANE) ^ k)

    def up(r):
        return (r + PLANE) % ring

    def ints(*values):
        return jnp.stack([jnp.asarray(v, jnp.int32) for v in values])

    def piece(block, k):
        s = y ^ (k >> 1)
        h = c ^ (k & 1)
        return lax.dynamic_slice(block, (s, 0, 0, h * half_bins), (1, 2, width, half_bins))[0]

    def after(values, *others):
        return lax.optimization_barrier((*values, *others))[:len(values)]

    def in_core(parts):
        each = len(parts) // PLANE
        rows = [parts[m * each:(m + 1) * each] for m in range(PLANE)]
        got = [[move(x, to_plane(1)) for x in row] for row in rows[1::2]]
        passed = [a + b for a, b in zip(rows[2], got[1])]
        return rows[0], got[0], jnp.concatenate(passed, 0)

    def across(sums):
        return [*sums[0], *sums[1], move(sums[2], to_plane(2))]

    slots = ints(*[q ^ k for k in range(PLANE)])

    mine = piece(own, 0)
    (rest,) = after([own], mine)
    near0 = move(mine, up)
    sib, cross, diag = [move(piece(rest, k), to_plane(k)) for k in range(1, PLANE)]
    near1 = move(sib, up)
    (cross,) = after([cross], near0)
    near2 = move(cross, up)
    (diag,) = after([diag], near1)
    near3 = move(diag, up)
    here = [mine, sib, cross, diag]
    near = [near0, near1, near2, near3]
    half = ints(c)
    same_core = in_core(products(here, [], half, slots, slots, tables))
    same_sum = across(same_core)

    odd = c == 1
    low = y == 0
    far = [move(jnp.where(low, near2, near0), up)]
    send = jnp.where(low, near3, near1)
    far.append(move(send, up))
    a, b, d, e = after(near, send)
    last_send = jnp.where(low, jnp.where(odd, a, b), jnp.where(odd, d, e))
    last = move(last_send, up)

    near_core = in_core(
        products(here, after(near, same_core[2], last_send), half, slots, slots, tables)
    )
    near_sum = across(near_core)
    far_core = in_core(products(
        here, after(far, near_core[2], same_sum[2]), half, slots, ints(c, 1 - c), tables,
        skip=PLANE - 1,
    ))
    far_sum = across(far_core)
    (last_part,) = products(
        here, after([last], far_core[2]), half, slots, ints(0), tables, last=True
    )
    last_sum = [last_part] + [move(last_part, to_plane(k), k) for k in (1, 2, 3)]

    return pl.pallas_call(
        functools.partial(final_kernel, norm),
        out_shape=jax.ShapeDtypeStruct((1, steps, width, LAGS * width), jnp.float32),
        in_specs=[pl.BlockSpec(memory_space=pltpu.SMEM)] * 2
        + [pl.BlockSpec(memory_space=pltpu.VMEM)] * 17,
        out_specs=pl.BlockSpec(memory_space=pltpu.VMEM),
        compiler_params=pltpu.CompilerParams(vmem_limit_bytes=LIMIT),
    )(ints(q), pair_valid[0], *same_sum, *near_sum, *far_sum, *last_sum)


def solution(mesh):
    return jax.shard_map(
        per_device,
        mesh=mesh,
        in_specs=(P(("groups", "chan"), None, None, None, None), P(("groups", "chan"), None)),
        out_specs=P(("groups", "chan"), None, None, None),
        check_vma=False,
    )
```

time: 253 us -> 108 us (0.43)
  waiting for transfers between devices: 122 us -> 54.3 us
  matrix products: 66.3 us -> 0 us
  Pallas kernels: 0 us -> 25 us
  other arithmetic: 28.5 us -> 4.17 us
  local copies, waits for them, and re-layouts: 29.6 us -> 7.2 us
  starting transfers between devices: 0.47 us -> 16.1 us
  loops' own time: 4.71 us -> 0 us
    ppermute x7 -> x26, waiting for transfers between devices: 122 us -> 54.3 us  [move(): return lax.ppermute(value, 'chan', pairs)]
    dot_general x8 -> x0, matrix products: 66.3 us -> none  [pair_result(): jnp.einsum('itscf,scjf->itj', modulated, moving, preferred_element_type=j...]
    pallas_call x0 -> x5, Pallas kernels: none -> 25 us  [the longest x4 22.8 us: products(): pl.pallas_call(body, out_shape=outs, grid_spec=pltpu.PrefetchScalarGridSp...]
    ppermute x7 -> x26, starting transfers between devices: 0.47 us -> 16.1 us  [move(): return lax.ppermute(value, 'chan', pairs)]
    another operation x8 -> x0, local copies, waits for them, and re-layouts: 11.7 us -> none
    another operation x10 -> x2, other arithmetic: 11.8 us -> 0.15 us  [ints(): return jnp.stack([jnp.asarray(v, jnp.int32) for v in values])]
    convert_element_type x2 -> x0, other arithmetic: 8.73 us -> none  [the longest x1 6.71 us: modulate(): return jnp.transpose(stacked, (2, 3, 0, 1, 4)).astype(jnp.bfloat16)]
    scatter x8 -> x0, other arithmetic: 7.32 us -> none  [place(): return output.at[0, distance].set(value)]
  transfers between devices with their start and end apart: 7 -> 26, of which waited for: 7 -> 13; matrix products, arithmetic and copies ran while one was open for 28% -> 4% of each run, Pallas kernels for 0% -> 21%
where the time goes in v2:
time: 108 us; the launch traced here: 107 us
  waiting for transfers between devices  54.3 us (50%)
  Pallas kernels  25 us (23%)
  starting transfers between devices  16.1 us (15%)
  local copies, waits for them, and re-layouts  7.2 us (7%)
  other arithmetic  4.17 us (4%)
    ppermute x26, waiting for transfers between devices, move(): return lax.ppermute(value, 'chan', pairs)  54.3 us
    pallas_call x4, Pallas kernels, products(): pl.pallas_call(body, out_shape=outs, grid_spec=pltpu.PrefetchScalarGridSp...  22.8 us
    ppermute x26, starting transfers between devices, move(): return lax.ppermute(value, 'chan', pairs)  16.1 us
    unnamed x38, local copies, waits for them, and re-layouts  3.77 us
    squeeze x2, local copies, waits for them, and re-layouts, piece(): lax.dynamic_slice(block, (s, 0, 0, h * half_bins), (1, 2, width, half_bins))  3.43 us
    pallas_call x1, Pallas kernels, per_device(): pl.pallas_call(functools.partial(final_kernel, norm), out_shape=jax.Shape...  2.24 us
  transfers between devices with their start and end apart: 26, of which 13 were waited for; matrix products, arithmetic and copies ran while one was open for 4% of the time, Pallas kernels for 21%

profile of v2, /device:TPU:0, one launch (start us, length us, event | category | flops | bytes accessed | tf_op | source)
XLA Modules:
  0.0 107.2 jit_solution(14468608279803973555)
XLA Ops:
  0.0 1.1 %dynamic-slice_bitcast_fusion.3.refs_0_ = bf16[2,64,2048]{2,1,0:T(8,128)(2,1)S(1)} fusion(bf16[1,2,2,64,4096]{4,3,2,1,0:T(8,128)(2,1)} %param.4, s32[]{:T(128)S(6)} %select_n.49, s32[]{:T(128)S(6)} %select_n.50), kind=kLoop, calls=%fused_computation.6 | loop fusion | bytes 1048584 | tf_op jit(solution)/shard_map/squeeze | solution.py:197
  1.1 2.3 %dynamic-slice_bitcast_fusion = (bf16[2,64,2048]{2,1,0:T(8,128)(2,1)}, bf16[2,64,2048]{2,1,0:T(8,128)(2,1)S(1)}, bf16[2,64,2048]{2,1,0:T(8,128)(2,1)S(1)}) fusion(bf16[2,2,64,4096]{3,2,1,0:T(8,128)(2,1)} %bitcast.17, s32[]{:T(128)S(6)} %select_n.52, s32[]{:T(128)S(6)} %select_n.51, s32[]{:T(128)S(6)} %select_n.50, s32[]{:T(128)S(6)} %select_n.49), kind=kLoop, calls=%fused_computation.3 | loop fusion | bytes 3145744 | tf_op jit(solution)/shard_map/squeeze | solution.py:197
  3.9 2.5 %collective-permute-start.1 = (bf16[2,64,2048]{2,1,0:T(8,128)(2,1)S(1)}, bf16[2,64,2048]{2,1,0:T(8,128)(2,1)S(1)}, u32[]{:S(2)}, u32[]{:S(2)}) collective-permute-start(bf16[2,64,2048]{2,1,0:T(8,128)(2,1)S(1)} %get-tuple-element.74), channel_id=1, source_target_pairs={{0,2},{1,3},{2,0},{3,1},{4,6},{5,7},{6,4},{7,5},{8,10},{9,11},{10,... | collective-permute-start | bytes 1572872 | tf_op jit(solution)/shard_map/ppermute | solution.py:183
  6.4 1.6 %collective-permute-start.2 = (bf16[2,64,2048]{2,1,0:T(8,128)(2,1)S(1)}, bf16[2,64,2048]{2,1,0:T(8,128)(2,1)S(1)}, u32[]{:S(2)}, u32[]{:S(2)}) collective-permute-start(bf16[2,64,2048]{2,1,0:T(8,128)(2,1)S(1)} %dynamic-slice_bitcast_fusion.3.refs_0_), channel_id=1, source_target_pairs={{0,4},{1,5},{2,6},{3,7},{4,8},{5,9},{6,10},{7,11},{8,12},{9,13},{1... | collective-permute-start | bytes 1572872 | tf_op jit(solution)/shard_map/ppermute | solution.py:183
  8.1 1.6 %collective-permute-start.4 = (bf16[2,64,2048]{2,1,0:T(8,128)(2,1)S(1)}, bf16[2,64,2048]{2,1,0:T(8,128)(2,1)S(1)}, u32[]{:S(2)}, u32[]{:S(2)}) collective-permute-start(bf16[2,64,2048]{2,1,0:T(8,128)(2,1)S(1)} %collective-permute-done.refs_1_), channel_id=1, source_target_pairs={{0,4},{1,5},{2,6},{3,7},{4,8},{5,9},{6,10},{7,11},{8,12},{9,13},{1... | collective-permute-start | bytes 1572872 | tf_op jit(solution)/shard_map/ppermute | solution.py:183
  9.6 9.6 %collective-permute-done.1.refs_2_ = bf16[2,64,2048]{2,1,0:T(8,128)(2,1)S(1)} collective-permute-done((bf16[2,64,2048]{2,1,0:T(8,128)(2,1)S(1)}, bf16[2,64,2048]{2,1,0:T(8,128)(2,1)S(1)}, u32[]{:S(2)}, u32[]{:S(2)}) %collective-permute-start.1) | collective-permute-done | bytes 524320 | tf_op jit(solution)/shard_map/ppermute | solution.py:183
  19.2 3.8 %collective-permute-done.2.refs_4_ = bf16[2,64,2048]{2,1,0:T(8,128)(2,1)S(1)} collective-permute-done((bf16[2,64,2048]{2,1,0:T(8,128)(2,1)S(1)}, bf16[2,64,2048]{2,1,0:T(8,128)(2,1)S(1)}, u32[]{:S(2)}, u32[]{:S(2)}) %collective-permute-start.2) | collective-permute-done | bytes 524320 | tf_op jit(solution)/shard_map/ppermute | solution.py:183
  23.0 7.0 %collective-permute-done.3.refs_3_ = bf16[2,64,2048]{2,1,0:T(8,128)(2,1)S(1)} collective-permute-done((bf16[2,64,2048]{2,1,0:T(8,128)(2,1)}, bf16[2,64,2048]{2,1,0:T(8,128)(2,1)S(1)}, u32[]{:S(2)}, u32[]{:S(2)}) %collective-permute-start.3) | collective-permute-done | bytes 524320 | tf_op jit(solution)/shard_map/ppermute | solution.py:183
  30.1 4.1 %collective-permute-done.4.refs_5_ = bf16[2,64,2048]{2,1,0:T(8,128)(2,1)S(1)} collective-permute-done((bf16[2,64,2048]{2,1,0:T(8,128)(2,1)S(1)}, bf16[2,64,2048]{2,1,0:T(8,128)(2,1)S(1)}, u32[]{:S(2)}, u32[]{:S(2)}) %collective-permute-start.4) | collective-permute-done | bytes 524320 | tf_op jit(solution)/shard_map/ppermute | solution.py:183
  34.2 6.4 %shard_map.46 = (f32[2,64,512]{2,1,0:T(8,128)S(1)}, f32[2,64,512]{2,1,0:T(8,128)S(1)}, f32[2,64,512]{2,1,0:T(8,128)S(1)}, f32[2,64,512]{2,1,0:T(8,128)}, f32[2,6...) custom-call(s32[1]{0:T(128)} %bitcast.2.half_ref, ...), custom_call_target="tpu_custom_call" | custom-call | flops 1024 | bytes 1024 | tf_op jit(solution)/shard_map/pallas_call | solution.py:116
  41.1 4.4 %collective-permute-done.10.refs_6_ = bf16[2,64,2048]{2,1,0:T(8,128)(2,1)} collective-permute-done((bf16[2,64,2048]{2,1,0:T(8,128)(2,1)S(1)}, bf16[2,64,2048]{2,1,0:T(8,128)(2,1)}, u32[]{:S(2)}, u32[]{:S(2)}) %collective-permute-start.10) | collective-permute-done | bytes 524320 | tf_op jit(solution)/shard_map/ppermute | solution.py:183
  45.5 1.1 %broadcast_select_fusion = bf16[2,64,2048]{2,1,0:T(8,128)(2,1)S(1)} fusion(bf16[2,64,2048]{2,1,0:T(8,128)(2,1)} %collective-permute-done.10.refs_6_, bf16[2,64,2048]{2,1,0:T(8,128)(2,1)S(1)} %collective-permute-done.2.refs_4_, pred[]{:T(512)S(6)} %eq.6), kind=kLoop, calls=%fused_computation.7 | loop fusion | flops 262144 | bytes 1572865 | tf_op jit(solution)/shard_map/jit(_where)/select_n | solution.py:231
  47.7 9.0 %collective-permute-done.11.refs_7_ = bf16[2,64,2048]{2,1,0:T(8,128)(2,1)S(1)} collective-permute-done((bf16[2,64,2048]{2,1,0:T(8,128)(2,1)S(1)}, bf16[2,64,2048]{2,1,0:T(8,128)(2,1)S(1)}, u32[]{:S(2)}, u32[]{:S(2)}) %collective-permute-start.11) | collective-permute-done | bytes 524320 | tf_op jit(solution)/shard_map/ppermute | solution.py:183
  58.0 7.2 %shard_map.47 = (f32[2,64,512]{2,1,0:T(8,128)S(1)}, f32[2,64,512]{2,1,0:T(8,128)S(1)}, f32[2,64,512]{2,1,0:T(8,128)}, f32[2,64,512]{2,1,0:T(8,128)S(1)}, f32[2,6...) custom-call(s32[1]{0:T(128)} %bitcast.2.half_ref, ...), custom_call_target="tpu_custom_call" | custom-call | flops 1024 | bytes 1024 | tf_op jit(solution)/shard_map/pallas_call | solution.py:116
  67.1 1.3 %collective-permute-start.22 = (bf16[2,64,2048]{2,1,0:T(8,128)(2,1)}, bf16[2,64,2048]{2,1,0:T(8,128)(2,1)}, u32[]{:S(2)}, u32[]{:S(2)}) collective-permute-start(bf16[2,64,2048]{2,1,0:T(8,128)(2,1)} %select_select_fusion), channel_id=1, source_target_pairs={{0,4},{1,5},{2,6},{3,7},{4,8},{5,9},{6,10},{7,11},{8,12},{9,13},{1... | collective-permute-start | bytes 1572872 | tf_op jit(solution)/shard_map/ppermute | solution.py:183
  70.9 8.3 %collective-permute-done.18.refs_5_ = bf16[2,64,2048]{2,1,0:T(8,128)(2,1)S(1)} collective-permute-done((bf16[2,64,2048]{2,1,0:T(8,128)(2,1)S(1)}, bf16[2,64,2048]{2,1,0:T(8,128)(2,1)S(1)}, u32[]{:S(2)}, u32[]{:S(2)}) %collective-permute-start.18) | collective-permute-done | bytes 524320 | tf_op jit(solution)/shard_map/ppermute | solution.py:183
  82.4 5.3 %shard_map.48 = (f32[2,64,512]{2,1,0:T(8,128)S(1)}, f32[2,64,512]{2,1,0:T(8,128)S(1)}, f32[2,64,512]{2,1,0:T(8,128)S(1)}, f32[2,64,512]{2,1,0:T(8,128)S(1)}) custom-call(s32[1]{0:T(128)} %bitcast.2.half_ref, s32[4]{0:T(128)S(1)} %pad_add_fusion.rows_ref.cols_ref, s32[2]{0:T(128)S(1)} %pad_add_fusion.1.cols_ref, ...), custom_call_target="tpu_custom_call" | custom-call | flops 1024 | bytes 1024 | tf_op jit(solution)/shard_map/pallas_call | solution.py:116
  89.9 1.6 %collective-permute-start.21 = (f32[2,64,512]{2,1,0:T(8,128)S(1)}, f32[2,64,512]{2,1,0:T(8,128)S(1)}, u32[]{:S(2)}, u32[]{:S(2)}) collective-permute-start(f32[2,64,512]{2,1,0:T(8,128)S(1)} %add.41), channel_id=1, source_target_pairs={{0,2},{1,3},{2,0},{3,1},{4,6},{5,7},{6,4},{7,5},{8,10},{9,11},{10,... | collective-permute-start | bytes 786440 | tf_op jit(solution)/shard_map/ppermute | solution.py:183
  91.4 3.9 %shard_map.49.refs_13_ = f32[1,64,512]{2,1,0:T(8,128)S(1)} custom-call(s32[1]{0:T(128)} %bitcast.2.half_ref, s32[4]{0:T(128)S(1)} %pad_add_fusion.rows_ref.cols_ref, s32[1]{0:T(128)} %constant.44.clone.1.cols_ref, bf16[2,64,2048]{2,1,0:T(8,128)(2,1)S(1)} %dynamic-slice_bitcast_fusion.3.refs_0_, bf16[2,64,2048]{2,1,0:T(8,128)(2,1)S(1)} %collective-permute-done.refs_1_, ...), custom_call_target="tpu_custom_call" | custom-call | flops 1024 | bytes 1024 | tf_op jit(solution)/shard_map/pallas_call | solution.py:116
  95.3 1.3 %collective-permute-start.23 = (f32[1,64,512]{2,1,0:T(8,128)S(1)}, f32[1,64,512]{2,1,0:T(8,128)S(1)}, u32[]{:S(2)}, u32[]{:S(2)}) collective-permute-start(f32[1,64,512]{2,1,0:T(8,128)S(1)} %shard_map.49.refs_13_), channel_id=1, source_target_pairs={{1,0},{5,4},{9,8},{13,12},{17,16},{21,20},{25,24},{29,28}} | collective-permute-start | bytes 393224 | tf_op jit(solution)/shard_map/ppermute | solution.py:183
  96.6 1.3 %collective-permute-start.24 = (f32[1,64,512]{2,1,0:T(8,128)S(1)}, f32[1,64,512]{2,1,0:T(8,128)S(1)}, u32[]{:S(2)}, u32[]{:S(2)}) collective-permute-start(f32[1,64,512]{2,1,0:T(8,128)S(1)} %shard_map.49.refs_13_), channel_id=1, source_target_pairs={{2,0},{6,4},{10,8},{14,12},{18,16},{22,20},{26,24},{30,28}} | collective-permute-start | bytes 393224 | tf_op jit(solution)/shard_map/ppermute | solution.py:183
  97.9 1.3 %collective-permute-start.25 = (f32[1,64,512]{2,1,0:T(8,128)S(1)}, f32[1,64,512]{2,1,0:T(8,128)S(1)}, u32[]{:S(2)}, u32[]{:S(2)}) collective-permute-start(f32[1,64,512]{2,1,0:T(8,128)S(1)} %shard_map.49.refs_13_), channel_id=1, source_target_pairs={{3,0},{7,4},{11,8},{15,12},{19,16},{23,20},{27,24},{31,28}} | collective-permute-start | bytes 393224 | tf_op jit(solution)/shard_map/ppermute | solution.py:183
  99.3 4.9 %collective-permute-done.24.refs_15_ = f32[1,64,512]{2,1,0:T(8,128)S(1)} collective-permute-done((f32[1,64,512]{2,1,0:T(8,128)S(1)}, f32[1,64,512]{2,1,0:T(8,128)S(1)}, u32[]{:S(2)}, u32[]{:S(2)}) %collective-permute-start.24) | collective-permute-done | bytes 131104 | tf_op jit(solution)/shard_map/ppermute | solution.py:183
  104.9 2.2 %shard_map.50 = f32[1,8,64,512]{3,2,1,0:T(8,128)} custom-call(s32[1]{0:T(128)} %bitcast.q_ref, s32[8]{0:T(128)S(1)} %bitcast.16, f32[2,64,512]{2,1,0:T(8,128)S(1)} %copy-done.7, f32[2,64,512]{2,1,0:T(8,128)S(1)} %copy-done.9, f32[2,64,512]{2,1,0:T(8,128)S(1)} %copy-done.15, f32[2,64,512]{2,1,0:T(8,128)} %collective-permute-done.6.refs_3_, ...), custom_call_target="tpu_custom_call" | custom-call | tf_op jit(solution)/shard_map/pallas_call | solution.py:252
  (85 shorter events, 13.7 us)
Async XLA Ops:
  3.4 4.6 %collective-permute-start = (bf16[2,64,2048]{2,1,0:T(8,128)(2,1)S(1)}, bf16[2,64,2048]{2,1,0:T(8,128)(2,1)S(1)}, u32[]{:S(2)}, u32[]{:S(2)}) collective-permute-start(bf16[2,64,2048]{2,1,0:T(8,128)(2,1)S(1)} %get-tuple-element.75), channel_id=1, source_target_pairs={{0,1},{1,0},{2,3},{3,2},{4,5},{5,4},{6,7},{7,6},{8,9},{9,8},{10,11... | collective-permute-start | bytes 1572872 | tf_op jit(solution)/shard_map/ppermute | solution.py:183
  3.9 15.3 %collective-permute-start.1 = (bf16[2,64,2048]{2,1,0:T(8,128)(2,1)S(1)}, bf16[2,64,2048]{2,1,0:T(8,128)(2,1)S(1)}, u32[]{:S(2)}, u32[]{:S(2)}) collective-permute-start(bf16[2,64,2048]{2,1,0:T(8,128)(2,1)S(1)} %get-tuple-element.74), channel_id=1, source_target_pairs={{0,2},{1,3},{2,0},{3,1},{4,6},{5,7},{6,4},{7,5},{8,10},{9,11},{10,... | collective-permute-start | bytes 1572872 | tf_op jit(solution)/shard_map/ppermute | solution.py:183
  6.4 16.5 %collective-permute-start.2 = (bf16[2,64,2048]{2,1,0:T(8,128)(2,1)S(1)}, bf16[2,64,2048]{2,1,0:T(8,128)(2,1)S(1)}, u32[]{:S(2)}, u32[]{:S(2)}) collective-permute-start(bf16[2,64,2048]{2,1,0:T(8,128)(2,1)S(1)} %dynamic-slice_bitcast_fusion.3.refs_0_), channel_id=1, source_target_pairs={{0,4},{1,5},{2,6},{3,7},{4,8},{5,9},{6,10},{7,11},{8,12},{9,13},{1... | collective-permute-start | bytes 1572872 | tf_op jit(solution)/shard_map/ppermute | solution.py:183
  8.0 22.1 %collective-permute-start.3 = (bf16[2,64,2048]{2,1,0:T(8,128)(2,1)}, bf16[2,64,2048]{2,1,0:T(8,128)(2,1)S(1)}, u32[]{:S(2)}, u32[]{:S(2)}) collective-permute-start(bf16[2,64,2048]{2,1,0:T(8,128)(2,1)} %get-tuple-element.73), channel_id=1, source_target_pairs={{0,3},{1,2},{2,1},{3,0},{4,7},{5,6},{6,5},{7,4},{8,11},{9,10},{10,... | collective-permute-start | bytes 1572872 | tf_op jit(solution)/shard_map/ppermute | solution.py:183
  8.1 26.1 %collective-permute-start.4 = (bf16[2,64,2048]{2,1,0:T(8,128)(2,1)S(1)}, bf16[2,64,2048]{2,1,0:T(8,128)(2,1)S(1)}, u32[]{:S(2)}, u32[]{:S(2)}) collective-permute-start(bf16[2,64,2048]{2,1,0:T(8,128)(2,1)S(1)} %collective-permute-done.refs_1_), channel_id=1, source_target_pairs={{0,4},{1,5},{2,6},{3,7},{4,8},{5,9},{6,10},{7,11},{8,12},{9,13},{1... | collective-permute-start | bytes 1572872 | tf_op jit(solution)/shard_map/ppermute | solution.py:183
  23.0 22.6 %collective-permute-start.10 = (bf16[2,64,2048]{2,1,0:T(8,128)(2,1)S(1)}, bf16[2,64,2048]{2,1,0:T(8,128)(2,1)}, u32[]{:S(2)}, u32[]{:S(2)}) collective-permute-start(bf16[2,64,2048]{2,1,0:T(8,128)(2,1)S(1)} %collective-permute-done.1.refs_2_), channel_id=1, source_target_pairs={{0,4},{1,5},{2,6},{3,7},{4,8},{5,9},{6,10},{7,11},{8,12},{9,13},{1... | collective-permute-start | bytes 1572872 | tf_op jit(solution)/shard_map/ppermute | solution.py:183
  34.2 22.5 %collective-permute-start.11 = (bf16[2,64,2048]{2,1,0:T(8,128)(2,1)S(1)}, bf16[2,64,2048]{2,1,0:T(8,128)(2,1)S(1)}, u32[]{:S(2)}, u32[]{:S(2)}) collective-permute-start(bf16[2,64,2048]{2,1,0:T(8,128)(2,1)S(1)} %collective-permute-done.3.refs_3_), channel_id=1, source_target_pairs={{0,4},{1,5},{2,6},{3,7},{4,8},{5,9},{6,10},{7,11},{8,12},{9,13},{1... | collective-permute-start | bytes 1572872 | tf_op jit(solution)/shard_map/ppermute | solution.py:183
  40.6 6.1 %collective-permute-start.8 = (f32[2,64,512]{2,1,0:T(8,128)S(1)}, f32[2,64,512]{2,1,0:T(8,128)S(1)}, u32[]{:S(2)}, u32[]{:S(2)}) collective-permute-start(f32[2,64,512]{2,1,0:T(8,128)S(1)} %get-tuple-element.49), channel_id=1, source_target_pairs={{0,1},{1,0},{2,3},{3,2},{4,5},{5,4},{6,7},{7,6},{8,9},{9,8},{10,11... | collective-permute-start | bytes 786440 | tf_op jit(solution)/shard_map/ppermute | solution.py:183
  40.6 6.1 %collective-permute-start.7 = (f32[2,64,512]{2,1,0:T(8,128)S(1)}, f32[2,64,512]{2,1,0:T(8,128)S(1)}, u32[]{:S(2)}, u32[]{:S(2)}) collective-permute-start(f32[2,64,512]{2,1,0:T(8,128)S(1)} %get-tuple-element.47), channel_id=1, source_target_pairs={{0,1},{1,0},{2,3},{3,2},{4,5},{5,4},{6,7},{7,6},{8,9},{9,8},{10,11... | collective-permute-start | bytes 786440 | tf_op jit(solution)/shard_map/ppermute | solution.py:183
  46.6 22.9 %collective-permute-start.17 = (bf16[2,64,2048]{2,1,0:T(8,128)(2,1)S(1)}, bf16[2,64,2048]{2,1,0:T(8,128)(2,1)S(1)}, u32[]{:S(2)}, u32[]{:S(2)}) collective-permute-start(bf16[2,64,2048]{2,1,0:T(8,128)(2,1)S(1)} %broadcast_select_fusion), channel_id=1, source_target_pairs={{0,4},{1,5},{2,6},{3,7},{4,8},{5,9},{6,10},{7,11},{8,12},{9,13},{1... | collective-permute-start | bytes 1572872 | tf_op jit(solution)/shard_map/ppermute | solution.py:183
  56.7 22.4 %collective-permute-start.18 = (bf16[2,64,2048]{2,1,0:T(8,128)(2,1)S(1)}, bf16[2,64,2048]{2,1,0:T(8,128)(2,1)S(1)}, u32[]{:S(2)}, u32[]{:S(2)}) collective-permute-start(bf16[2,64,2048]{2,1,0:T(8,128)(2,1)S(1)} %broadcast_select_fusion.1), channel_id=1, source_target_pairs={{0,4},{1,5},{2,6},{3,7},{4,8},{5,9},{6,10},{7,11},{8,12},{9,13},{1... | collective-permute-start | bytes 1572872 | tf_op jit(solution)/shard_map/ppermute | solution.py:183
  65.2 1.9 %collective-permute-start.14 = (f32[2,64,512]{2,1,0:T(8,128)S(1)}, f32[2,64,512]{2,1,0:T(8,128)S(1)}, u32[]{:S(2)}, u32[]{:S(2)}) collective-permute-start(f32[2,64,512]{2,1,0:T(8,128)S(1)} %get-tuple-element.63), channel_id=1, source_target_pairs={{0,1},{1,0},{2,3},{3,2},{4,5},{5,4},{6,7},{7,6},{8,9},{9,8},{10,11... | collective-permute-start | bytes 786440 | tf_op jit(solution)/shard_map/ppermute | solution.py:183
  65.7 2.8 %collective-permute-start.5 = (f32[2,64,512]{2,1,0:T(8,128)S(1)}, f32[2,64,512]{2,1,0:T(8,128)S(1)}, u32[]{:S(2)}, u32[]{:S(2)}) collective-permute-start(f32[2,64,512]{2,1,0:T(8,128)S(1)} %get-tuple-element.44), channel_id=1, source_target_pairs={{0,1},{1,0},{2,3},{3,2},{4,5},{5,4},{6,7},{7,6},{8,9},{9,8},{10,11... | collective-permute-start | bytes 786440 | tf_op jit(solution)/shard_map/ppermute | solution.py:183
  66.8 21.0 %collective-permute-start.6 = (f32[2,64,512]{2,1,0:T(8,128)}, f32[2,64,512]{2,1,0:T(8,128)}, u32[]{:S(2)}, u32[]{:S(2)}) collective-permute-start(f32[2,64,512]{2,1,0:T(8,128)} %get-tuple-element.45), channel_id=1, source_target_pairs={{0,1},{1,0},{2,3},{3,2},{4,5},{5,4},{6,7},{7,6},{8,9},{9,8},{10,11... | collective-permute-start | bytes 786440 | tf_op jit(solution)/shard_map/ppermute | solution.py:183
  67.1 22.7 %collective-permute-start.22 = (bf16[2,64,2048]{2,1,0:T(8,128)(2,1)}, bf16[2,64,2048]{2,1,0:T(8,128)(2,1)}, u32[]{:S(2)}, u32[]{:S(2)}) collective-permute-start(bf16[2,64,2048]{2,1,0:T(8,128)(2,1)} %select_select_fusion), channel_id=1, source_target_pairs={{0,4},{1,5},{2,6},{3,7},{4,8},{5,9},{6,10},{7,11},{8,12},{9,13},{1... | collective-permute-start | bytes 1572872 | tf_op jit(solution)/shard_map/ppermute | solution.py:183
  68.6 19.3 %collective-permute-start.12 = (f32[2,64,512]{2,1,0:T(8,128)}, f32[2,64,512]{2,1,0:T(8,128)}, u32[]{:S(2)}, u32[]{:S(2)}) collective-permute-start(f32[2,64,512]{2,1,0:T(8,128)} %get-tuple-element.60), channel_id=1, source_target_pairs={{0,1},{1,0},{2,3},{3,2},{4,5},{5,4},{6,7},{7,6},{8,9},{9,8},{10,11... | collective-permute-start | bytes 786440 | tf_op jit(solution)/shard_map/ppermute | solution.py:183
  70.3 26.3 %collective-permute-start.9 = (f32[4,64,512]{2,1,0:T(8,128)}, f32[4,64,512]{2,1,0:T(8,128)S(1)}, u32[]{:S(2)}, u32[]{:S(2)}) collective-permute-start(f32[4,64,512]{2,1,0:T(8,128)} %pad_maximum_fusion), channel_id=1, source_target_pairs={{0,2},{1,3},{2,0},{3,1},{4,6},{5,7},{6,4},{7,5},{8,10},{9,11},{10,... | collective-permute-start | bytes 1572872 | tf_op jit(solution)/shard_map/ppermute | solution.py:183
  80.0 18.0 %collective-permute-start.16 = (f32[4,64,512]{2,1,0:T(8,128)}, f32[4,64,512]{2,1,0:T(8,128)S(1)}, u32[]{:S(2)}, u32[]{:S(2)}) collective-permute-start(f32[4,64,512]{2,1,0:T(8,128)} %pad_maximum_fusion.1), channel_id=1, source_target_pairs={{0,2},{1,3},{2,0},{3,1},{4,6},{5,7},{6,4},{7,5},{8,10},{9,11},{10,... | collective-permute-start | bytes 1572872 | tf_op jit(solution)/shard_map/ppermute | solution.py:183
  87.9 7.4 %collective-permute-start.13 = (f32[2,64,512]{2,1,0:T(8,128)S(1)}, f32[2,64,512]{2,1,0:T(8,128)S(1)}, u32[]{:S(2)}, u32[]{:S(2)}) collective-permute-start(f32[2,64,512]{2,1,0:T(8,128)S(1)} %copy-done.18), channel_id=1, source_target_pairs={{0,1},{1,0},{2,3},{3,2},{4,5},{5,4},{6,7},{7,6},{8,9},{9,8},{10,11... | collective-permute-start | bytes 786440 | tf_op jit(solution)/shard_map/ppermute | solution.py:183
  89.4 9.9 %collective-permute-start.19 = (f32[2,64,512]{2,1,0:T(8,128)S(1)}, f32[2,64,512]{2,1,0:T(8,128)S(1)}, u32[]{:S(2)}, u32[]{:S(2)}) collective-permute-start(f32[2,64,512]{2,1,0:T(8,128)S(1)} %get-tuple-element.69), channel_id=1, source_target_pairs={{0,1},{1,0},{2,3},{3,2},{4,5},{5,4},{6,7},{7,6},{8,9},{9,8},{10,11... | collective-permute-start | bytes 786440 | tf_op jit(solution)/shard_map/ppermute | solution.py:183
  89.9 15.0 %collective-permute-start.21 = (f32[2,64,512]{2,1,0:T(8,128)S(1)}, f32[2,64,512]{2,1,0:T(8,128)S(1)}, u32[]{:S(2)}, u32[]{:S(2)}) collective-permute-start(f32[2,64,512]{2,1,0:T(8,128)S(1)} %add.41), channel_id=1, source_target_pairs={{0,2},{1,3},{2,0},{3,1},{4,6},{5,7},{6,4},{7,5},{8,10},{9,11},{10,... | collective-permute-start | bytes 786440 | tf_op jit(solution)/shard_map/ppermute | solution.py:183
  95.3 3.9 %collective-permute-start.23 = (f32[1,64,512]{2,1,0:T(8,128)S(1)}, f32[1,64,512]{2,1,0:T(8,128)S(1)}, u32[]{:S(2)}, u32[]{:S(2)}) collective-permute-start(f32[1,64,512]{2,1,0:T(8,128)S(1)} %shard_map.49.refs_13_), channel_id=1, source_target_pairs={{1,0},{5,4},{9,8},{13,12},{17,16},{21,20},{25,24},{29,28}} | collective-permute-start | bytes 393224 | tf_op jit(solution)/shard_map/ppermute | solution.py:183
  96.6 7.6 %collective-permute-start.24 = (f32[1,64,512]{2,1,0:T(8,128)S(1)}, f32[1,64,512]{2,1,0:T(8,128)S(1)}, u32[]{:S(2)}, u32[]{:S(2)}) collective-permute-start(f32[1,64,512]{2,1,0:T(8,128)S(1)} %shard_map.49.refs_13_), channel_id=1, source_target_pairs={{2,0},{6,4},{10,8},{14,12},{18,16},{22,20},{26,24},{30,28}} | collective-permute-start | bytes 393224 | tf_op jit(solution)/shard_map/ppermute | solution.py:183
  97.9 7.0 %collective-permute-start.25 = (f32[1,64,512]{2,1,0:T(8,128)S(1)}, f32[1,64,512]{2,1,0:T(8,128)S(1)}, u32[]{:S(2)}, u32[]{:S(2)}) collective-permute-start(f32[1,64,512]{2,1,0:T(8,128)S(1)} %shard_map.49.refs_13_), channel_id=1, source_target_pairs={{3,0},{7,4},{11,8},{15,12},{19,16},{23,20},{27,24},{31,28}} | collective-permute-start | bytes 393224 | tf_op jit(solution)/shard_map/ppermute | solution.py:183
  (21 other events, 241.0 us)

commit v3 on v2

--- a/solution.py
+++ b/solution.py
@@ -68,9 +68,14 @@
             out[:, t * width:(t + 2) * width] = jnp.concatenate(pair, 1)
 
 
-def plane_kernel(count, skip, half_ref, rows_ref, cols_ref, *refs):
+def plane_kernel(count, skip, copies, half_ref, rows_ref, cols_ref, *refs):
     here, other, refs = refs[:PLANE], refs[PLANE:PLANE + count], refs[PLANE + count:]
-    (cos_ref, sin_ref), outs, (mod, rhs, acc) = refs[:2], refs[2:-3], refs[-3:]
+    (cos_ref, sin_ref), (mod, rhs, acc) = refs[:2], refs[-3:]
+    n = PLANE * (count or PLANE) // 2 + copies
+    outs = refs[-3 - n:-3]
+    for k in range(copies):
+        outs[n - copies + k][...] = refs[2 + k][...]
+    outs = outs[:n - copies]
     if not count:
         other = here
     each = len(outs) // PLANE
@@ -89,7 +94,8 @@
 
 
 def last_kernel(half_ref, rows_ref, cols_ref, *refs):
-    here, (other, cos_ref, sin_ref, out, mod, rhs, acc) = refs[:PLANE], refs[PLANE:]
+    here, (other, cos_ref, sin_ref) = refs[:PLANE], refs[PLANE:PLANE + 3]
+    out, mod, rhs, acc = refs[-4:]
     gather_columns(rhs, [other], cols_ref)
     for m in range(PLANE):
         @pl.when(rows_ref[m] == 0)
@@ -98,16 +104,17 @@
     product(acc, mod.at[0], rhs, [out], here[0].shape[1])
 
 
-def products(here, other, half, rows, cols, tables, skip=None, last=False):
+def products(here, other, half, rows, cols, tables, skip=None, last=False, copy=(), before=()):
     count = len(other)
     _, width, bins = here[0].shape
     columns = (count or PLANE) * width
-    body = last_kernel if last else functools.partial(plane_kernel, count, skip)
+    body = last_kernel if last else functools.partial(plane_kernel, count, skip, len(copy))
     shape = (1 if last else 2, width, LAGS * width)
     outs = [jax.ShapeDtypeStruct(shape, jnp.float32)]
     if not last:
         outs = outs * (PLANE * (count or PLANE) // 2)
-    arrays = [*here, *other, *tables]
+    outs += [jax.ShapeDtypeStruct(x.shape, x.dtype) for x in copy]
+    arrays = [*here, *other, *tables, *copy]
 
     def whole(x):
         zeros = (0,) * len(x.shape)
@@ -119,7 +126,8 @@
         grid_spec=pltpu.PrefetchScalarGridSpec(
             num_scalar_prefetch=3,
             grid=(1,),
-            in_specs=[whole(x) for x in arrays],
+            in_specs=[whole(x) for x in arrays]
+            + [pl.BlockSpec(memory_space=pl.ANY)] * len(before),
             out_specs=[whole(x) for x in outs],
             scratch_shapes=[
                 pltpu.VMEM((1 if last else 2, LAGS * width, 2 * bins), jnp.bfloat16),
@@ -129,7 +137,7 @@
         ),
         compiler_params=pltpu.CompilerParams(vmem_limit_bytes=LIMIT),
         cost_estimate=pl.CostEstimate(flops=1024, bytes_accessed=1024, transcendentals=0),
-    )(half, rows, cols, *arrays)
+    )(half, rows, cols, *arrays, *before)
 
 
 def final_kernel(norm, q_ref, flags_ref, *refs):
@@ -212,7 +220,7 @@
     slots = ints(*[q ^ k for k in range(PLANE)])
 
     mine = piece(own, 0)
-    (rest,) = after([own], mine)
+    rest = own
     near0 = move(mine, up)
     sib, cross, diag = [move(piece(rest, k), to_plane(k)) for k in range(1, PLANE)]
     near1 = move(sib, up)
@@ -236,16 +244,17 @@
     last = move(last_send, up)
 
     near_core = in_core(
-        products(here, after(near, same_core[2], last_send), half, slots, slots, tables)
+        products(here, near, half, slots, slots, tables, before=[same_sum[-1], last_send])
     )
     near_sum = across(near_core)
     far_core = in_core(products(
-        here, after(far, near_core[2], same_sum[2]), half, slots, ints(c, 1 - c), tables,
-        skip=PLANE - 1,
+        here, far, half, slots, ints(c, 1 - c), tables,
+        skip=PLANE - 1, before=[near_core[2]],
     ))
     far_sum = across(far_core)
     (last_part,) = products(
-        here, after([last], far_core[2]), half, slots, ints(0), tables, last=True
+        here, [last], half, slots, ints(0), tables, last=True,
+        before=[far_core[2], near_sum[-1]],
     )
     last_sum = [last_part] + [move(last_part, to_plane(k), k) for k in (1, 2, 3)]
 

time: 108 us -> 105 us (0.972)
  local copies, waits for them, and re-layouts: 7.2 us -> 2.62 us
  waiting for transfers between devices: 54.3 us -> 58.3 us
  starting transfers between devices: 16.1 us -> 13.9 us
    ppermute x26, waiting for transfers between devices: 54.3 us -> 58.3 us  [move(): return lax.ppermute(value, 'chan', pairs)]
    unnamed x38 -> x40, local copies, waits for them, and re-layouts: 3.77 us -> 0.09 us
    ppermute x26, starting transfers between devices: 16.1 us -> 13.9 us  [move(): return lax.ppermute(value, 'chan', pairs)]
    concatenate x2, other arithmetic: 1.7 us -> 0.07 us  [in_core(): return (rows[0], got[0], jnp.concatenate(passed, 0))]
    squeeze x2 -> x1, local copies, waits for them, and re-layouts: 3.43 us -> 2.53 us  [piece(): lax.dynamic_slice(block, (s, 0, 0, h * half_bins), (1, 2, width, half_bins))]
  transfers between devices with their start and end apart: 26 -> 26, of which waited for: 13 -> 15; matrix products, arithmetic and copies ran while one was open for 4% -> 4% of each run, Pallas kernels for 21% -> 23%
where the time goes in v3:
time: 105 us
  waiting for transfers between devices  58.3 us (56%)
  Pallas kernels  25.5 us (24%)
  starting transfers between devices  13.9 us (13%)
  other arithmetic  4.1 us (4%)
  local copies, waits for them, and re-layouts  2.62 us (2%)
    ppermute x26, waiting for transfers between devices, move(): return lax.ppermute(value, 'chan', pairs)  58.3 us
    pallas_call x4, Pallas kernels, products(): pl.pallas_call(body, out_shape=outs, grid_spec=pltpu.PrefetchScalarGridSp...  23.7 us
    ppermute x26, starting transfers between devices, move(): return lax.ppermute(value, 'chan', pairs)  13.9 us
    squeeze x1, local copies, waits for them, and re-layouts, piece(): lax.dynamic_slice(block, (s, 0, 0, h * half_bins), (1, 2, width, half_bins))  2.53 us
  transfers between devices with their start and end apart: 26, of which 15 were waited for; matrix products, arithmetic and copies ran while one was open for 4% of the time, Pallas kernels for 23%

profile of v3, /device:TPU:0, one launch (start us, length us, event | category | flops | bytes accessed | tf_op | source)
XLA Modules:
  0.0 104.7 jit_solution(1778646899704712741)
XLA Ops:
  0.0 2.5 %dynamic-slice_bitcast_fusion = (bf16[2,64,2048]{2,1,0:T(8,128)(2,1)}, bf16[2,64,2048]{2,1,0:T(8,128)(2,1)S(1)}, bf16[2,64,2048]{2,1,0:T(8,128)(2,1)S(1)}, bf16[2,64,2048]{2,1,0:T(8,128)(2,1)S(1)}) fusion(bf16[1,2,2,64,4096]{4,3,2,1,0:T(8,128)(2,1)} %param.4, s32[]{:T(128)S(6)} %select_n.52, s32[]{:T(128)S(6)} %select_n.51, s32[]{:T(128)S(6)} %select_n.49, ...), kind=kLoop, calls=%fused_computation.3 | loop fusion | bytes 4194320 | tf_op jit(solution)/shard_map/squeeze | solution.py:205
  3.0 2.5 %collective-permute-start.1 = (bf16[2,64,2048]{2,1,0:T(8,128)(2,1)S(1)}, bf16[2,64,2048]{2,1,0:T(8,128)(2,1)S(1)}, u32[]{:S(2)}, u32[]{:S(2)}) collective-permute-start(bf16[2,64,2048]{2,1,0:T(8,128)(2,1)S(1)} %get-tuple-element.60), channel_id=1, source_target_pairs={{0,2},{1,3},{2,0},{3,1},{4,6},{5,7},{6,4},{7,5},{8,10},{9,11},{10,... | collective-permute-start | bytes 1572872 | tf_op jit(solution)/shard_map/ppermute | solution.py:191
  5.5 1.6 %collective-permute-start.2 = (bf16[2,64,2048]{2,1,0:T(8,128)(2,1)S(1)}, bf16[2,64,2048]{2,1,0:T(8,128)(2,1)S(1)}, u32[]{:S(2)}, u32[]{:S(2)}) collective-permute-start(bf16[2,64,2048]{2,1,0:T(8,128)(2,1)S(1)} %get-tuple-element.59.refs_0_), channel_id=1, source_target_pairs={{0,4},{1,5},{2,6},{3,7},{4,8},{5,9},{6,10},{7,11},{8,12},{9,13},{1... | collective-permute-start | bytes 1572872 | tf_op jit(solution)/shard_map/ppermute | solution.py:191
  7.1 1.6 %collective-permute-start.4 = (bf16[2,64,2048]{2,1,0:T(8,128)(2,1)S(1)}, bf16[2,64,2048]{2,1,0:T(8,128)(2,1)S(1)}, u32[]{:S(2)}, u32[]{:S(2)}) collective-permute-start(bf16[2,64,2048]{2,1,0:T(8,128)(2,1)S(1)} %collective-permute-done.refs_1_), channel_id=1, source_target_pairs={{0,4},{1,5},{2,6},{3,7},{4,8},{5,9},{6,10},{7,11},{8,12},{9,13},{1... | collective-permute-start | bytes 1572872 | tf_op jit(solution)/shard_map/ppermute | solution.py:191
  8.7 9.6 %collective-permute-done.1.refs_2_ = bf16[2,64,2048]{2,1,0:T(8,128)(2,1)S(1)} collective-permute-done((bf16[2,64,2048]{2,1,0:T(8,128)(2,1)S(1)}, bf16[2,64,2048]{2,1,0:T(8,128)(2,1)S(1)}, u32[]{:S(2)}, u32[]{:S(2)}) %collective-permute-start.1) | collective-permute-done | bytes 524320 | tf_op jit(solution)/shard_map/ppermute | solution.py:191
  18.3 3.8 %collective-permute-done.2.refs_4_ = bf16[2,64,2048]{2,1,0:T(8,128)(2,1)S(1)} collective-permute-done((bf16[2,64,2048]{2,1,0:T(8,128)(2,1)S(1)}, bf16[2,64,2048]{2,1,0:T(8,128)(2,1)S(1)}, u32[]{:S(2)}, u32[]{:S(2)}) %collective-permute-start.2) | collective-permute-done | bytes 524320 | tf_op jit(solution)/shard_map/ppermute | solution.py:191
  22.1 7.0 %collective-permute-done.3.refs_3_ = bf16[2,64,2048]{2,1,0:T(8,128)(2,1)S(1)} collective-permute-done((bf16[2,64,2048]{2,1,0:T(8,128)(2,1)}, bf16[2,64,2048]{2,1,0:T(8,128)(2,1)S(1)}, u32[]{:S(2)}, u32[]{:S(2)}) %collective-permute-start.3) | collective-permute-done | bytes 524320 | tf_op jit(solution)/shard_map/ppermute | solution.py:191
  29.1 4.1 %collective-permute-done.4.refs_5_ = bf16[2,64,2048]{2,1,0:T(8,128)(2,1)S(1)} collective-permute-done((bf16[2,64,2048]{2,1,0:T(8,128)(2,1)S(1)}, bf16[2,64,2048]{2,1,0:T(8,128)(2,1)S(1)}, u32[]{:S(2)}, u32[]{:S(2)}) %collective-permute-start.4) | collective-permute-done | bytes 524320 | tf_op jit(solution)/shard_map/ppermute | solution.py:191
  33.3 6.1 %shard_map.46 = (f32[2,64,512]{2,1,0:T(8,128)S(1)}, f32[2,64,512]{2,1,0:T(8,128)S(1)}, f32[2,64,512]{2,1,0:T(8,128)S(1)}, f32[2,64,512]{2,1,0:T(8,128)S(1)}, f32...) custom-call(s32[1]{0:T(128)} %bitcast.2.half_ref, ...), custom_call_target="tpu_custom_call" | custom-call | flops 1024 | bytes 1024 | tf_op jit(solution)/shard_map/pallas_call | solution.py:123
  40.0 4.6 %collective-permute-done.10.refs_6_ = bf16[2,64,2048]{2,1,0:T(8,128)(2,1)} collective-permute-done((bf16[2,64,2048]{2,1,0:T(8,128)(2,1)S(1)}, bf16[2,64,2048]{2,1,0:T(8,128)(2,1)}, u32[]{:S(2)}, u32[]{:S(2)}) %collective-permute-start.10) | collective-permute-done | bytes 524320 | tf_op jit(solution)/shard_map/ppermute | solution.py:191
  44.6 1.9 %broadcast_select_fusion = bf16[2,64,2048]{2,1,0:T(8,128)(2,1)} fusion(bf16[2,64,2048]{2,1,0:T(8,128)(2,1)} %collective-permute-done.10.refs_6_, bf16[2,64,2048]{2,1,0:T(8,128)(2,1)S(1)} %collective-permute-done.2.refs_4_, pred[]{:T(512)S(6)} %eq.6), kind=kLoop, calls=%fused_computation.7 | loop fusion | flops 262144 | bytes 1572865 | tf_op jit(solution)/shard_map/jit(_where)/select_n | solution.py:239
  46.8 8.9 %collective-permute-done.11.refs_7_ = bf16[2,64,2048]{2,1,0:T(8,128)(2,1)S(1)} collective-permute-done((bf16[2,64,2048]{2,1,0:T(8,128)(2,1)S(1)}, bf16[2,64,2048]{2,1,0:T(8,128)(2,1)S(1)}, u32[]{:S(2)}, u32[]{:S(2)}) %collective-permute-start.11) | collective-permute-done | bytes 524320 | tf_op jit(solution)/shard_map/ppermute | solution.py:191
  57.5 2.0 %collective-permute-done.9.refs_10_.refs_4_ = f32[4,64,512]{2,1,0:T(8,128)S(1)} collective-permute-done((f32[4,64,512]{2,1,0:T(8,128)S(1)}, f32[4,64,512]{2,1,0:T(8,128)S(1)}, u32[]{:S(2)}, u32[]{:S(2)}) %collective-permute-start.9) | collective-permute-done | bytes 524320 | tf_op jit(solution)/shard_map/ppermute | solution.py:191
  59.5 7.2 %shard_map.47 = (f32[2,64,512]{2,1,0:T(8,128)S(1)}, f32[2,64,512]{2,1,0:T(8,128)S(1)}, f32[2,64,512]{2,1,0:T(8,128)S(1)}, f32[2,64,512]{2,1,0:T(8,128)S(1)}, f32...) custom-call(s32[1]{0:T(128)} %bitcast.2.half_ref, ...), custom_call_target="tpu_custom_call" | custom-call | flops 1024 | bytes 1024 | tf_op jit(solution)/shard_map/pallas_call | solution.py:123
  67.3 0.9 collective-permute-start.22
  69.3 9.1 %collective-permute-done.18.refs_5_ = bf16[2,64,2048]{2,1,0:T(8,128)(2,1)} collective-permute-done((bf16[2,64,2048]{2,1,0:T(8,128)(2,1)}, bf16[2,64,2048]{2,1,0:T(8,128)(2,1)}, u32[]{:S(2)}, u32[]{:S(2)}) %collective-permute-start.18) | collective-permute-done | bytes 524320 | tf_op jit(solution)/shard_map/ppermute | solution.py:191
  78.3 6.5 %shard_map.48 = (f32[2,64,512]{2,1,0:T(8,128)S(1)}, f32[2,64,512]{2,1,0:T(8,128)S(1)}, f32[2,64,512]{2,1,0:T(8,128)S(1)}, f32[2,64,512]{2,1,0:T(8,128)S(1)}) custom-call(s32[1]{0:T(128)} %bitcast.2.half_ref, s32[4]{0:T(128)S(1)} %pad_add_fusion.rows_ref.cols_ref, s32[2]{0:T(128)S(1)} %pad_add_fusion.1.cols_ref, ...), custom_call_target="tpu_custom_call" | custom-call | flops 1024 | bytes 1024 | tf_op jit(solution)/shard_map/pallas_call | solution.py:123
  86.7 2.2 %collective-permute-done.22.refs_4_ = bf16[2,64,2048]{2,1,0:T(8,128)(2,1)} collective-permute-done((bf16[2,64,2048]{2,1,0:T(8,128)(2,1)}, bf16[2,64,2048]{2,1,0:T(8,128)(2,1)}, u32[]{:S(2)}, u32[]{:S(2)}) %collective-permute-start.22) | collective-permute-done | bytes 524320 | tf_op jit(solution)/shard_map/ppermute | solution.py:191
  89.5 3.9 %shard_map.49.refs_13_ = f32[1,64,512]{2,1,0:T(8,128)S(1)} custom-call(s32[1]{0:T(128)} %bitcast.2.half_ref, s32[4]{0:T(128)S(1)} %pad_add_fusion.rows_ref.cols_ref, s32[1]{0:T(128)} %constant.47.clone.1.cols_ref, bf16[2,64,2048]{2,1,0:T(8,128)(2,1)S(1)} %get-tuple-element.59.refs_0_, bf16[2,64,2048]{2,1,0:T(8,128)(2,1)S(1)} %collective-permute-done.refs_1_, ...), custom_call_target="tpu_custom_call" | custom-call | flops 1024 | bytes 1024 | tf_op jit(solution)/shard_map/pallas_call | solution.py:123
  93.4 1.3 %collective-permute-start.23 = (f32[1,64,512]{2,1,0:T(8,128)S(1)}, f32[1,64,512]{2,1,0:T(8,128)S(1)}, u32[]{:S(2)}, u32[]{:S(2)}) collective-permute-start(f32[1,64,512]{2,1,0:T(8,128)S(1)} %shard_map.49.refs_13_), channel_id=1, source_target_pairs={{1,0},{5,4},{9,8},{13,12},{17,16},{21,20},{25,24},{29,28}} | collective-permute-start | bytes 393224 | tf_op jit(solution)/shard_map/ppermute | solution.py:191
  94.7 1.3 %collective-permute-start.24 = (f32[1,64,512]{2,1,0:T(8,128)S(1)}, f32[1,64,512]{2,1,0:T(8,128)S(1)}, u32[]{:S(2)}, u32[]{:S(2)}) collective-permute-start(f32[1,64,512]{2,1,0:T(8,128)S(1)} %shard_map.49.refs_13_), channel_id=1, source_target_pairs={{2,0},{6,4},{10,8},{14,12},{18,16},{22,20},{26,24},{30,28}} | collective-permute-start | bytes 393224 | tf_op jit(solution)/shard_map/ppermute | solution.py:191
  96.0 1.3 %collective-permute-start.25 = (f32[1,64,512]{2,1,0:T(8,128)S(1)}, f32[1,64,512]{2,1,0:T(8,128)S(1)}, u32[]{:S(2)}, u32[]{:S(2)}) collective-permute-start(f32[1,64,512]{2,1,0:T(8,128)S(1)} %shard_map.49.refs_13_), channel_id=1, source_target_pairs={{3,0},{7,4},{11,8},{15,12},{19,16},{23,20},{27,24},{31,28}} | collective-permute-start | bytes 393224 | tf_op jit(solution)/shard_map/ppermute | solution.py:191
  97.7 4.6 %collective-permute-done.24.refs_15_ = f32[1,64,512]{2,1,0:T(8,128)S(1)} collective-permute-done((f32[1,64,512]{2,1,0:T(8,128)S(1)}, f32[1,64,512]{2,1,0:T(8,128)S(1)}, u32[]{:S(2)}, u32[]{:S(2)}) %collective-permute-start.24) | collective-permute-done | bytes 131104 | tf_op jit(solution)/shard_map/ppermute | solution.py:191
  103.0 1.8 %shard_map.50 = f32[1,8,64,512]{3,2,1,0:T(8,128)} custom-call(s32[1]{0:T(128)} %bitcast.q_ref, s32[8]{0:T(128)S(1)} %bitcast.15, f32[2,64,512]{2,1,0:T(8,128)S(1)} %copy-done.5, f32[2,64,512]{2,1,0:T(8,128)S(1)} %copy-done.7, f32[2,64,512]{2,1,0:T(8,128)S(1)} %collective-permute-done.5.refs_2_, f32[2,64,512]{2,1,0:T(8,128)S(1)} %collective-permute-done.6.refs_3_, ...), custom_call_target="tpu_custom_call" | custom-call | tf_op jit(solution)/shard_map/pallas_call | solution.py:261
  (86 shorter events, 8.1 us)
Async XLA Ops:
  2.5 4.6 %collective-permute-start = (bf16[2,64,2048]{2,1,0:T(8,128)(2,1)S(1)}, bf16[2,64,2048]{2,1,0:T(8,128)(2,1)S(1)}, u32[]{:S(2)}, u32[]{:S(2)}) collective-permute-start(bf16[2,64,2048]{2,1,0:T(8,128)(2,1)S(1)} %get-tuple-element.58), channel_id=1, source_target_pairs={{0,1},{1,0},{2,3},{3,2},{4,5},{5,4},{6,7},{7,6},{8,9},{9,8},{10,11... | collective-permute-start | bytes 1572872 | tf_op jit(solution)/shard_map/ppermute | solution.py:191
  3.0 15.3 %collective-permute-start.1 = (bf16[2,64,2048]{2,1,0:T(8,128)(2,1)S(1)}, bf16[2,64,2048]{2,1,0:T(8,128)(2,1)S(1)}, u32[]{:S(2)}, u32[]{:S(2)}) collective-permute-start(bf16[2,64,2048]{2,1,0:T(8,128)(2,1)S(1)} %get-tuple-element.60), channel_id=1, source_target_pairs={{0,2},{1,3},{2,0},{3,1},{4,6},{5,7},{6,4},{7,5},{8,10},{9,11},{10,... | collective-permute-start | bytes 1572872 | tf_op jit(solution)/shard_map/ppermute | solution.py:191
  5.5 16.5 %collective-permute-start.2 = (bf16[2,64,2048]{2,1,0:T(8,128)(2,1)S(1)}, bf16[2,64,2048]{2,1,0:T(8,128)(2,1)S(1)}, u32[]{:S(2)}, u32[]{:S(2)}) collective-permute-start(bf16[2,64,2048]{2,1,0:T(8,128)(2,1)S(1)} %get-tuple-element.59.refs_0_), channel_id=1, source_target_pairs={{0,4},{1,5},{2,6},{3,7},{4,8},{5,9},{6,10},{7,11},{8,12},{9,13},{1... | collective-permute-start | bytes 1572872 | tf_op jit(solution)/shard_map/ppermute | solution.py:191
  7.1 22.1 %collective-permute-start.3 = (bf16[2,64,2048]{2,1,0:T(8,128)(2,1)}, bf16[2,64,2048]{2,1,0:T(8,128)(2,1)S(1)}, u32[]{:S(2)}, u32[]{:S(2)}) collective-permute-start(bf16[2,64,2048]{2,1,0:T(8,128)(2,1)} %get-tuple-element.57), channel_id=1, source_target_pairs={{0,3},{1,2},{2,1},{3,0},{4,7},{5,6},{6,5},{7,4},{8,11},{9,10},{10,... | collective-permute-start | bytes 1572872 | tf_op jit(solution)/shard_map/ppermute | solution.py:191
  7.1 26.1 %collective-permute-start.4 = (bf16[2,64,2048]{2,1,0:T(8,128)(2,1)S(1)}, bf16[2,64,2048]{2,1,0:T(8,128)(2,1)S(1)}, u32[]{:S(2)}, u32[]{:S(2)}) collective-permute-start(bf16[2,64,2048]{2,1,0:T(8,128)(2,1)S(1)} %collective-permute-done.refs_1_), channel_id=1, source_target_pairs={{0,4},{1,5},{2,6},{3,7},{4,8},{5,9},{6,10},{7,11},{8,12},{9,13},{1... | collective-permute-start | bytes 1572872 | tf_op jit(solution)/shard_map/ppermute | solution.py:191
  22.1 22.6 %collective-permute-start.10 = (bf16[2,64,2048]{2,1,0:T(8,128)(2,1)S(1)}, bf16[2,64,2048]{2,1,0:T(8,128)(2,1)}, u32[]{:S(2)}, u32[]{:S(2)}) collective-permute-start(bf16[2,64,2048]{2,1,0:T(8,128)(2,1)S(1)} %collective-permute-done.1.refs_2_), channel_id=1, source_target_pairs={{0,4},{1,5},{2,6},{3,7},{4,8},{5,9},{6,10},{7,11},{8,12},{9,13},{1... | collective-permute-start | bytes 1572872 | tf_op jit(solution)/shard_map/ppermute | solution.py:191
  33.3 22.5 %collective-permute-start.11 = (bf16[2,64,2048]{2,1,0:T(8,128)(2,1)S(1)}, bf16[2,64,2048]{2,1,0:T(8,128)(2,1)S(1)}, u32[]{:S(2)}, u32[]{:S(2)}) collective-permute-start(bf16[2,64,2048]{2,1,0:T(8,128)(2,1)S(1)} %collective-permute-done.3.refs_3_), channel_id=1, source_target_pairs={{0,4},{1,5},{2,6},{3,7},{4,8},{5,9},{6,10},{7,11},{8,12},{9,13},{1... | collective-permute-start | bytes 1572872 | tf_op jit(solution)/shard_map/ppermute | solution.py:191
  39.5 7.1 %collective-permute-start.8 = (f32[2,64,512]{2,1,0:T(8,128)S(1)}, f32[2,64,512]{2,1,0:T(8,128)S(1)}, u32[]{:S(2)}, u32[]{:S(2)}) collective-permute-start(f32[2,64,512]{2,1,0:T(8,128)S(1)} %get-tuple-element.40), channel_id=1, source_target_pairs={{0,1},{1,0},{2,3},{3,2},{4,5},{5,4},{6,7},{7,6},{8,9},{9,8},{10,11... | collective-permute-start | bytes 786440 | tf_op jit(solution)/shard_map/ppermute | solution.py:191
  39.6 7.1 %collective-permute-start.7 = (f32[2,64,512]{2,1,0:T(8,128)S(1)}, f32[2,64,512]{2,1,0:T(8,128)S(1)}, u32[]{:S(2)}, u32[]{:S(2)}) collective-permute-start(f32[2,64,512]{2,1,0:T(8,128)S(1)} %get-tuple-element.38), channel_id=1, source_target_pairs={{0,1},{1,0},{2,3},{3,2},{4,5},{5,4},{6,7},{7,6},{8,9},{9,8},{10,11... | collective-permute-start | bytes 786440 | tf_op jit(solution)/shard_map/ppermute | solution.py:191
  46.6 22.7 %collective-permute-start.17 = (bf16[2,64,2048]{2,1,0:T(8,128)(2,1)}, bf16[2,64,2048]{2,1,0:T(8,128)(2,1)}, u32[]{:S(2)}, u32[]{:S(2)}) collective-permute-start(bf16[2,64,2048]{2,1,0:T(8,128)(2,1)} %broadcast_select_fusion), channel_id=1, source_target_pairs={{0,4},{1,5},{2,6},{3,7},{4,8},{5,9},{6,10},{7,11},{8,12},{9,13},{1... | collective-permute-start | bytes 1572872 | tf_op jit(solution)/shard_map/ppermute | solution.py:191
  46.7 12.7 %collective-permute-start.9 = (f32[4,64,512]{2,1,0:T(8,128)S(1)}, f32[4,64,512]{2,1,0:T(8,128)S(1)}, u32[]{:S(2)}, u32[]{:S(2)}) collective-permute-start(f32[4,64,512]{2,1,0:T(8,128)S(1)} %pad_maximum_fusion), channel_id=1, source_target_pairs={{0,2},{1,3},{2,0},{3,1},{4,6},{5,7},{6,4},{7,5},{8,10},{9,11},{10,... | collective-permute-start | bytes 1572872 | tf_op jit(solution)/shard_map/ppermute | solution.py:191
  56.6 21.7 %collective-permute-start.18 = (bf16[2,64,2048]{2,1,0:T(8,128)(2,1)}, bf16[2,64,2048]{2,1,0:T(8,128)(2,1)}, u32[]{:S(2)}, u32[]{:S(2)}) collective-permute-start(bf16[2,64,2048]{2,1,0:T(8,128)(2,1)} %broadcast_select_fusion.1), channel_id=1, source_target_pairs={{0,4},{1,5},{2,6},{3,7},{4,8},{5,9},{6,10},{7,11},{8,12},{9,13},{1... | collective-permute-start | bytes 1572872 | tf_op jit(solution)/shard_map/ppermute | solution.py:191
  66.8 1.9 %collective-permute-start.14 = (f32[2,64,512]{2,1,0:T(8,128)S(1)}, f32[2,64,512]{2,1,0:T(8,128)S(1)}, u32[]{:S(2)}, u32[]{:S(2)}) collective-permute-start(f32[2,64,512]{2,1,0:T(8,128)S(1)} %get-tuple-element.50), channel_id=1, source_target_pairs={{0,1},{1,0},{2,3},{3,2},{4,5},{5,4},{6,7},{7,6},{8,9},{9,8},{10,11... | collective-permute-start | bytes 786440 | tf_op jit(solution)/shard_map/ppermute | solution.py:191
  67.3 21.7 %collective-permute-start.22 = (bf16[2,64,2048]{2,1,0:T(8,128)(2,1)}, bf16[2,64,2048]{2,1,0:T(8,128)(2,1)}, u32[]{:S(2)}, u32[]{:S(2)}) collective-permute-start(bf16[2,64,2048]{2,1,0:T(8,128)(2,1)} %select_select_fusion.refs_11_), channel_id=1, source_target_pairs={{0,4},{1,5},{2,6},{3,7},{4,8},{5,9},{6,10},{7,11},{8,12},{9,13},{1... | collective-permute-start | bytes 1572872 | tf_op jit(solution)/shard_map/ppermute | solution.py:191
  68.8 20.1 %collective-permute-start.16 = (f32[4,64,512]{2,1,0:T(8,128)S(1)}, f32[4,64,512]{2,1,0:T(8,128)S(1)}, u32[]{:S(2)}, u32[]{:S(2)}) collective-permute-start(f32[4,64,512]{2,1,0:T(8,128)S(1)} %pad_maximum_fusion.1.refs_8_), channel_id=1, source_target_pairs={{0,2},{1,3},{2,0},{3,1},{4,6},{5,7},{6,4},{7,5},{8,10},{9,11},{10,... | collective-permute-start | bytes 1572872 | tf_op jit(solution)/shard_map/ppermute | solution.py:191
  69.2 16.2 %collective-permute-start.5 = (f32[2,64,512]{2,1,0:T(8,128)}, f32[2,64,512]{2,1,0:T(8,128)S(1)}, u32[]{:S(2)}, u32[]{:S(2)}) collective-permute-start(f32[2,64,512]{2,1,0:T(8,128)} %copy-done.15), channel_id=1, source_target_pairs={{0,1},{1,0},{2,3},{3,2},{4,5},{5,4},{6,7},{7,6},{8,9},{9,8},{10,11... | collective-permute-start | bytes 786440 | tf_op jit(solution)/shard_map/ppermute | solution.py:191
  84.9 8.4 %collective-permute-start.6 = (f32[2,64,512]{2,1,0:T(8,128)S(1)}, f32[2,64,512]{2,1,0:T(8,128)S(1)}, u32[]{:S(2)}, u32[]{:S(2)}) collective-permute-start(f32[2,64,512]{2,1,0:T(8,128)S(1)} %copy-done.14), channel_id=1, source_target_pairs={{0,1},{1,0},{2,3},{3,2},{4,5},{5,4},{6,7},{7,6},{8,9},{9,8},{10,11... | collective-permute-start | bytes 786440 | tf_op jit(solution)/shard_map/ppermute | solution.py:191
  85.4 9.2 %collective-permute-start.12 = (f32[2,64,512]{2,1,0:T(8,128)S(1)}, f32[2,64,512]{2,1,0:T(8,128)S(1)}, u32[]{:S(2)}, u32[]{:S(2)}) collective-permute-start(f32[2,64,512]{2,1,0:T(8,128)S(1)} %copy-done.19), channel_id=1, source_target_pairs={{0,1},{1,0},{2,3},{3,2},{4,5},{5,4},{6,7},{7,6},{8,9},{9,8},{10,11... | collective-permute-start | bytes 786440 | tf_op jit(solution)/shard_map/ppermute | solution.py:191
  86.5 9.5 %collective-permute-start.13 = (f32[2,64,512]{2,1,0:T(8,128)S(1)}, f32[2,64,512]{2,1,0:T(8,128)S(1)}, u32[]{:S(2)}, u32[]{:S(2)}) collective-permute-start(f32[2,64,512]{2,1,0:T(8,128)S(1)} %copy-done.17), channel_id=1, source_target_pairs={{0,1},{1,0},{2,3},{3,2},{4,5},{5,4},{6,7},{7,6},{8,9},{9,8},{10,11... | collective-permute-start | bytes 786440 | tf_op jit(solution)/shard_map/ppermute | solution.py:191
  88.9 8.3 %collective-permute-start.19 = (f32[2,64,512]{2,1,0:T(8,128)S(1)}, f32[2,64,512]{2,1,0:T(8,128)S(1)}, u32[]{:S(2)}, u32[]{:S(2)}) collective-permute-start(f32[2,64,512]{2,1,0:T(8,128)S(1)} %get-tuple-element.54), channel_id=1, source_target_pairs={{0,1},{1,0},{2,3},{3,2},{4,5},{5,4},{6,7},{7,6},{8,9},{9,8},{10,11... | collective-permute-start | bytes 786440 | tf_op jit(solution)/shard_map/ppermute | solution.py:191
  88.9 8.7 %collective-permute-start.21 = (f32[2,64,512]{2,1,0:T(8,128)S(1)}, f32[2,64,512]{2,1,0:T(8,128)S(1)}, u32[]{:S(2)}, u32[]{:S(2)}) collective-permute-start(f32[2,64,512]{2,1,0:T(8,128)S(1)} %add.41.refs_7_), channel_id=1, source_target_pairs={{0,2},{1,3},{2,0},{3,1},{4,6},{5,7},{6,4},{7,5},{8,10},{9,11},{10,... | collective-permute-start | bytes 786440 | tf_op jit(solution)/shard_map/ppermute | solution.py:191
  93.4 4.3 %collective-permute-start.23 = (f32[1,64,512]{2,1,0:T(8,128)S(1)}, f32[1,64,512]{2,1,0:T(8,128)S(1)}, u32[]{:S(2)}, u32[]{:S(2)}) collective-permute-start(f32[1,64,512]{2,1,0:T(8,128)S(1)} %shard_map.49.refs_13_), channel_id=1, source_target_pairs={{1,0},{5,4},{9,8},{13,12},{17,16},{21,20},{25,24},{29,28}} | collective-permute-start | bytes 393224 | tf_op jit(solution)/shard_map/ppermute | solution.py:191
  94.7 7.6 %collective-permute-start.24 = (f32[1,64,512]{2,1,0:T(8,128)S(1)}, f32[1,64,512]{2,1,0:T(8,128)S(1)}, u32[]{:S(2)}, u32[]{:S(2)}) collective-permute-start(f32[1,64,512]{2,1,0:T(8,128)S(1)} %shard_map.49.refs_13_), channel_id=1, source_target_pairs={{2,0},{6,4},{10,8},{14,12},{18,16},{22,20},{26,24},{30,28}} | collective-permute-start | bytes 393224 | tf_op jit(solution)/shard_map/ppermute | solution.py:191
  96.0 7.0 %collective-permute-start.25 = (f32[1,64,512]{2,1,0:T(8,128)S(1)}, f32[1,64,512]{2,1,0:T(8,128)S(1)}, u32[]{:S(2)}, u32[]{:S(2)}) collective-permute-start(f32[1,64,512]{2,1,0:T(8,128)S(1)} %shard_map.49.refs_13_), channel_id=1, source_target_pairs={{3,0},{7,4},{11,8},{15,12},{19,16},{23,20},{27,24},{31,28}} | collective-permute-start | bytes 393224 | tf_op jit(solution)/shard_map/ppermute | solution.py:191
  (22 other events, 261.5 us)

commit v4 on v3

--- a/solution.py
+++ b/solution.py
@@ -61,6 +61,10 @@
     acc[...] = lax.dot_general(
         mod[...], rhs[...], (((1,), (1,)), ((), ())), preferred_element_type=jnp.float32
     )
+    emit(acc, outs, width)
+
+
+def emit(acc, outs, width):
     places = [out.at[j] for out in outs for j in range(out.shape[0])]
     for j, out in enumerate(places):
         for t in range(0, LAGS, 2):
@@ -68,14 +72,16 @@
             out[:, t * width:(t + 2) * width] = jnp.concatenate(pair, 1)
 
 
-def plane_kernel(count, skip, copies, half_ref, rows_ref, cols_ref, *refs):
+def plane_kernel(count, skip, lead, half_ref, rows_ref, cols_ref, *refs):
     here, other, refs = refs[:PLANE], refs[PLANE:PLANE + count], refs[PLANE + count:]
     (cos_ref, sin_ref), (mod, rhs, acc) = refs[:2], refs[-3:]
-    n = PLANE * (count or PLANE) // 2 + copies
+    n = PLANE * (count or PLANE) // 2 + lead
     outs = refs[-3 - n:-3]
-    for k in range(copies):
-        outs[n - copies + k][...] = refs[2 + k][...]
-    outs = outs[:n - copies]
+    if lead:
+        for m in range(PLANE):
+            @pl.when(rows_ref[m] == 0)
+            def _():
+                outs[-1][...] = here[m][...]
     if not count:
         other = here
     each = len(outs) // PLANE
@@ -93,28 +99,66 @@
             pl.when(rows_ref[m] != skip)(functools.partial(one, m))
 
 
-def last_kernel(half_ref, rows_ref, cols_ref, *refs):
-    here, (other, cos_ref, sin_ref) = refs[:PLANE], refs[PLANE:PLANE + 3]
+def last_kernel(half_ref, lead, other, cos_ref, sin_ref, *refs):
     out, mod, rhs, acc = refs[-4:]
-    gather_columns(rhs, [other], cols_ref)
-    for m in range(PLANE):
-        @pl.when(rows_ref[m] == 0)
-        def _():
-            modulate_into(mod.at[0], here[m], half_ref[0], cos_ref, sin_ref)
-    product(acc, mod.at[0], rhs, [out], here[0].shape[1])
-
-
-def products(here, other, half, rows, cols, tables, skip=None, last=False, copy=(), before=()):
+    _, width, tile = lead.shape
+    step = pl.program_id(0)
+    for c in range(2):
+        rhs[:, c * tile:(c + 1) * tile] = other[c]
+    modulate_into(mod, lead, 0, cos_ref, sin_ref)
+    part = lax.dot_general(
+        mod[...], rhs[...], (((1,), (1,)), ((), ())), preferred_element_type=jnp.float32
+    )
+
+    @pl.when(step == 0)
+    def _():
+        acc[...] = part
+
+    @pl.when(step > 0)
+    def _():
+        acc[...] += part
+
+    @pl.when(step == pl.num_programs(0) - 1)
+    def _():
+        emit(acc, [out], width)
+
+
+def last_product(lead, other, half, tables, before):
+    _, width, bins = lead.shape
+    steps = bins // TILE
+    tile = pl.BlockSpec((2, width, TILE), lambda f, half: (0, 0, f))
+    table = pl.BlockSpec((8, TILE), lambda f, half: (0, half[0] * steps + f))
+    shape = (1, width, LAGS * width)
+    return pl.pallas_call(
+        last_kernel,
+        out_shape=jax.ShapeDtypeStruct(shape, jnp.float32),
+        grid_spec=pltpu.PrefetchScalarGridSpec(
+            num_scalar_prefetch=1,
+            grid=(steps,),
+            in_specs=[tile, tile, table, table]
+            + [pl.BlockSpec(memory_space=pl.ANY)] * len(before),
+            out_specs=pl.BlockSpec(shape, lambda f, half: (0, 0, 0)),
+            scratch_shapes=[
+                pltpu.VMEM((LAGS * width, 2 * TILE), jnp.bfloat16),
+                pltpu.VMEM((width, 2 * TILE), jnp.bfloat16),
+                pltpu.VMEM((LAGS * width, width), jnp.float32),
+            ],
+        ),
+        compiler_params=pltpu.CompilerParams(vmem_limit_bytes=LIMIT),
+        cost_estimate=pl.CostEstimate(flops=1024, bytes_accessed=1024, transcendentals=0),
+    )(half, lead, other, *tables, *before)
+
+
+def products(here, other, half, rows, cols, tables, skip=None, lead=False, before=()):
     count = len(other)
     _, width, bins = here[0].shape
     columns = (count or PLANE) * width
-    body = last_kernel if last else functools.partial(plane_kernel, count, skip, len(copy))
-    shape = (1 if last else 2, width, LAGS * width)
-    outs = [jax.ShapeDtypeStruct(shape, jnp.float32)]
-    if not last:
-        outs = outs * (PLANE * (count or PLANE) // 2)
-    outs += [jax.ShapeDtypeStruct(x.shape, x.dtype) for x in copy]
-    arrays = [*here, *other, *tables, *copy]
+    body = functools.partial(plane_kernel, count, skip, lead)
+    shape = (2, width, LAGS * width)
+    outs = [jax.ShapeDtypeStruct(shape, jnp.float32)] * (PLANE * (count or PLANE) // 2)
+    if lead:
+        outs.append(jax.ShapeDtypeStruct(here[0].shape, here[0].dtype))
+    arrays = [*here, *other, *tables]
 
     def whole(x):
         zeros = (0,) * len(x.shape)
@@ -130,7 +174,7 @@
             + [pl.BlockSpec(memory_space=pl.ANY)] * len(before),
             out_specs=[whole(x) for x in outs],
             scratch_shapes=[
-                pltpu.VMEM((1 if last else 2, LAGS * width, 2 * bins), jnp.bfloat16),
+                pltpu.VMEM((2, LAGS * width, 2 * bins), jnp.bfloat16),
                 pltpu.VMEM((columns, 2 * bins), jnp.bfloat16),
                 pltpu.VMEM((LAGS * width, columns), jnp.float32),
             ],
@@ -138,6 +182,22 @@
         compiler_params=pltpu.CompilerParams(vmem_limit_bytes=LIMIT),
         cost_estimate=pl.CostEstimate(flops=1024, bytes_accessed=1024, transcendentals=0),
     )(half, rows, cols, *arrays, *before)
+
+
+def gate_kernel(given, *refs):
+    for n in range(given.shape[0]):
+        refs[-1][n] = given[n]
+
+
+def gate(scalars, others, weight):
+    return pl.pallas_call(
+        gate_kernel,
+        out_shape=jax.ShapeDtypeStruct(scalars.shape, jnp.int32),
+        in_specs=[pl.BlockSpec(memory_space=pltpu.SMEM)]
+        + [pl.BlockSpec(memory_space=pl.ANY)] * len(others),
+        out_specs=pl.BlockSpec(memory_space=pltpu.SMEM),
+        cost_estimate=pl.CostEstimate(flops=weight, bytes_accessed=1024, transcendentals=0),
+    )(scalars, *others)
 
 
 def final_kernel(norm, q_ref, flags_ref, *refs):
@@ -220,9 +280,8 @@
     slots = ints(*[q ^ k for k in range(PLANE)])
 
     mine = piece(own, 0)
-    rest = own
     near0 = move(mine, up)
-    sib, cross, diag = [move(piece(rest, k), to_plane(k)) for k in range(1, PLANE)]
+    sib, cross, diag = [move(piece(own, k), to_plane(k)) for k in range(1, PLANE)]
     near1 = move(sib, up)
     (cross,) = after([cross], near0)
     near2 = move(cross, up)
@@ -231,7 +290,8 @@
     here = [mine, sib, cross, diag]
     near = [near0, near1, near2, near3]
     half = ints(c)
-    same_core = in_core(products(here, [], half, slots, slots, tables))
+    *parts, lead = products(here, [], half, slots, slots, tables, lead=True, before=[])
+    same_core = in_core(parts)
     same_sum = across(same_core)
 
     odd = c == 1
@@ -244,18 +304,15 @@
     last = move(last_send, up)
 
     near_core = in_core(
-        products(here, near, half, slots, slots, tables, before=[same_sum[-1], last_send])
+        products(here, near, half, slots, gate(slots, [near0, near1, near2, near3], 9200000000), tables, before=[same_sum[-1], last_send])
     )
     near_sum = across(near_core)
     far_core = in_core(products(
         here, far, half, slots, ints(c, 1 - c), tables,
-        skip=PLANE - 1, before=[near_core[2]],
+        skip=PLANE - 1, before=[near_core[2], same_sum[-1]],
     ))
     far_sum = across(far_core)
-    (last_part,) = products(
-        here, [last], half, slots, ints(0), tables, last=True,
-        before=[far_core[2], near_sum[-1]],
-    )
+    last_part = last_product(lead, last, half, tables, [far_core[2], near_sum[-1]])
     last_sum = [last_part] + [move(last_part, to_plane(k), k) for k in (1, 2, 3)]
 
     return pl.pallas_call(

time: 105 us -> 102 us (0.971)
  waiting for transfers between devices: 58.3 us -> 52.8 us
  Pallas kernels: 25.5 us -> 26.9 us
    ppermute x26, waiting for transfers between devices: 58.3 us -> 52.8 us  [move(): return lax.ppermute(value, 'chan', pairs)]
    pallas_call x0 -> x2, Pallas kernels: none -> 3.43 us  [the longest x1 2.11 us: last_product(): pl.pallas_call(last_kernel, out_shape=jax.ShapeDtypeStruct(shape, jnp.flo...]
    pallas_call x4 -> x3, Pallas kernels: 23.7 us -> 21.7 us  [products(): pl.pallas_call(body, out_shape=outs, grid_spec=pltpu.PrefetchScalarGridSp...]
    select_n x1, other arithmetic: 0.9 us -> 2.04 us  [per_device(): last_send = jnp.where(low, jnp.where(odd, a, b), jnp.where(odd, d, e))]
    ppermute x26, starting transfers between devices: 13.9 us -> 14.9 us  [move(): return lax.ppermute(value, 'chan', pairs)]
  transfers between devices with their start and end apart: 26 -> 26, of which waited for: 15 -> 13; matrix products, arithmetic and copies ran while one was open for 4% -> 5% of each run, Pallas kernels for 23% -> 25%
where the time goes in v4:
time: 102 us
  waiting for transfers between devices  52.8 us (52%)
  Pallas kernels  26.9 us (26%)
  starting transfers between devices  14.9 us (15%)
  other arithmetic  5.12 us (5%)
  local copies, waits for them, and re-layouts  1.83 us (2%)
    ppermute x26, waiting for transfers between devices, move(): return lax.ppermute(value, 'chan', pairs)  52.8 us
    pallas_call x3, Pallas kernels, products(): pl.pallas_call(body, out_shape=outs, grid_spec=pltpu.PrefetchScalarGridSp...  21.7 us
    ppermute x26, starting transfers between devices, move(): return lax.ppermute(value, 'chan', pairs)  14.9 us
    pallas_call x1, Pallas kernels, last_product(): pl.pallas_call(last_kernel, out_shape=jax.ShapeDtypeStruct(shape, jnp.flo...  2.11 us
  transfers between devices with their start and end apart: 26, of which 13 were waited for; matrix products, arithmetic and copies ran while one was open for 5% of the time, Pallas kernels for 25%

profile of v4, /device:TPU:0, one launch (start us, length us, event | category | flops | bytes accessed | tf_op | source)
XLA Modules:
  0.0 102.1 jit_solution(11644395262518048356)
XLA Ops:
  0.0 1.7 %dynamic-slice_bitcast_fusion = (bf16[2,64,2048]{2,1,0:T(8,128)(2,1)S(1)}, bf16[2,64,2048]{2,1,0:T(8,128)(2,1)S(1)}, bf16[2,64,2048]{2,1,0:T(8,128)(2,1)S(1)}, bf16[2,64,2048]{2,1,0:T(8,128)(2,1)S(1)}) fusion(bf16[1,2,2,64,4096]{4,3,2,1,0:T(8,128)(2,1)} %param.4, s32[]{:T(128)S(6)} %select_n.52, s32[]{:T(128)S(6)} %select_n.51, s32[]{:T(128)S(6)} %select_n.49, ...), kind=kLoop, calls=%fused_computation.3 | loop fusion | bytes 4194320 | tf_op jit(solution)/shard_map/squeeze | solution.py:265
  2.2 2.6 %collective-permute-start.1 = (bf16[2,64,2048]{2,1,0:T(8,128)(2,1)S(1)}, bf16[2,64,2048]{2,1,0:T(8,128)(2,1)}, u32[]{:S(2)}, u32[]{:S(2)}) collective-permute-start(bf16[2,64,2048]{2,1,0:T(8,128)(2,1)S(1)} %get-tuple-element.62), channel_id=1, source_target_pairs={{0,2},{1,3},{2,0},{3,1},{4,6},{5,7},{6,4},{7,5},{8,10},{9,11},{10,... | collective-permute-start | bytes 1572872 | tf_op jit(solution)/shard_map/ppermute | solution.py:251
  4.8 1.6 %collective-permute-start.2 = (bf16[2,64,2048]{2,1,0:T(8,128)(2,1)S(1)}, bf16[2,64,2048]{2,1,0:T(8,128)(2,1)S(1)}, u32[]{:S(2)}, u32[]{:S(2)}) collective-permute-start(bf16[2,64,2048]{2,1,0:T(8,128)(2,1)S(1)} %get-tuple-element.61.refs_0_), channel_id=1, source_target_pairs={{0,4},{1,5},{2,6},{3,7},{4,8},{5,9},{6,10},{7,11},{8,12},{9,13},{1... | collective-permute-start | bytes 1572872 | tf_op jit(solution)/shard_map/ppermute | solution.py:251
  6.4 1.6 %collective-permute-start.4 = (bf16[2,64,2048]{2,1,0:T(8,128)(2,1)S(1)}, bf16[2,64,2048]{2,1,0:T(8,128)(2,1)S(1)}, u32[]{:S(2)}, u32[]{:S(2)}) collective-permute-start(bf16[2,64,2048]{2,1,0:T(8,128)(2,1)S(1)} %collective-permute-done.refs_1_), channel_id=1, source_target_pairs={{0,4},{1,5},{2,6},{3,7},{4,8},{5,9},{6,10},{7,11},{8,12},{9,13},{1... | collective-permute-start | bytes 1572872 | tf_op jit(solution)/shard_map/ppermute | solution.py:251
  8.0 9.7 %collective-permute-done.1.refs_2_ = bf16[2,64,2048]{2,1,0:T(8,128)(2,1)} collective-permute-done((bf16[2,64,2048]{2,1,0:T(8,128)(2,1)S(1)}, bf16[2,64,2048]{2,1,0:T(8,128)(2,1)}, u32[]{:S(2)}, u32[]{:S(2)}) %collective-permute-start.1) | collective-permute-done | bytes 524320 | tf_op jit(solution)/shard_map/ppermute | solution.py:251
  17.7 3.7 %collective-permute-done.2.refs_0_.refs_4_ = bf16[2,64,2048]{2,1,0:T(8,128)(2,1)S(1)} collective-permute-done((bf16[2,64,2048]{2,1,0:T(8,128)(2,1)S(1)}, bf16[2,64,2048]{2,1,0:T(8,128)(2,1)S(1)}, u32[]{:S(2)}, u32[]{:S(2)}) %collective-permute-start.2) | collective-permute-done | bytes 524320 | tf_op jit(solution)/shard_map/ppermute | solution.py:251
  21.5 7.0 %collective-permute-done.3.refs_3_ = bf16[2,64,2048]{2,1,0:T(8,128)(2,1)} collective-permute-done((bf16[2,64,2048]{2,1,0:T(8,128)(2,1)S(1)}, bf16[2,64,2048]{2,1,0:T(8,128)(2,1)}, u32[]{:S(2)}, u32[]{:S(2)}) %collective-permute-start.3) | collective-permute-done | bytes 524320 | tf_op jit(solution)/shard_map/ppermute | solution.py:251
  28.4 4.2 %collective-permute-done.4.refs_1_.refs_5_ = bf16[2,64,2048]{2,1,0:T(8,128)(2,1)S(1)} collective-permute-done((bf16[2,64,2048]{2,1,0:T(8,128)(2,1)S(1)}, bf16[2,64,2048]{2,1,0:T(8,128)(2,1)S(1)}, u32[]{:S(2)}, u32[]{:S(2)}) %collective-permute-start.4) | collective-permute-done | bytes 524320 | tf_op jit(solution)/shard_map/ppermute | solution.py:251
  32.6 7.5 %shard_map.46 = (f32[2,64,512]{2,1,0:T(8,128)S(1)}, f32[2,64,512]{2,1,0:T(8,128)S(1)}, f32[2,64,512]{2,1,0:T(8,128)S(1)}, f32[2,64,512]{2,1,0:T(8,128)S(1)}, f32...) custom-call(s32[1]{0:T(128)} %bitcast.2.half_ref, ...), custom_call_target="tpu_custom_call" | custom-call | flops 1024 | bytes 1024 | tf_op jit(solution)/shard_map/pallas_call | solution.py:167
  40.8 3.0 %collective-permute-done.10.refs_2_.refs_6_ = bf16[2,64,2048]{2,1,0:T(8,128)(2,1)S(1)} collective-permute-done((bf16[2,64,2048]{2,1,0:T(8,128)(2,1)}, bf16[2,64,2048]{2,1,0:T(8,128)(2,1)S(1)}, u32[]{:S(2)}, u32[]{:S(2)}) %collective-permute-start.10) | collective-permute-done | bytes 524320 | tf_op jit(solution)/shard_map/ppermute | solution.py:251
  46.1 8.9 %collective-permute-done.11.refs_3_.refs_7_ = bf16[2,64,2048]{2,1,0:T(8,128)(2,1)S(1)} collective-permute-done((bf16[2,64,2048]{2,1,0:T(8,128)(2,1)}, bf16[2,64,2048]{2,1,0:T(8,128)(2,1)S(1)}, u32[]{:S(2)}, u32[]{:S(2)}) %collective-permute-start.11) | collective-permute-done | bytes 524320 | tf_op jit(solution)/shard_map/ppermute | solution.py:251
  56.3 1.3 %shard_map.47.cols_ref = s32[4]{0:T(128)} custom-call(s32[4]{0:T(128)} %copy-done.22, bf16[2,64,2048]{2,1,0:T(8,128)(2,1)} %copy-done, bf16[2,64,2048]{2,1,0:T(8,128)(2,1)} %copy-done.2, bf16[2,64,2048]{2,1,0:T(8,128)(2,1)} %copy-done.4, bf16[2,64,2048]{2,1,0:T(8,128)(2,1)} %copy-done.6), custom_call_target="tpu_custom_call" | custom-call | flops 9200000000 | bytes 1024 | tf_op jit(solution)/shard_map/pallas_call | solution.py:193
  57.7 2.0 %select_select_fusion.refs_11_ = bf16[2,64,2048]{2,1,0:T(8,128)(2,1)} fusion(bf16[2,64,2048]{2,1,0:T(8,128)(2,1)S(1)} %copy-done.5, bf16[2,64,2048]{2,1,0:T(8,128)(2,1)} %copy-done.6, bf16[2,64,2048]{2,1,0:T(8,128)(2,1)S(1)} %copy-done.1, bf16[2,64,2048]{2,1,0:T(8,128)(2,1)S(1)} %copy-done.3, pred[]{:T(512)S(6)} %eq.7, pred[]{:T(512)S(6)} %eq.6), kind=kLoop, calls=%fused_computation.2 | loop fusion | flops 786432 | bytes 2621442 | tf_op jit(solution)/shard_map/jit(_where)/select_n | solution.py:303
  59.8 7.3 %shard_map.48 = (f32[2,64,512]{2,1,0:T(8,128)S(1)}, f32[2,64,512]{2,1,0:T(8,128)S(1)}, f32[2,64,512]{2,1,0:T(8,128)S(1)}, f32[2,64,512]{2,1,0:T(8,128)S(1)}, f32...) custom-call(s32[1]{0:T(128)} %bitcast.2.half_ref, ...), custom_call_target="tpu_custom_call" | custom-call | flops 1024 | bytes 1024 | tf_op jit(solution)/shard_map/pallas_call | solution.py:167
  69.8 7.8 %collective-permute-done.18.refs_5_ = bf16[2,64,2048]{2,1,0:T(8,128)(2,1)} collective-permute-done((bf16[2,64,2048]{2,1,0:T(8,128)(2,1)}, bf16[2,64,2048]{2,1,0:T(8,128)(2,1)}, u32[]{:S(2)}, u32[]{:S(2)}) %collective-permute-start.18) | collective-permute-done | bytes 524320 | tf_op jit(solution)/shard_map/ppermute | solution.py:251
  77.7 6.8 %shard_map.49 = (f32[2,64,512]{2,1,0:T(8,128)S(1)}, f32[2,64,512]{2,1,0:T(8,128)S(1)}, f32[2,64,512]{2,1,0:T(8,128)S(1)}, f32[2,64,512]{2,1,0:T(8,128)S(1)}) custom-call(s32[1]{0:T(128)} %bitcast.2.half_ref, s32[4]{0:T(128)S(1)} %copy-done.23, s32[2]{0:T(128)S(1)} %pad_add_fusion.1.cols_ref, bf16[2,64,2048]{2,1,0:T(8,128)(2,1)S(1)} %get-tuple-element.61.refs_0_, ...), custom_call_target="tpu_custom_call" | custom-call | flops 1024 | bytes 1024 | tf_op jit(solution)/shard_map/pallas_call | solution.py:167
  86.3 1.8 %collective-permute-done.22.other = bf16[2,64,2048]{2,1,0:T(8,128)(2,1)S(1)} collective-permute-done((bf16[2,64,2048]{2,1,0:T(8,128)(2,1)}, bf16[2,64,2048]{2,1,0:T(8,128)(2,1)S(1)}, u32[]{:S(2)}, u32[]{:S(2)}) %collective-permute-start.22) | collective-permute-done | bytes 524320 | tf_op jit(solution)/shard_map/ppermute | solution.py:251
  88.6 2.1 %shard_map.50.refs_13_ = f32[1,64,512]{2,1,0:T(8,128)S(1)} custom-call(s32[1]{0:T(128)} %bitcast.2.half_ref, bf16[2,64,2048]{2,1,0:T(8,128)(2,1)S(1)} %copy-done.13, bf16[2,64,2048]{2,1,0:T(8,128)(2,1)S(1)} %collective-permute-done.22.other, f32[8,4096]{1,0:T(8,128)S(1)} %copy-done.10, f32[8,4096]{1,0:T(8,128)S(1)} %copy-done.11, ...), custom_call_target="tpu_custom_call" | custom-call | flops 1024 | bytes 1024 | tf_op jit(solution)/shard_map/pallas_call | solution.py:132
  90.7 1.3 %collective-permute-start.23 = (f32[1,64,512]{2,1,0:T(8,128)S(1)}, f32[1,64,512]{2,1,0:T(8,128)S(1)}, u32[]{:S(2)}, u32[]{:S(2)}) collective-permute-start(f32[1,64,512]{2,1,0:T(8,128)S(1)} %shard_map.50.refs_13_), channel_id=1, source_target_pairs={{1,0},{5,4},{9,8},{13,12},{17,16},{21,20},{25,24},{29,28}} | collective-permute-start | bytes 393224 | tf_op jit(solution)/shard_map/ppermute | solution.py:251
  92.0 1.3 %collective-permute-start.24 = (f32[1,64,512]{2,1,0:T(8,128)S(1)}, f32[1,64,512]{2,1,0:T(8,128)S(1)}, u32[]{:S(2)}, u32[]{:S(2)}) collective-permute-start(f32[1,64,512]{2,1,0:T(8,128)S(1)} %shard_map.50.refs_13_), channel_id=1, source_target_pairs={{2,0},{6,4},{10,8},{14,12},{18,16},{22,20},{26,24},{30,28}} | collective-permute-start | bytes 393224 | tf_op jit(solution)/shard_map/ppermute | solution.py:251
  93.3 1.3 %collective-permute-start.25 = (f32[1,64,512]{2,1,0:T(8,128)S(1)}, f32[1,64,512]{2,1,0:T(8,128)S(1)}, u32[]{:S(2)}, u32[]{:S(2)}) collective-permute-start(f32[1,64,512]{2,1,0:T(8,128)S(1)} %shard_map.50.refs_13_), channel_id=1, source_target_pairs={{3,0},{7,4},{11,8},{15,12},{19,16},{23,20},{27,24},{31,28}} | collective-permute-start | bytes 393224 | tf_op jit(solution)/shard_map/ppermute | solution.py:251
  94.7 2.1 %collective-permute-done.21.refs_12_ = f32[2,64,512]{2,1,0:T(8,128)S(1)} collective-permute-done((f32[2,64,512]{2,1,0:T(8,128)S(1)}, f32[2,64,512]{2,1,0:T(8,128)S(1)}, u32[]{:S(2)}, u32[]{:S(2)}) %collective-permute-start.21) | collective-permute-done | bytes 262176 | tf_op jit(solution)/shard_map/ppermute | solution.py:251
  96.8 2.8 %collective-permute-done.24.refs_15_ = f32[1,64,512]{2,1,0:T(8,128)S(1)} collective-permute-done((f32[1,64,512]{2,1,0:T(8,128)S(1)}, f32[1,64,512]{2,1,0:T(8,128)S(1)}, u32[]{:S(2)}, u32[]{:S(2)}) %collective-permute-start.24) | collective-permute-done | bytes 131104 | tf_op jit(solution)/shard_map/ppermute | solution.py:251
  100.3 1.7 %shard_map.51 = f32[1,8,64,512]{3,2,1,0:T(8,128)} custom-call(s32[1]{0:T(128)} %bitcast.q_ref, s32[8]{0:T(128)S(1)} %bitcast.15, f32[2,64,512]{2,1,0:T(8,128)S(1)} %copy-done.15, f32[2,64,512]{2,1,0:T(8,128)S(1)} %copy-done.17, f32[2,64,512]{2,1,0:T(8,128)S(1)} %collective-permute-done.5.refs_2_, f32[2,64,512]{2,1,0:T(8,128)S(1)} %collective-permute-done.6.refs_3_, ...), custom_call_target="tpu_custom_call" | custom-call | tf_op jit(solution)/shard_map/pallas_call | solution.py:318
  (113 shorter events, 10.3 us)
Async XLA Ops:
  1.7 4.7 %collective-permute-start = (bf16[2,64,2048]{2,1,0:T(8,128)(2,1)S(1)}, bf16[2,64,2048]{2,1,0:T(8,128)(2,1)S(1)}, u32[]{:S(2)}, u32[]{:S(2)}) collective-permute-start(bf16[2,64,2048]{2,1,0:T(8,128)(2,1)S(1)} %get-tuple-element.60), channel_id=1, source_target_pairs={{0,1},{1,0},{2,3},{3,2},{4,5},{5,4},{6,7},{7,6},{8,9},{9,8},{10,11... | collective-permute-start | bytes 1572872 | tf_op jit(solution)/shard_map/ppermute | solution.py:251
  2.2 15.5 %collective-permute-start.1 = (bf16[2,64,2048]{2,1,0:T(8,128)(2,1)S(1)}, bf16[2,64,2048]{2,1,0:T(8,128)(2,1)}, u32[]{:S(2)}, u32[]{:S(2)}) collective-permute-start(bf16[2,64,2048]{2,1,0:T(8,128)(2,1)S(1)} %get-tuple-element.62), channel_id=1, source_target_pairs={{0,2},{1,3},{2,0},{3,1},{4,6},{5,7},{6,4},{7,5},{8,10},{9,11},{10,... | collective-permute-start | bytes 1572872 | tf_op jit(solution)/shard_map/ppermute | solution.py:251
  4.8 16.6 %collective-permute-start.2 = (bf16[2,64,2048]{2,1,0:T(8,128)(2,1)S(1)}, bf16[2,64,2048]{2,1,0:T(8,128)(2,1)S(1)}, u32[]{:S(2)}, u32[]{:S(2)}) collective-permute-start(bf16[2,64,2048]{2,1,0:T(8,128)(2,1)S(1)} %get-tuple-element.61.refs_0_), channel_id=1, source_target_pairs={{0,4},{1,5},{2,6},{3,7},{4,8},{5,9},{6,10},{7,11},{8,12},{9,13},{1... | collective-permute-start | bytes 1572872 | tf_op jit(solution)/shard_map/ppermute | solution.py:251
  6.4 22.0 %collective-permute-start.3 = (bf16[2,64,2048]{2,1,0:T(8,128)(2,1)S(1)}, bf16[2,64,2048]{2,1,0:T(8,128)(2,1)}, u32[]{:S(2)}, u32[]{:S(2)}) collective-permute-start(bf16[2,64,2048]{2,1,0:T(8,128)(2,1)S(1)} %get-tuple-element.59), channel_id=1, source_target_pairs={{0,3},{1,2},{2,1},{3,0},{4,7},{5,6},{6,5},{7,4},{8,11},{9,10},{10,... | collective-permute-start | bytes 1572872 | tf_op jit(solution)/shard_map/ppermute | solution.py:251
  6.4 26.2 %collective-permute-start.4 = (bf16[2,64,2048]{2,1,0:T(8,128)(2,1)S(1)}, bf16[2,64,2048]{2,1,0:T(8,128)(2,1)S(1)}, u32[]{:S(2)}, u32[]{:S(2)}) collective-permute-start(bf16[2,64,2048]{2,1,0:T(8,128)(2,1)S(1)} %collective-permute-done.refs_1_), channel_id=1, source_target_pairs={{0,4},{1,5},{2,6},{3,7},{4,8},{5,9},{6,10},{7,11},{8,12},{9,13},{1... | collective-permute-start | bytes 1572872 | tf_op jit(solution)/shard_map/ppermute | solution.py:251
  21.4 22.5 %collective-permute-start.10 = (bf16[2,64,2048]{2,1,0:T(8,128)(2,1)}, bf16[2,64,2048]{2,1,0:T(8,128)(2,1)S(1)}, u32[]{:S(2)}, u32[]{:S(2)}) collective-permute-start(bf16[2,64,2048]{2,1,0:T(8,128)(2,1)} %collective-permute-done.1.refs_2_), channel_id=1, source_target_pairs={{0,4},{1,5},{2,6},{3,7},{4,8},{5,9},{6,10},{7,11},{8,12},{9,13},{1... | collective-permute-start | bytes 1572872 | tf_op jit(solution)/shard_map/ppermute | solution.py:251
  32.6 22.5 %collective-permute-start.11 = (bf16[2,64,2048]{2,1,0:T(8,128)(2,1)}, bf16[2,64,2048]{2,1,0:T(8,128)(2,1)S(1)}, u32[]{:S(2)}, u32[]{:S(2)}) collective-permute-start(bf16[2,64,2048]{2,1,0:T(8,128)(2,1)} %collective-permute-done.3.refs_3_), channel_id=1, source_target_pairs={{0,4},{1,5},{2,6},{3,7},{4,8},{5,9},{6,10},{7,11},{8,12},{9,13},{1... | collective-permute-start | bytes 1572872 | tf_op jit(solution)/shard_map/ppermute | solution.py:251
  40.2 4.6 %collective-permute-start.7 = (f32[2,64,512]{2,1,0:T(8,128)S(1)}, f32[2,64,512]{2,1,0:T(8,128)S(1)}, u32[]{:S(2)}, u32[]{:S(2)}) collective-permute-start(f32[2,64,512]{2,1,0:T(8,128)S(1)} %get-tuple-element.39), channel_id=1, source_target_pairs={{0,1},{1,0},{2,3},{3,2},{4,5},{5,4},{6,7},{7,6},{8,9},{9,8},{10,11... | collective-permute-start | bytes 786440 | tf_op jit(solution)/shard_map/ppermute | solution.py:251
  40.3 4.6 %collective-permute-start.8 = (f32[2,64,512]{2,1,0:T(8,128)S(1)}, f32[2,64,512]{2,1,0:T(8,128)S(1)}, u32[]{:S(2)}, u32[]{:S(2)}) collective-permute-start(f32[2,64,512]{2,1,0:T(8,128)S(1)} %get-tuple-element.41), channel_id=1, source_target_pairs={{0,1},{1,0},{2,3},{3,2},{4,5},{5,4},{6,7},{7,6},{8,9},{9,8},{10,11... | collective-permute-start | bytes 786440 | tf_op jit(solution)/shard_map/ppermute | solution.py:251
  44.8 25.0 %collective-permute-start.17 = (bf16[2,64,2048]{2,1,0:T(8,128)(2,1)}, bf16[2,64,2048]{2,1,0:T(8,128)(2,1)}, u32[]{:S(2)}, u32[]{:S(2)}) collective-permute-start(bf16[2,64,2048]{2,1,0:T(8,128)(2,1)} %broadcast_select_fusion), channel_id=1, source_target_pairs={{0,4},{1,5},{2,6},{3,7},{4,8},{5,9},{6,10},{7,11},{8,12},{9,13},{1... | collective-permute-start | bytes 1572872 | tf_op jit(solution)/shard_map/ppermute | solution.py:251
  45.8 14.0 %collective-permute-start.9 = (f32[4,64,512]{2,1,0:T(8,128)}, f32[4,64,512]{2,1,0:T(8,128)S(1)}, u32[]{:S(2)}, u32[]{:S(2)}) collective-permute-start(f32[4,64,512]{2,1,0:T(8,128)} %pad_maximum_fusion), channel_id=1, source_target_pairs={{0,2},{1,3},{2,0},{3,1},{4,6},{5,7},{6,4},{7,5},{8,10},{9,11},{10,... | collective-permute-start | bytes 1572872 | tf_op jit(solution)/shard_map/ppermute | solution.py:251
  56.0 21.6 %collective-permute-start.18 = (bf16[2,64,2048]{2,1,0:T(8,128)(2,1)}, bf16[2,64,2048]{2,1,0:T(8,128)(2,1)}, u32[]{:S(2)}, u32[]{:S(2)}) collective-permute-start(bf16[2,64,2048]{2,1,0:T(8,128)(2,1)} %broadcast_select_fusion.1), channel_id=1, source_target_pairs={{0,4},{1,5},{2,6},{3,7},{4,8},{5,9},{6,10},{7,11},{8,12},{9,13},{1... | collective-permute-start | bytes 1572872 | tf_op jit(solution)/shard_map/ppermute | solution.py:251
  67.2 1.9 %collective-permute-start.15 = (f32[2,64,512]{2,1,0:T(8,128)S(1)}, f32[2,64,512]{2,1,0:T(8,128)S(1)}, u32[]{:S(2)}, u32[]{:S(2)}) collective-permute-start(f32[2,64,512]{2,1,0:T(8,128)S(1)} %get-tuple-element.53), channel_id=1, source_target_pairs={{0,1},{1,0},{2,3},{3,2},{4,5},{5,4},{6,7},{7,6},{8,9},{9,8},{10,11... | collective-permute-start | bytes 786440 | tf_op jit(solution)/shard_map/ppermute | solution.py:251
  67.7 20.4 %collective-permute-start.22 = (bf16[2,64,2048]{2,1,0:T(8,128)(2,1)}, bf16[2,64,2048]{2,1,0:T(8,128)(2,1)S(1)}, u32[]{:S(2)}, u32[]{:S(2)}) collective-permute-start(bf16[2,64,2048]{2,1,0:T(8,128)(2,1)} %select_select_fusion.refs_11_), channel_id=1, source_target_pairs={{0,4},{1,5},{2,6},{3,7},{4,8},{5,9},{6,10},{7,11},{8,12},{9,13},{1... | collective-permute-start | bytes 1572872 | tf_op jit(solution)/shard_map/ppermute | solution.py:251
  69.2 18.9 %collective-permute-start.16 = (f32[4,64,512]{2,1,0:T(8,128)S(1)}, f32[4,64,512]{2,1,0:T(8,128)S(1)}, u32[]{:S(2)}, u32[]{:S(2)}) collective-permute-start(f32[4,64,512]{2,1,0:T(8,128)S(1)} %pad_maximum_fusion.1.refs_8_), channel_id=1, source_target_pairs={{0,2},{1,3},{2,0},{3,1},{4,6},{5,7},{6,4},{7,5},{8,10},{9,11},{10,... | collective-permute-start | bytes 1572872 | tf_op jit(solution)/shard_map/ppermute | solution.py:251
  69.7 15.4 %collective-permute-start.5 = (f32[2,64,512]{2,1,0:T(8,128)}, f32[2,64,512]{2,1,0:T(8,128)S(1)}, u32[]{:S(2)}, u32[]{:S(2)}) collective-permute-start(f32[2,64,512]{2,1,0:T(8,128)} %copy-done.28), channel_id=1, source_target_pairs={{0,1},{1,0},{2,3},{3,2},{4,5},{5,4},{6,7},{7,6},{8,9},{9,8},{10,11... | collective-permute-start | bytes 786440 | tf_op jit(solution)/shard_map/ppermute | solution.py:251
  84.6 6.1 %collective-permute-start.6 = (f32[2,64,512]{2,1,0:T(8,128)S(1)}, f32[2,64,512]{2,1,0:T(8,128)S(1)}, u32[]{:S(2)}, u32[]{:S(2)}) collective-permute-start(f32[2,64,512]{2,1,0:T(8,128)S(1)} %copy-done.27), channel_id=1, source_target_pairs={{0,1},{1,0},{2,3},{3,2},{4,5},{5,4},{6,7},{7,6},{8,9},{9,8},{10,11... | collective-permute-start | bytes 786440 | tf_op jit(solution)/shard_map/ppermute | solution.py:251
  85.1 6.9 %collective-permute-start.12 = (f32[2,64,512]{2,1,0:T(8,128)S(1)}, f32[2,64,512]{2,1,0:T(8,128)S(1)}, u32[]{:S(2)}, u32[]{:S(2)}) collective-permute-start(f32[2,64,512]{2,1,0:T(8,128)S(1)} %copy-done.32), channel_id=1, source_target_pairs={{0,1},{1,0},{2,3},{3,2},{4,5},{5,4},{6,7},{7,6},{8,9},{9,8},{10,11... | collective-permute-start | bytes 786440 | tf_op jit(solution)/shard_map/ppermute | solution.py:251
  86.1 7.2 %collective-permute-start.13 = (f32[2,64,512]{2,1,0:T(8,128)S(1)}, f32[2,64,512]{2,1,0:T(8,128)S(1)}, u32[]{:S(2)}, u32[]{:S(2)}) collective-permute-start(f32[2,64,512]{2,1,0:T(8,128)S(1)} %copy-done.30), channel_id=1, source_target_pairs={{0,1},{1,0},{2,3},{3,2},{4,5},{5,4},{6,7},{7,6},{8,9},{9,8},{10,11... | collective-permute-start | bytes 786440 | tf_op jit(solution)/shard_map/ppermute | solution.py:251
  88.1 6.6 %collective-permute-start.19 = (f32[2,64,512]{2,1,0:T(8,128)S(1)}, f32[2,64,512]{2,1,0:T(8,128)S(1)}, u32[]{:S(2)}, u32[]{:S(2)}) collective-permute-start(f32[2,64,512]{2,1,0:T(8,128)S(1)} %get-tuple-element.55), channel_id=1, source_target_pairs={{0,1},{1,0},{2,3},{3,2},{4,5},{5,4},{6,7},{7,6},{8,9},{9,8},{10,11... | collective-permute-start | bytes 786440 | tf_op jit(solution)/shard_map/ppermute | solution.py:251
  88.1 8.7 %collective-permute-start.21 = (f32[2,64,512]{2,1,0:T(8,128)S(1)}, f32[2,64,512]{2,1,0:T(8,128)S(1)}, u32[]{:S(2)}, u32[]{:S(2)}) collective-permute-start(f32[2,64,512]{2,1,0:T(8,128)S(1)} %add.41.refs_0_), channel_id=1, source_target_pairs={{0,2},{1,3},{2,0},{3,1},{4,6},{5,7},{6,4},{7,5},{8,10},{9,11},{10,... | collective-permute-start | bytes 786440 | tf_op jit(solution)/shard_map/ppermute | solution.py:251
  90.7 6.1 %collective-permute-start.23 = (f32[1,64,512]{2,1,0:T(8,128)S(1)}, f32[1,64,512]{2,1,0:T(8,128)S(1)}, u32[]{:S(2)}, u32[]{:S(2)}) collective-permute-start(f32[1,64,512]{2,1,0:T(8,128)S(1)} %shard_map.50.refs_13_), channel_id=1, source_target_pairs={{1,0},{5,4},{9,8},{13,12},{17,16},{21,20},{25,24},{29,28}} | collective-permute-start | bytes 393224 | tf_op jit(solution)/shard_map/ppermute | solution.py:251
  92.0 7.6 %collective-permute-start.24 = (f32[1,64,512]{2,1,0:T(8,128)S(1)}, f32[1,64,512]{2,1,0:T(8,128)S(1)}, u32[]{:S(2)}, u32[]{:S(2)}) collective-permute-start(f32[1,64,512]{2,1,0:T(8,128)S(1)} %shard_map.50.refs_13_), channel_id=1, source_target_pairs={{2,0},{6,4},{10,8},{14,12},{18,16},{22,20},{26,24},{30,28}} | collective-permute-start | bytes 393224 | tf_op jit(solution)/shard_map/ppermute | solution.py:251
  93.3 7.0 %collective-permute-start.25 = (f32[1,64,512]{2,1,0:T(8,128)S(1)}, f32[1,64,512]{2,1,0:T(8,128)S(1)}, u32[]{:S(2)}, u32[]{:S(2)}) collective-permute-start(f32[1,64,512]{2,1,0:T(8,128)S(1)} %shard_map.50.refs_13_), channel_id=1, source_target_pairs={{3,0},{7,4},{11,8},{15,12},{19,16},{23,20},{27,24},{31,28}} | collective-permute-start | bytes 393224 | tf_op jit(solution)/shard_map/ppermute | solution.py:251
  (35 other events, 383.6 us)

commit v5 on v4

--- a/solution.py
+++ b/solution.py
@@ -14,6 +14,7 @@
 LAGS = 8
 MID = LAGS // 2
 TILE = 512
+FIRST, SECOND = 3_450_000_000, 23_000_000_000
 LIMIT = 40 * 1024 * 1024
 
 
@@ -200,34 +201,45 @@
     )(scalars, *others)
 
 
-def final_kernel(norm, q_ref, flags_ref, *refs):
-    same, near, far, last = refs[0:5], refs[5:10], refs[10:13], refs[13:17]
-    out = refs[17]
+def plane_sum(parts, j):
+    each = len(parts) // 2
+    n, r = divmod(j, 2)
+    return parts[n][r] + parts[each + n][r] + parts[-1][j]
+
+
+def early_kernel(norm, q_ref, flags_ref, *refs):
+    same, near, out = refs[0:5], refs[5:10], refs[10]
     q = q_ref[0]
-
-    def emit(total, d):
-        out[0, d] = total * (flags_ref[d].astype(jnp.float32) * norm)
-
-    def plane_sum(parts, j):
-        each = len(parts) // 2
-        n, r = divmod(j, 2)
-        return parts[n][r] + parts[each + n][r] + parts[-1][j]
-
     for j in range(PLANE):
-        emit(plane_sum(near, j), PLANE + q - j)
+        d = PLANE + q - j
+        out[0, d] = plane_sum(near, j) * (flags_ref[d].astype(jnp.float32) * norm)
 
         @pl.when(j <= q)
         def _():
-            emit(plane_sum(same, j), q - j)
-
-    for j in (2, 3):
-        @pl.when(j > q)
-        def _():
-            emit(plane_sum(far, j - 2), 2 * PLANE + q - j)
-
-    @pl.when(q == 0)
-    def _():
-        emit(last[0][0] + last[1][0] + last[2][0] + last[3][0], 2 * PLANE - 1)
+            out[0, q - j] = plane_sum(same, j) * (flags_ref[q - j].astype(jnp.float32) * norm)
+
+
+def final_kernel(norm, q_ref, flags_ref, _, *refs):
+    far, last, (out, buf, sems) = refs[0:3], refs[3:-3], refs[-3:]
+    q = q_ref[0]
+
+    def each(act):
+        for n, j in enumerate((2, 3, 1)):
+            d = 2 * PLANE + q - j
+            pl.when(j > q)(functools.partial(act, n, j, d)) if j > 1 else pl.when(q == 0)(
+                functools.partial(act, n, j, d)
+            )
+
+    def write(n, j, d):
+        total = plane_sum(far, j - 2) if j > 1 else sum([x[0] for x in last[1:]], last[0][0])
+        buf[n] = total * (flags_ref[d].astype(jnp.float32) * norm)
+        pltpu.make_async_copy(buf.at[n], out.at[0, d], sems.at[n]).start()
+
+    def wait(n, j, d):
+        pltpu.make_async_copy(buf.at[n], out.at[0, d], sems.at[n]).wait()
+
+    each(write)
+    each(wait)
 
 
 def per_device(spectra, pair_valid):
@@ -290,7 +302,9 @@
     here = [mine, sib, cross, diag]
     near = [near0, near1, near2, near3]
     half = ints(c)
-    *parts, lead = products(here, [], half, slots, slots, tables, lead=True, before=[])
+    *parts, lead = products(
+        here, [], half, slots, gate(slots, [near0], FIRST), tables, lead=True
+    )
     same_core = in_core(parts)
     same_sum = across(same_core)
 
@@ -304,7 +318,10 @@
     last = move(last_send, up)
 
     near_core = in_core(
-        products(here, near, half, slots, gate(slots, [near0, near1, near2, near3], 9200000000), tables, before=[same_sum[-1], last_send])
+        products(
+            here, near, half, slots, gate(slots, near, SECOND), tables,
+            before=[same_sum[-1], last_send],
+        )
     )
     near_sum = across(near_core)
     far_core = in_core(products(
@@ -313,16 +330,33 @@
     ))
     far_sum = across(far_core)
     last_part = last_product(lead, last, half, tables, [far_core[2], near_sum[-1]])
-    last_sum = [last_part] + [move(last_part, to_plane(k), k) for k in (1, 2, 3)]
-
+    from_y = move(last_part, to_plane(2), 2) + move(last_part, to_plane(3), 3)
+    last_sum = [last_part, move(last_part, to_plane(1), 1), from_y]
+
+    smem = pl.BlockSpec(memory_space=pltpu.SMEM)
+    vmem = pl.BlockSpec(memory_space=pltpu.VMEM)
+    anywhere = pl.BlockSpec(memory_space=pl.ANY)
+    shape = jax.ShapeDtypeStruct((1, steps, width, LAGS * width), jnp.float32)
+    params = pltpu.CompilerParams(vmem_limit_bytes=LIMIT)
+    early = pl.pallas_call(
+        functools.partial(early_kernel, norm),
+        out_shape=shape,
+        in_specs=[smem] * 2 + [vmem] * 10,
+        out_specs=vmem,
+        compiler_params=params,
+        cost_estimate=pl.CostEstimate(flops=1024, bytes_accessed=1024, transcendentals=0),
+    )(ints(q), pair_valid[0], *same_sum, *near_sum)
     return pl.pallas_call(
         functools.partial(final_kernel, norm),
-        out_shape=jax.ShapeDtypeStruct((1, steps, width, LAGS * width), jnp.float32),
-        in_specs=[pl.BlockSpec(memory_space=pltpu.SMEM)] * 2
-        + [pl.BlockSpec(memory_space=pltpu.VMEM)] * 17,
-        out_specs=pl.BlockSpec(memory_space=pltpu.VMEM),
-        compiler_params=pltpu.CompilerParams(vmem_limit_bytes=LIMIT),
-    )(ints(q), pair_valid[0], *same_sum, *near_sum, *far_sum, *last_sum)
+        out_shape=shape,
+        in_specs=[smem] * 2 + [anywhere] + [vmem] * 6,
+        out_specs=anywhere,
+        scratch_shapes=[
+            pltpu.VMEM((3, width, LAGS * width), jnp.float32), pltpu.SemaphoreType.DMA((3,))
+        ],
+        input_output_aliases={2: 0},
+        compiler_params=params,
+    )(ints(q), pair_valid[0], early, *far_sum, *last_sum)
 
 
 def solution(mesh):

time: 102 us -> 101 us (level)
  waiting for transfers between devices: 52.8 us -> 41.6 us
  starting transfers between devices: 14.9 us -> 20.5 us
  Pallas kernels: 26.9 us -> 29.5 us
  local copies, waits for them, and re-layouts: 1.83 us -> 3.25 us
    ppermute x26, waiting for transfers between devices: 52.8 us -> 41.6 us  [move(): return lax.ppermute(value, 'chan', pairs)]
    ppermute x26, starting transfers between devices: 14.9 us -> 20.5 us  [move(): return lax.ppermute(value, 'chan', pairs)]
    pallas_call x1 -> x2, Pallas kernels: 1.73 us -> 3.51 us  [the longest x1 2.17 us: per_device(): pl.pallas_call(functools.partial(early_kernel, norm), out_shape=shape, in...]
    pallas_call x1 -> x2, Pallas kernels: 1.32 us -> 2.63 us  [gate(): pl.pallas_call(gate_kernel, out_shape=jax.ShapeDtypeStruct(scalars.shape,...]
  transfers between devices with their start and end apart: 26 -> 26, of which waited for: 13 -> 11; matrix products, arithmetic and copies ran while one was open for 5% -> 5% of each run, Pallas kernels for 25% -> 28%
where the time goes in v5:
time: 101 us
  waiting for transfers between devices  41.6 us (41%)
  Pallas kernels  29.5 us (29%)
  starting transfers between devices  20.5 us (20%)
  other arithmetic  5.55 us (5%)
  local copies, waits for them, and re-layouts  3.25 us (3%)
    ppermute x26, waiting for transfers between devices, move(): return lax.ppermute(value, 'chan', pairs)  41.6 us
    pallas_call x3, Pallas kernels, products(): pl.pallas_call(body, out_shape=outs, grid_spec=pltpu.PrefetchScalarGridSp...  21.2 us
    ppermute x26, starting transfers between devices, move(): return lax.ppermute(value, 'chan', pairs)  20.5 us
    pallas_call x2, Pallas kernels, gate(): pl.pallas_call(gate_kernel, out_shape=jax.ShapeDtypeStruct(scalars.shape,...  2.63 us
    squeeze x1, local copies, waits for them, and re-layouts, piece(): lax.dynamic_slice(block, (s, 0, 0, h * half_bins), (1, 2, width, half_bins))  2.49 us
    pallas_call x1, Pallas kernels, per_device(): pl.pallas_call(functools.partial(early_kernel, norm), out_shape=shape, in...  2.17 us
    pallas_call x1, Pallas kernels, last_product(): pl.pallas_call(last_kernel, out_shape=jax.ShapeDtypeStruct(shape, jnp.flo...  2.12 us
  transfers between devices with their start and end apart: 26, of which 11 were waited for; matrix products, arithmetic and copies ran while one was open for 5% of the time, Pallas kernels for 28%

profile of v5, /device:TPU:0, one launch (start us, length us, event | category | flops | bytes accessed | tf_op | source)
XLA Modules:
  0.0 101.1 jit_solution(7664316576717764699)
XLA Ops:
  0.0 2.5 %dynamic-slice_bitcast_fusion = (bf16[2,64,2048]{2,1,0:T(8,128)(2,1)}, bf16[2,64,2048]{2,1,0:T(8,128)(2,1)S(1)}, bf16[2,64,2048]{2,1,0:T(8,128)(2,1)S(1)}, bf16[2,64,2048]{2,1,0:T(8,128)(2,1)S(1)}) fusion(bf16[1,2,2,64,4096]{4,3,2,1,0:T(8,128)(2,1)} %param.4, s32[]{:T(128)S(6)} %select_n.52, s32[]{:T(128)S(6)} %select_n.51, s32[]{:T(128)S(6)} %select_n.49, ...), kind=kLoop, calls=%fused_computation.3 | loop fusion | bytes 4194320 | tf_op jit(solution)/shard_map/squeeze | solution.py:277
  2.9 2.6 %collective-permute-start = (bf16[2,64,2048]{2,1,0:T(8,128)(2,1)S(1)}, bf16[2,64,2048]{2,1,0:T(8,128)(2,1)S(1)}, u32[]{:S(2)}, u32[]{:S(2)}) collective-permute-start(bf16[2,64,2048]{2,1,0:T(8,128)(2,1)S(1)} %get-tuple-element.61.refs_0_), channel_id=1, source_target_pairs={{0,4},{1,5},{2,6},{3,7},{4,8},{5,9},{6,10},{7,11},{8,12},{9,13},{1... | collective-permute-start | bytes 1572872 | tf_op jit(solution)/shard_map/ppermute | solution.py:263
  5.5 1.5 %collective-permute-start.2 = (bf16[2,64,2048]{2,1,0:T(8,128)(2,1)S(1)}, bf16[2,64,2048]{2,1,0:T(8,128)(2,1)}, u32[]{:S(2)}, u32[]{:S(2)}) collective-permute-start(bf16[2,64,2048]{2,1,0:T(8,128)(2,1)S(1)} %get-tuple-element.62), channel_id=1, source_target_pairs={{0,2},{1,3},{2,0},{3,1},{4,6},{5,7},{6,4},{7,5},{8,10},{9,11},{10,... | collective-permute-start | bytes 1572872 | tf_op jit(solution)/shard_map/ppermute | solution.py:263
  7.1 1.6 %collective-permute-start.4 = (bf16[2,64,2048]{2,1,0:T(8,128)(2,1)S(1)}, bf16[2,64,2048]{2,1,0:T(8,128)(2,1)S(1)}, u32[]{:S(2)}, u32[]{:S(2)}) collective-permute-start(bf16[2,64,2048]{2,1,0:T(8,128)(2,1)S(1)} %collective-permute-done.1.refs_1_), channel_id=1, source_target_pairs={{0,4},{1,5},{2,6},{3,7},{4,8},{5,9},{6,10},{7,11},{8,12},{9,13},{1... | collective-permute-start | bytes 1572872 | tf_op jit(solution)/shard_map/ppermute | solution.py:263
  8.7 11.6 %collective-permute-done.refs_0_.refs_4_ = bf16[2,64,2048]{2,1,0:T(8,128)(2,1)S(1)} collective-permute-done((bf16[2,64,2048]{2,1,0:T(8,128)(2,1)S(1)}, bf16[2,64,2048]{2,1,0:T(8,128)(2,1)S(1)}, u32[]{:S(2)}, u32[]{:S(2)}) %collective-permute-start) | collective-permute-done | bytes 524320 | tf_op jit(solution)/shard_map/ppermute | solution.py:263
  20.4 1.6 %collective-permute-start.10 = (bf16[2,64,2048]{2,1,0:T(8,128)(2,1)}, bf16[2,64,2048]{2,1,0:T(8,128)(2,1)S(1)}, u32[]{:S(2)}, u32[]{:S(2)}) collective-permute-start(bf16[2,64,2048]{2,1,0:T(8,128)(2,1)} %collective-permute-done.2.refs_2_), channel_id=1, source_target_pairs={{0,4},{1,5},{2,6},{3,7},{4,8},{5,9},{6,10},{7,11},{8,12},{9,13},{1... | collective-permute-start | bytes 1572872 | tf_op jit(solution)/shard_map/ppermute | solution.py:263
  23.9 6.2 %collective-permute-done.3.refs_3_ = bf16[2,64,2048]{2,1,0:T(8,128)(2,1)S(1)} collective-permute-done((bf16[2,64,2048]{2,1,0:T(8,128)(2,1)}, bf16[2,64,2048]{2,1,0:T(8,128)(2,1)S(1)}, u32[]{:S(2)}, u32[]{:S(2)}) %collective-permute-start.3) | collective-permute-done | bytes 524320 | tf_op jit(solution)/shard_map/ppermute | solution.py:263
  30.1 1.4 %collective-permute-done.4.refs_1_.refs_5_ = bf16[2,64,2048]{2,1,0:T(8,128)(2,1)S(1)} collective-permute-done((bf16[2,64,2048]{2,1,0:T(8,128)(2,1)S(1)}, bf16[2,64,2048]{2,1,0:T(8,128)(2,1)S(1)}, u32[]{:S(2)}, u32[]{:S(2)}) %collective-permute-start.4) | collective-permute-done | bytes 524320 | tf_op jit(solution)/shard_map/ppermute | solution.py:263
  32.4 7.3 %shard_map.47 = (f32[2,64,512]{2,1,0:T(8,128)S(1)}, f32[2,64,512]{2,1,0:T(8,128)S(1)}, f32[2,64,512]{2,1,0:T(8,128)S(1)}, f32[2,64,512]{2,1,0:T(8,128)S(1)}, f32...) custom-call(s32[1]{0:T(128)} %bitcast.2.half_ref, ...), custom_call_target="tpu_custom_call" | custom-call | flops 1024 | bytes 1024 | tf_op jit(solution)/shard_map/pallas_call | solution.py:168
  40.5 2.3 %collective-permute-done.10.refs_2_.refs_6_ = bf16[2,64,2048]{2,1,0:T(8,128)(2,1)S(1)} collective-permute-done((bf16[2,64,2048]{2,1,0:T(8,128)(2,1)}, bf16[2,64,2048]{2,1,0:T(8,128)(2,1)S(1)}, u32[]{:S(2)}, u32[]{:S(2)}) %collective-permute-start.10) | collective-permute-done | bytes 524320 | tf_op jit(solution)/shard_map/ppermute | solution.py:263
  44.7 1.7 %collective-permute-start.9 = (f32[4,64,512]{2,1,0:T(8,128)}, f32[4,64,512]{2,1,0:T(8,128)}, u32[]{:S(2)}, u32[]{:S(2)}) collective-permute-start(f32[4,64,512]{2,1,0:T(8,128)} %pad_maximum_fusion), channel_id=1, source_target_pairs={{0,2},{1,3},{2,0},{3,1},{4,6},{5,7},{6,4},{7,5},{8,10},{9,11},{10,... | collective-permute-start | bytes 1572872 | tf_op jit(solution)/shard_map/ppermute | solution.py:263
  46.4 7.6 %collective-permute-done.11.refs_3_.refs_7_ = bf16[2,64,2048]{2,1,0:T(8,128)(2,1)S(1)} collective-permute-done((bf16[2,64,2048]{2,1,0:T(8,128)(2,1)S(1)}, bf16[2,64,2048]{2,1,0:T(8,128)(2,1)S(1)}, u32[]{:S(2)}, u32[]{:S(2)}) %collective-permute-start.11) | collective-permute-done | bytes 524320 | tf_op jit(solution)/shard_map/ppermute | solution.py:263
  56.6 2.0 %select_select_fusion.refs_11_ = bf16[2,64,2048]{2,1,0:T(8,128)(2,1)} fusion(bf16[2,64,2048]{2,1,0:T(8,128)(2,1)S(1)} %copy-done.6, bf16[2,64,2048]{2,1,0:T(8,128)(2,1)} %copy-done.7, bf16[2,64,2048]{2,1,0:T(8,128)(2,1)S(1)} %copy-done.2, bf16[2,64,2048]{2,1,0:T(8,128)(2,1)S(1)} %copy-done.4, pred[]{:T(512)S(6)} %eq.7, pred[]{:T(512)S(6)} %eq.6), kind=kLoop, calls=%fused_computation.2 | loop fusion | flops 786432 | bytes 2621442 | tf_op jit(solution)/shard_map/jit(_where)/select_n | solution.py:317
  58.7 7.2 %shard_map.49 = (f32[2,64,512]{2,1,0:T(8,128)S(1)}, f32[2,64,512]{2,1,0:T(8,128)S(1)}, f32[2,64,512]{2,1,0:T(8,128)S(1)}, f32[2,64,512]{2,1,0:T(8,128)S(1)}, f32...) custom-call(s32[1]{0:T(128)} %bitcast.2.half_ref, ...), custom_call_target="tpu_custom_call" | custom-call | flops 1024 | bytes 1024 | tf_op jit(solution)/shard_map/pallas_call | solution.py:168
  66.5 1.3 %collective-permute-start.22 = (bf16[2,64,2048]{2,1,0:T(8,128)(2,1)}, bf16[2,64,2048]{2,1,0:T(8,128)(2,1)S(1)}, u32[]{:S(2)}, u32[]{:S(2)}) collective-permute-start(bf16[2,64,2048]{2,1,0:T(8,128)(2,1)} %select_select_fusion.refs_11_), channel_id=1, source_target_pairs={{0,4},{1,5},{2,6},{3,7},{4,8},{5,9},{6,10},{7,11},{8,12},{9,13},{1... | collective-permute-start | bytes 1572872 | tf_op jit(solution)/shard_map/ppermute | solution.py:263
  68.0 1.7 %collective-permute-start.16 = (f32[4,64,512]{2,1,0:T(8,128)S(1)}, f32[4,64,512]{2,1,0:T(8,128)S(1)}, u32[]{:S(2)}, u32[]{:S(2)}) collective-permute-start(f32[4,64,512]{2,1,0:T(8,128)S(1)} %pad_maximum_fusion.1.refs_8_), channel_id=1, source_target_pairs={{0,2},{1,3},{2,0},{3,1},{4,6},{5,7},{6,4},{7,5},{8,10},{9,11},{10,... | collective-permute-start | bytes 1572872 | tf_op jit(solution)/shard_map/ppermute | solution.py:263
  69.9 6.7 %collective-permute-done.18.refs_5_ = bf16[2,64,2048]{2,1,0:T(8,128)(2,1)} collective-permute-done((bf16[2,64,2048]{2,1,0:T(8,128)(2,1)}, bf16[2,64,2048]{2,1,0:T(8,128)(2,1)}, u32[]{:S(2)}, u32[]{:S(2)}) %collective-permute-start.18) | collective-permute-done | bytes 524320 | tf_op jit(solution)/shard_map/ppermute | solution.py:263
  76.6 6.7 %shard_map.51 = (f32[2,64,512]{2,1,0:T(8,128)S(1)}, f32[2,64,512]{2,1,0:T(8,128)S(1)}, f32[2,64,512]{2,1,0:T(8,128)S(1)}, f32[2,64,512]{2,1,0:T(8,128)S(1)}) custom-call(s32[1]{0:T(128)} %bitcast.2.half_ref, s32[4]{0:T(128)S(1)} %copy-done.25, s32[2]{0:T(128)S(1)} %pad_add_fusion.1.cols_ref, bf16[2,64,2048]{2,1,0:T(8,128)(2,1)S(1)} %get-tuple-element.61.refs_0_, ...), custom_call_target="tpu_custom_call" | custom-call | flops 1024 | bytes 1024 | tf_op jit(solution)/shard_map/pallas_call | solution.py:168
  85.1 2.4 %collective-permute-done.22.other = bf16[2,64,2048]{2,1,0:T(8,128)(2,1)S(1)} collective-permute-done((bf16[2,64,2048]{2,1,0:T(8,128)(2,1)}, bf16[2,64,2048]{2,1,0:T(8,128)(2,1)S(1)}, u32[]{:S(2)}, u32[]{:S(2)}) %collective-permute-start.22) | collective-permute-done | bytes 524320 | tf_op jit(solution)/shard_map/ppermute | solution.py:263
  87.6 1.5 %collective-permute-start.21 = (f32[2,64,512]{2,1,0:T(8,128)S(1)}, f32[2,64,512]{2,1,0:T(8,128)S(1)}, u32[]{:S(2)}, u32[]{:S(2)}) collective-permute-start(f32[2,64,512]{2,1,0:T(8,128)S(1)} %add.44.refs_0_), channel_id=1, source_target_pairs={{0,2},{1,3},{2,0},{3,1},{4,6},{5,7},{6,4},{7,5},{8,10},{9,11},{10,... | collective-permute-start | bytes 786440 | tf_op jit(solution)/shard_map/ppermute | solution.py:263
  89.1 2.1 %shard_map.52.refs_3_ = f32[1,64,512]{2,1,0:T(8,128)S(1)} custom-call(s32[1]{0:T(128)} %bitcast.2.half_ref, bf16[2,64,2048]{2,1,0:T(8,128)(2,1)S(1)} %copy-done.15, bf16[2,64,2048]{2,1,0:T(8,128)(2,1)S(1)} %collective-permute-done.22.other, f32[8,4096]{1,0:T(8,128)S(1)} %copy-done.12, f32[8,4096]{1,0:T(8,128)S(1)} %copy-done.13, ...), custom_call_target="tpu_custom_call" | custom-call | flops 1024 | bytes 1024 | tf_op jit(solution)/shard_map/pallas_call | solution.py:133
  95.2 2.2 %shard_map.50._ = f32[1,8,64,512]{3,2,1,0:T(8,128)} custom-call(s32[1]{0:T(128)} %bitcast.q_ref, s32[8]{0:T(128)S(1)} %bitcast.15, f32[2,64,512]{2,1,0:T(8,128)S(1)} %copy-done.17, f32[2,64,512]{2,1,0:T(8,128)S(1)} %copy-done.19, f32[2,64,512]{2,1,0:T(8,128)S(1)} %collective-permute-done.5.refs_2_, f32[2,64,512]{2,1,0:T(8,128)S(1)} %collective-permute-done.6.refs_3_, ...), custom_call_target="tpu_custom_call" | custom-call | flops 1024 | bytes 1024 | tf_op jit(solution)/shard_map/pallas_call | solution.py:341
  97.4 1.4 %collective-permute-done.24 = f32[1,64,512]{2,1,0:T(8,128)S(1)} collective-permute-done((f32[1,64,512]{2,1,0:T(8,128)S(1)}, f32[1,64,512]{2,1,0:T(8,128)S(1)}, u32[]{:S(2)}, u32[]{:S(2)}) %collective-permute-start.24) | collective-permute-done | bytes 131104 | tf_op jit(solution)/shard_map/ppermute | solution.py:263
  99.5 1.3 %shard_map.53 = f32[1,8,64,512]{3,2,1,0:T(8,128)} custom-call(s32[1]{0:T(128)} %bitcast.q_ref, s32[8]{0:T(128)S(1)} %bitcast.16, f32[1,8,64,512]{3,2,1,0:T(8,128)} %shard_map.50._, f32[2,64,512]{2,1,0:T(8,128)S(1)} %get-tuple-element.54.refs_0_, f32[2,64,512]{2,1,0:T(8,128)S(1)} %collective-permute-done.19.refs_1_, ...), custom_call_target="tpu_custom_call", output_to_operand_aliasing={{}: (2, {})} | custom-call | tf_op jit(solution)/shard_map/pallas_call | solution.py:349
  (122 shorter events, 15.6 us)
Async XLA Ops:
  2.5 4.6 %collective-permute-start.1 = (bf16[2,64,2048]{2,1,0:T(8,128)(2,1)S(1)}, bf16[2,64,2048]{2,1,0:T(8,128)(2,1)S(1)}, u32[]{:S(2)}, u32[]{:S(2)}) collective-permute-start(bf16[2,64,2048]{2,1,0:T(8,128)(2,1)S(1)} %get-tuple-element.60), channel_id=1, source_target_pairs={{0,1},{1,0},{2,3},{3,2},{4,5},{5,4},{6,7},{7,6},{8,9},{9,8},{10,11... | collective-permute-start | bytes 1572872 | tf_op jit(solution)/shard_map/ppermute | solution.py:263
  2.9 17.4 %collective-permute-start = (bf16[2,64,2048]{2,1,0:T(8,128)(2,1)S(1)}, bf16[2,64,2048]{2,1,0:T(8,128)(2,1)S(1)}, u32[]{:S(2)}, u32[]{:S(2)}) collective-permute-start(bf16[2,64,2048]{2,1,0:T(8,128)(2,1)S(1)} %get-tuple-element.61.refs_0_), channel_id=1, source_target_pairs={{0,4},{1,5},{2,6},{3,7},{4,8},{5,9},{6,10},{7,11},{8,12},{9,13},{1... | collective-permute-start | bytes 1572872 | tf_op jit(solution)/shard_map/ppermute | solution.py:263
  5.5 14.9 %collective-permute-start.2 = (bf16[2,64,2048]{2,1,0:T(8,128)(2,1)S(1)}, bf16[2,64,2048]{2,1,0:T(8,128)(2,1)}, u32[]{:S(2)}, u32[]{:S(2)}) collective-permute-start(bf16[2,64,2048]{2,1,0:T(8,128)(2,1)S(1)} %get-tuple-element.62), channel_id=1, source_target_pairs={{0,2},{1,3},{2,0},{3,1},{4,6},{5,7},{6,4},{7,5},{8,10},{9,11},{10,... | collective-permute-start | bytes 1572872 | tf_op jit(solution)/shard_map/ppermute | solution.py:263
  7.0 23.1 %collective-permute-start.3 = (bf16[2,64,2048]{2,1,0:T(8,128)(2,1)}, bf16[2,64,2048]{2,1,0:T(8,128)(2,1)S(1)}, u32[]{:S(2)}, u32[]{:S(2)}) collective-permute-start(bf16[2,64,2048]{2,1,0:T(8,128)(2,1)} %get-tuple-element.59), channel_id=1, source_target_pairs={{0,3},{1,2},{2,1},{3,0},{4,7},{5,6},{6,5},{7,4},{8,11},{9,10},{10,... | collective-permute-start | bytes 1572872 | tf_op jit(solution)/shard_map/ppermute | solution.py:263
  7.1 24.5 %collective-permute-start.4 = (bf16[2,64,2048]{2,1,0:T(8,128)(2,1)S(1)}, bf16[2,64,2048]{2,1,0:T(8,128)(2,1)S(1)}, u32[]{:S(2)}, u32[]{:S(2)}) collective-permute-start(bf16[2,64,2048]{2,1,0:T(8,128)(2,1)S(1)} %collective-permute-done.1.refs_1_), channel_id=1, source_target_pairs={{0,4},{1,5},{2,6},{3,7},{4,8},{5,9},{6,10},{7,11},{8,12},{9,13},{1... | collective-permute-start | bytes 1572872 | tf_op jit(solution)/shard_map/ppermute | solution.py:263
  20.4 22.4 %collective-permute-start.10 = (bf16[2,64,2048]{2,1,0:T(8,128)(2,1)}, bf16[2,64,2048]{2,1,0:T(8,128)(2,1)S(1)}, u32[]{:S(2)}, u32[]{:S(2)}) collective-permute-start(bf16[2,64,2048]{2,1,0:T(8,128)(2,1)} %collective-permute-done.2.refs_2_), channel_id=1, source_target_pairs={{0,4},{1,5},{2,6},{3,7},{4,8},{5,9},{6,10},{7,11},{8,12},{9,13},{1... | collective-permute-start | bytes 1572872 | tf_op jit(solution)/shard_map/ppermute | solution.py:263
  31.6 22.5 %collective-permute-start.11 = (bf16[2,64,2048]{2,1,0:T(8,128)(2,1)S(1)}, bf16[2,64,2048]{2,1,0:T(8,128)(2,1)S(1)}, u32[]{:S(2)}, u32[]{:S(2)}) collective-permute-start(bf16[2,64,2048]{2,1,0:T(8,128)(2,1)S(1)} %collective-permute-done.3.refs_3_), channel_id=1, source_target_pairs={{0,4},{1,5},{2,6},{3,7},{4,8},{5,9},{6,10},{7,11},{8,12},{9,13},{1... | collective-permute-start | bytes 1572872 | tf_op jit(solution)/shard_map/ppermute | solution.py:263
  39.8 3.9 %collective-permute-start.7 = (f32[2,64,512]{2,1,0:T(8,128)S(1)}, f32[2,64,512]{2,1,0:T(8,128)S(1)}, u32[]{:S(2)}, u32[]{:S(2)}) collective-permute-start(f32[2,64,512]{2,1,0:T(8,128)S(1)} %get-tuple-element.39), channel_id=1, source_target_pairs={{0,1},{1,0},{2,3},{3,2},{4,5},{5,4},{6,7},{7,6},{8,9},{9,8},{10,11... | collective-permute-start | bytes 786440 | tf_op jit(solution)/shard_map/ppermute | solution.py:263
  40.4 3.4 %collective-permute-start.8 = (f32[2,64,512]{2,1,0:T(8,128)S(1)}, f32[2,64,512]{2,1,0:T(8,128)S(1)}, u32[]{:S(2)}, u32[]{:S(2)}) collective-permute-start(f32[2,64,512]{2,1,0:T(8,128)S(1)} %get-tuple-element.41), channel_id=1, source_target_pairs={{0,1},{1,0},{2,3},{3,2},{4,5},{5,4},{6,7},{7,6},{8,9},{9,8},{10,11... | collective-permute-start | bytes 786440 | tf_op jit(solution)/shard_map/ppermute | solution.py:263
  43.7 26.2 %collective-permute-start.17 = (bf16[2,64,2048]{2,1,0:T(8,128)(2,1)}, bf16[2,64,2048]{2,1,0:T(8,128)(2,1)}, u32[]{:S(2)}, u32[]{:S(2)}) collective-permute-start(bf16[2,64,2048]{2,1,0:T(8,128)(2,1)} %broadcast_select_fusion), channel_id=1, source_target_pairs={{0,4},{1,5},{2,6},{3,7},{4,8},{5,9},{6,10},{7,11},{8,12},{9,13},{1... | collective-permute-start | bytes 1572872 | tf_op jit(solution)/shard_map/ppermute | solution.py:263
  44.7 14.0 %collective-permute-start.9 = (f32[4,64,512]{2,1,0:T(8,128)}, f32[4,64,512]{2,1,0:T(8,128)}, u32[]{:S(2)}, u32[]{:S(2)}) collective-permute-start(f32[4,64,512]{2,1,0:T(8,128)} %pad_maximum_fusion), channel_id=1, source_target_pairs={{0,2},{1,3},{2,0},{3,1},{4,6},{5,7},{6,4},{7,5},{8,10},{9,11},{10,... | collective-permute-start | bytes 1572872 | tf_op jit(solution)/shard_map/ppermute | solution.py:263
  55.0 21.6 %collective-permute-start.18 = (bf16[2,64,2048]{2,1,0:T(8,128)(2,1)}, bf16[2,64,2048]{2,1,0:T(8,128)(2,1)}, u32[]{:S(2)}, u32[]{:S(2)}) collective-permute-start(bf16[2,64,2048]{2,1,0:T(8,128)(2,1)} %broadcast_select_fusion.1), channel_id=1, source_target_pairs={{0,4},{1,5},{2,6},{3,7},{4,8},{5,9},{6,10},{7,11},{8,12},{9,13},{1... | collective-permute-start | bytes 1572872 | tf_op jit(solution)/shard_map/ppermute | solution.py:263
  65.9 1.9 %collective-permute-start.14 = (f32[2,64,512]{2,1,0:T(8,128)S(1)}, f32[2,64,512]{2,1,0:T(8,128)S(1)}, u32[]{:S(2)}, u32[]{:S(2)}) collective-permute-start(f32[2,64,512]{2,1,0:T(8,128)S(1)} %get-tuple-element.51), channel_id=1, source_target_pairs={{0,1},{1,0},{2,3},{3,2},{4,5},{5,4},{6,7},{7,6},{8,9},{9,8},{10,11... | collective-permute-start | bytes 786440 | tf_op jit(solution)/shard_map/ppermute | solution.py:263
  66.5 21.1 %collective-permute-start.22 = (bf16[2,64,2048]{2,1,0:T(8,128)(2,1)}, bf16[2,64,2048]{2,1,0:T(8,128)(2,1)S(1)}, u32[]{:S(2)}, u32[]{:S(2)}) collective-permute-start(bf16[2,64,2048]{2,1,0:T(8,128)(2,1)} %select_select_fusion.refs_11_), channel_id=1, source_target_pairs={{0,4},{1,5},{2,6},{3,7},{4,8},{5,9},{6,10},{7,11},{8,12},{9,13},{1... | collective-permute-start | bytes 1572872 | tf_op jit(solution)/shard_map/ppermute | solution.py:263
  68.0 19.6 %collective-permute-start.16 = (f32[4,64,512]{2,1,0:T(8,128)S(1)}, f32[4,64,512]{2,1,0:T(8,128)S(1)}, u32[]{:S(2)}, u32[]{:S(2)}) collective-permute-start(f32[4,64,512]{2,1,0:T(8,128)S(1)} %pad_maximum_fusion.1.refs_8_), channel_id=1, source_target_pairs={{0,2},{1,3},{2,0},{3,1},{4,6},{5,7},{6,4},{7,5},{8,10},{9,11},{10,... | collective-permute-start | bytes 1572872 | tf_op jit(solution)/shard_map/ppermute | solution.py:263
  69.8 14.1 %collective-permute-start.5 = (f32[2,64,512]{2,1,0:T(8,128)}, f32[2,64,512]{2,1,0:T(8,128)S(1)}, u32[]{:S(2)}, u32[]{:S(2)}) collective-permute-start(f32[2,64,512]{2,1,0:T(8,128)} %copy-done.31), channel_id=1, source_target_pairs={{0,1},{1,0},{2,3},{3,2},{4,5},{5,4},{6,7},{7,6},{8,9},{9,8},{10,11... | collective-permute-start | bytes 786440 | tf_op jit(solution)/shard_map/ppermute | solution.py:263
  83.4 7.8 %collective-permute-start.6 = (f32[2,64,512]{2,1,0:T(8,128)S(1)}, f32[2,64,512]{2,1,0:T(8,128)S(1)}, u32[]{:S(2)}, u32[]{:S(2)}) collective-permute-start(f32[2,64,512]{2,1,0:T(8,128)S(1)} %copy-done.30), channel_id=1, source_target_pairs={{0,1},{1,0},{2,3},{3,2},{4,5},{5,4},{6,7},{7,6},{8,9},{9,8},{10,11... | collective-permute-start | bytes 786440 | tf_op jit(solution)/shard_map/ppermute | solution.py:263
  83.9 8.6 %collective-permute-start.12 = (f32[2,64,512]{2,1,0:T(8,128)S(1)}, f32[2,64,512]{2,1,0:T(8,128)S(1)}, u32[]{:S(2)}, u32[]{:S(2)}) collective-permute-start(f32[2,64,512]{2,1,0:T(8,128)S(1)} %copy-done.35), channel_id=1, source_target_pairs={{0,1},{1,0},{2,3},{3,2},{4,5},{5,4},{6,7},{7,6},{8,9},{9,8},{10,11... | collective-permute-start | bytes 786440 | tf_op jit(solution)/shard_map/ppermute | solution.py:263
  84.9 8.9 %collective-permute-start.13 = (f32[2,64,512]{2,1,0:T(8,128)S(1)}, f32[2,64,512]{2,1,0:T(8,128)S(1)}, u32[]{:S(2)}, u32[]{:S(2)}) collective-permute-start(f32[2,64,512]{2,1,0:T(8,128)S(1)} %copy-done.33), channel_id=1, source_target_pairs={{0,1},{1,0},{2,3},{3,2},{4,5},{5,4},{6,7},{7,6},{8,9},{9,8},{10,11... | collective-permute-start | bytes 786440 | tf_op jit(solution)/shard_map/ppermute | solution.py:263
  87.5 12.0 %collective-permute-start.19 = (f32[2,64,512]{2,1,0:T(8,128)S(1)}, f32[2,64,512]{2,1,0:T(8,128)S(1)}, u32[]{:S(2)}, u32[]{:S(2)}) collective-permute-start(f32[2,64,512]{2,1,0:T(8,128)S(1)} %get-tuple-element.55), channel_id=1, source_target_pairs={{0,1},{1,0},{2,3},{3,2},{4,5},{5,4},{6,7},{7,6},{8,9},{9,8},{10,11... | collective-permute-start | bytes 786440 | tf_op jit(solution)/shard_map/ppermute | solution.py:263
  87.6 12.0 %collective-permute-start.21 = (f32[2,64,512]{2,1,0:T(8,128)S(1)}, f32[2,64,512]{2,1,0:T(8,128)S(1)}, u32[]{:S(2)}, u32[]{:S(2)}) collective-permute-start(f32[2,64,512]{2,1,0:T(8,128)S(1)} %add.44.refs_0_), channel_id=1, source_target_pairs={{0,2},{1,3},{2,0},{3,1},{4,6},{5,7},{6,4},{7,5},{8,10},{9,11},{10,... | collective-permute-start | bytes 786440 | tf_op jit(solution)/shard_map/ppermute | solution.py:263
  91.2 7.6 %collective-permute-start.24 = (f32[1,64,512]{2,1,0:T(8,128)S(1)}, f32[1,64,512]{2,1,0:T(8,128)S(1)}, u32[]{:S(2)}, u32[]{:S(2)}) collective-permute-start(f32[1,64,512]{2,1,0:T(8,128)S(1)} %shard_map.52.refs_3_), channel_id=1, source_target_pairs={{2,0},{6,4},{10,8},{14,12},{18,16},{22,20},{26,24},{30,28}} | collective-permute-start | bytes 393224 | tf_op jit(solution)/shard_map/ppermute | solution.py:263
  92.5 7.0 %collective-permute-start.25 = (f32[1,64,512]{2,1,0:T(8,128)S(1)}, f32[1,64,512]{2,1,0:T(8,128)S(1)}, u32[]{:S(2)}, u32[]{:S(2)}) collective-permute-start(f32[1,64,512]{2,1,0:T(8,128)S(1)} %shard_map.52.refs_3_), channel_id=1, source_target_pairs={{3,0},{7,4},{11,8},{15,12},{19,16},{23,20},{27,24},{31,28}} | collective-permute-start | bytes 393224 | tf_op jit(solution)/shard_map/ppermute | solution.py:263
  93.8 5.7 %collective-permute-start.23 = (f32[1,64,512]{2,1,0:T(8,128)S(1)}, f32[1,64,512]{2,1,0:T(8,128)S(1)}, u32[]{:S(2)}, u32[]{:S(2)}) collective-permute-start(f32[1,64,512]{2,1,0:T(8,128)S(1)} %shard_map.52.refs_3_), channel_id=1, source_target_pairs={{1,0},{5,4},{9,8},{13,12},{17,16},{21,20},{25,24},{29,28}} | collective-permute-start | bytes 393224 | tf_op jit(solution)/shard_map/ppermute | solution.py:263
  (38 other events, 290.7 us)
